TPU v7x, 32 devices: a whole 2x2x4 slice. The times are simulated.
32 devices in a mesh: groups: 2 (over y), expert: 8 (over z, x), tensor: 2 (over core).
Axes of the slice: x: 2, y: 2, z: 4, core: 2. Of those that a mesh axis runs over, the one named last changes fastest.
Arguments:
- tokens: bfloat16 [2048, 7168], P(('groups', 'expert'), 'tensor'), parts along dimension 0, may hold values from -6 to 6
- expert_ids: int32 [2048, 8], P(('groups', 'expert')), parts along dimension 0, may hold values from 0 to 255, all different within a row; in each aligned block of 128 rows (0 to 127, 128 to 255, ...) at most 8 rows name the same one
- route_weight: float32 [2048, 8], P(('groups', 'expert')), parts along dimension 0, may hold values from 0.2 to 1
- gate_weight: bfloat16 [8, 7168, 2048], P('expert', 'tensor'), may hold values from -0.0625 to 0.0625
- up_weight: bfloat16 [8, 7168, 2048], P('expert', 'tensor'), may hold values from -0.0625 to 0.0625
- down_weight: bfloat16 [8, 2048, 7168], P('expert', None, 'tensor'), may hold values from -0.125 to 0.125
Outputs:
- mixed: bfloat16 [2048, 7168], P(('groups', 'expert'), 'tensor'), parts along dimension 0
There are 2 independent parts, one for each index of `groups`. A program takes and returns all parts, laid end to end along the dimension named above; an argument that names none is the same for every part. Nothing has to cross between parts.
Inputs may be any that keep to these rules, and one draw needn't show every extreme that they name: `expert_ids`: each row names 8 different experts; among the rows of one index of expert (128 rows, in order) no expert is named more than 8 times, a bound that some block reaches.
All inputs are finite; a program needn't handle non-finite values.
Results may differ from a plain program's by a relative error of at most 0.0057.
Values may be sent and summed in bfloat16 or wider, within the bound.
No kernel may reach another device: no remote copies, remote signals or barrier semaphores. Data moves between devices by JAX's collectives and lax.ppermute only.
A program may use at most 192 MiB of HBM per device.

v0:
```python
import jax
import jax.numpy as jnp
from jax import lax
from jax.sharding import PartitionSpec as P

HIDDEN_SIZE = 2048
ROUTED = 256


def local(tokens, expert_ids, route_weight, gate_weight, up_weight, down_weight):
    devices = lax.axis_size("expert")
    split = HIDDEN_SIZE // gate_weight.shape[2]
    experts = devices // split
    width = tokens.shape[1]
    top_count = expert_ids.shape[1]
    block_bound = max(4, 2 * tokens.shape[0] * top_count // ROUTED)
    gate_local = gate_weight[0]
    up_local = up_weight[0]
    down_local = down_weight[0]
    slot_count = min(block_bound, tokens.shape[0])
    count = tokens.shape[0] * top_count
    flat_ids = expert_ids.reshape(count)
    onehot = (flat_ids[:, None] == jnp.arange(experts, dtype=jnp.int32)[None, :]).astype(jnp.int32)
    before = jnp.cumsum(onehot, axis=0) - onehot
    slot = jnp.sum(before * onehot, axis=1)
    dump_row = experts * slot_count
    position = jnp.where(flat_ids < experts, flat_ids * slot_count + slot, dump_row)
    source_row = jnp.arange(count, dtype=jnp.int32) // top_count
    send = jnp.zeros((dump_row + 1, width), jnp.bfloat16)
    send = send.at[position].set(tokens[source_row])[:dump_row]
    send = jnp.repeat(send.reshape(experts, slot_count, width), split, axis=0)
    arrived = lax.all_to_all(send, "expert", split_axis=0, concat_axis=0, tiled=True)
    sources, items, features = arrived.shape
    flat = arrived.reshape(sources * items, features)
    gate = jnp.dot(flat, gate_local, preferred_element_type=jnp.float32)
    up = jnp.dot(flat, up_local, preferred_element_type=jnp.float32)
    gate_share = lax.psum_scatter(gate, "tensor", scatter_dimension=0, tiled=True)
    up_share = lax.psum_scatter(up, "tensor", scatter_dimension=0, tiled=True)
    hidden_share = (jax.nn.silu(gate_share) * up_share).astype(jnp.bfloat16)
    hidden = lax.all_gather(hidden_share, "tensor", axis=0, tiled=True)
    answer = jnp.dot(hidden, down_local, preferred_element_type=jnp.float32).astype(jnp.bfloat16)
    answer = answer.reshape(sources, items, features)
    back = lax.all_to_all(answer, "expert", split_axis=0, concat_axis=0, tiled=True)
    summed = jnp.sum(back.reshape(experts, split, slot_count, width).astype(jnp.float32), axis=1)
    summed = jnp.concatenate(
        [summed.reshape(dump_row, width), jnp.zeros((1, width), jnp.float32)], axis=0
    )
    picked = summed[position] * route_weight.reshape(count)[:, None]
    result = jnp.sum(picked.reshape(tokens.shape[0], top_count, width), axis=1)
    return result.astype(jnp.bfloat16)


def solution(mesh):
    return jax.shard_map(
        local,
        mesh=mesh,
        in_specs=(
            P(("groups", "expert"), "tensor"),
            P(("groups", "expert"), None),
            P(("groups", "expert"), None),
            P("expert", "tensor", None),
            P("expert", "tensor", None),
            P("expert", None, "tensor"),
        ),
        out_specs=P(("groups", "expert"), "tensor"),
        check_vma=False,
    )
```

profile of v0, /device:TPU:0, one launch (start us, length us, event | category | flops | bytes accessed | tf_op | source)
XLA Modules:
  0.0 150.4 jit_solution(464599894524030061)
XLA Ops:
  6.5 0.9 copy.10
  7.4 0.1 eq.29
  7.6 0.7 broadcast_multiply_fusion
  8.3 0.7 broadcast_compare_fusion
  9.0 2.3 %reduce-window.6 = s32[8,8,128]{2,1,0:T(8,128)S(1)} reduce-window(s32[8,8,128]{2,1,0:T(8,128)S(1)} %fusion.21, s32[]{:T(128)} %constant.31.clone.1), window={size=1x1x128 pad=0_0x0_0x127_0}, to_apply=%region_0.0 | reduce-window | flops 1040384 | bytes 65540 | tf_op jit(solution)/shard_map/reduce-window
  11.3 0.3 slice_reduce_fusion
  11.6 0.2 reduce-window.9
  11.8 0.1 copy.9
  11.9 0.1 mul.33
  12.0 0.1 copy.8
  12.1 0.1 lt.35
  12.3 32.1 %scatter_custom_fusion = bf16[65,3584]{1,0:T(8,128)(2,1)S(1)} fusion(s32[1024]{0:T(1024)S(1)} %bitcast.54, bf16[128,3584]{1,0:T(8,128)(2,1)S(1)} %copy-done, s32[1024]{0:T(1024)S(1)} %broadcast_clamp_fusion.1, bf16[]{:T(256)} %constant.29.clone.1), kind=kCustom, calls=%fused_computation.11 | custom fusion | bytes 465922 | tf_op jit(solution)/shard_map/scatter | solution.py:30
  44.5 20.3 %all_to_all.10 = bf16[8,8,3584]{2,1,0:T(8,128)(2,1)S(1)} all-to-all(bf16[8,8,3584]{2,1,0:T(8,128)(2,1)S(1)} %slice_bitcast_fusion), channel_id=1, replica_groups=mesh['groups'=2,'expert'=8,'tensor'=2] {'expert'}, dimensions={0} | all-to-all | bytes 917504 | tf_op jit(solution)/shard_map/all_to_all | solution.py:32
  64.8 8.6 %fusion.5 = f32[64,2048]{1,0:T(8,128)} fusion(bf16[1,3584,2048]{2,1,0:T(8,128)(2,1)} %param.9, bf16[8,8,3584]{2,1,0:T(8,128)(2,1)S(1)} %all_to_all.10), kind=kOutput, calls=%fused_computation.9 | convolution fusion | flops 939524096 | bytes 15663104 | tf_op jit(solution)/shard_map/dot_general | solution.py:35
  73.5 8.7 %fusion.3 = f32[64,2048]{1,0:T(8,128)} fusion(bf16[1,3584,2048]{2,1,0:T(8,128)(2,1)} %param.10, bf16[8,8,3584]{2,1,0:T(8,128)(2,1)S(1)} %all_to_all.10), kind=kOutput, calls=%fused_computation.7 | convolution fusion | flops 939524096 | bytes 15663104 | tf_op jit(solution)/shard_map/dot_general | solution.py:36
  82.3 9.7 %reduce-scatter.5.cloned.1.call-done = f32[32,2048]{1,0:T(8,128)} async-done(((f32[64,2048]{1,0:T(8,128)}), f32[32,2048]{1,0:T(8,128)}) %reduce-scatter.5.cloned.1.call-update) | async-done | bytes 262160 | tf_op jit(solution)/shard_map/reduce_scatter | solution.py:38
  91.9 1.1 multiply_convert_fusion
  93.0 2.0 %all_gather.3 = bf16[64,2048]{1,0:T(8,128)(2,1)S(1)} all-gather(bf16[32,2048]{1,0:T(8,128)(2,1)S(1)} %multiply_convert_fusion), channel_id=1, replica_groups=mesh['groups'=2,'expert'=8,'tensor'=2] {'tensor'}, dimensions={0}, use_global_device_ids=true | all-gather | bytes 393216 | tf_op jit(solution)/shard_map/all_gather | solution.py:40
  95.0 8.6 %fusion.12 = bf16[8,8,3584]{2,1,0:T(8,128)(2,1)} fusion(bf16[64,2048]{1,0:T(8,128)(2,1)S(1)} %all_gather.3, bf16[1,2048,3584]{2,1,0:T(8,128)(2,1)} %param.11), kind=kOutput, calls=%fused_computation.14 | convolution fusion | flops 939753472 | bytes 15400960 | tf_op jit(solution)/shard_map/dot_general | solution.py:41
  103.6 5.8 %all-to-all-start.1 = ((bf16[8,8,3584]{2,1,0:T(8,128)(2,1)}), bf16[8,8,3584]{2,1,0:T(8,128)(2,1)S(1)}, u32[]{:S(2)}, u32[]{:S(2)}) async-start(bf16[8,8,3584]{2,1,0:T(8,128)(2,1)} %fusion.12), calls=%async_computation.3 | async-start | bytes 917504 | tf_op jit(solution)/shard_map/all_to_all | solution.py:43
  109.4 0.1 copy.12
  109.5 13.4 %all-to-all-done.1 = bf16[8,8,3584]{2,1,0:T(8,128)(2,1)S(1)} async-done(((bf16[8,8,3584]{2,1,0:T(8,128)(2,1)}), bf16[8,8,3584]{2,1,0:T(8,128)(2,1)S(1)}, u32[]{:S(2)}, u32[]{:S(2)}) %all-to-all-start.1) | async-done | bytes 458784 | tf_op jit(solution)/shard_map/all_to_all | solution.py:43
  123.0 8.9 %gather_fusion = f32[1024,3584]{1,0:T(8,128)} fusion(f32[65,3584]{1,0:T(8,128)S(1)} %pad_convert_fusion, s32[1024]{0:T(1024)S(1)} %broadcast_clamp_fusion), kind=kCustom, calls=%fused_computation.1 | custom fusion | bytes 29364224 | tf_op jit(solution)/shard_map/gather | solution.py:48
  131.8 11.7 %fusion = bf16[128,3584]{1,0:T(8,128)(2,1)} fusion(f32[1024,3584]{1,0:T(8,128)} %gather_fusion, f32[128,8]{1,0:T(8,128)S(1)} %copy.12), kind=kLoop, calls=%fused_computation.4 | loop fusion | flops 6881280 | bytes 15601664 | tf_op jit(solution)/shard_map/reduce_sum | solution.py:49
  (19 shorter events, 0.4 us)
Async XLA Ops:
  6.5 5.8 %copy-start = (bf16[128,3584]{1,0:T(8,128)(2,1)S(1)}, bf16[128,3584]{1,0:T(8,128)(2,1)}, u32[]{:S(2)}) copy-start(bf16[128,3584]{1,0:T(8,128)(2,1)} %param.6) | copy-start | bytes 2752516
  6.5 75.7 %reduce-scatter.3.cloned.1.call-start = ((), (), s32[]{:S(2)}) async-start(), calls=%async_computation.4 | async-start | bytes 786432 | tf_op jit(solution)/shard_map/reduce_scatter | solution.py:37
  73.4 18.5 %reduce-scatter.5.cloned.1.call-start = ((), (), s32[]{:S(2)}) async-start(), calls=%async_computation.5 | async-start | bytes 786432 | tf_op jit(solution)/shard_map/reduce_scatter | solution.py:38
  82.2 27.2 %copy-start.1 = (f32[128,8]{0,1:T(8,128)S(1)}, f32[128,8]{0,1:T(8,128)}, u32[]{:S(2)}) copy-start(f32[128,8]{0,1:T(8,128)} %param.8) | copy-start | bytes 12292
  103.6 19.3 %all-to-all-start.1 = ((bf16[8,8,3584]{2,1,0:T(8,128)(2,1)}), bf16[8,8,3584]{2,1,0:T(8,128)(2,1)S(1)}, u32[]{:S(2)}, u32[]{:S(2)}) async-start(bf16[8,8,3584]{2,1,0:T(8,128)(2,1)} %fusion.12), calls=%async_computation.3 | async-start | bytes 917504 | tf_op jit(solution)/shard_map/all_to_all | solution.py:43
Sparse Core Ops, SparseCore 0:
  73.5 6.8 reduce-scatter.2
  82.8 9.1 reduce-scatter.4
where the time goes:
time: 151 us; the launch traced here: 150 us
  local copies, waits for them, and re-layouts  42.9 us (28%)
  matrix products  25.9 us (17%)
  waiting for transfers between devices  23.2 us (15%)
  blocking collectives  22.3 us (15%)
  other arithmetic  16.8 us (11%)
  between operations  13.5 us (9%)
  starting transfers between devices  5.8 us (4%)
    scatter x1, local copies, waits for them, and re-layouts, local(): send = send.at[position].set(tokens[source_row])[:dump_row]  32.1 us
    all_to_all x1, blocking collectives, local(): lax.all_to_all(send, 'expert', split_axis=0, concat_axis=0, tiled=True)  20.3 us
    all_to_all x1, waiting for transfers between devices, local(): lax.all_to_all(answer, 'expert', split_axis=0, concat_axis=0, tiled=True)  13.4 us
    reduce_sum x1, other arithmetic, local(): result = jnp.sum(picked.reshape(tokens.shape[0], top_count, width), axis=1)  11.7 us
    reduce_scatter x1, waiting for transfers between devices, local(): up_share = lax.psum_scatter(up, 'tensor', scatter_dimension=0, tiled=True)  9.67 us
    gather x1, local copies, waits for them, and re-layouts, local(): picked = summed[position] * route_weight.reshape(count)[:, None]  8.87 us
    dot_general x1, matrix products, local(): up = jnp.dot(flat, up_local, preferred_element_type=jnp.float32)  8.75 us
    dot_general x1, matrix products, local(): gate = jnp.dot(flat, gate_local, preferred_element_type=jnp.float32)  8.62 us
  transfers between devices with their start and end apart: 3, of which 2 were waited for; matrix products, arithmetic and copies ran while one was open for 6% of the time, Pallas kernels for 0%

commit v1 on v0

v1 whole, which is shorter than its diff:
```python
import functools

import jax
import jax.numpy as jnp
from jax import lax
from jax.experimental import pallas as pl
from jax.experimental.pallas import tpu as pltpu
from jax.sharding import PartitionSpec as P

HIDDEN_SIZE = 2048
ROUTED = 256
DIRECT = 8
BF16 = jnp.bfloat16
F32 = jnp.float32
VMEM = pl.BlockSpec(memory_space=pltpu.VMEM)


def params(*arrays):
    size = sum(a.size * a.dtype.itemsize for a in arrays)
    return pltpu.CompilerParams(vmem_limit_bytes=int(2 * size) + (6 << 20))


def shape(dims, dtype):
    return jax.ShapeDtypeStruct(dims, dtype)


def tiles(total, size):
    return [(at, min(size, total - at)) for at in range(0, total, size)]


def join(blocks):
    if len(blocks) == 1:
        return blocks[0]
    return jnp.concatenate([b.astype(F32) for b in blocks], axis=0).astype(BF16)


def spread(refs, value, at, size):
    rows = value.shape[0] // len(refs)
    for j, ref in enumerate(refs):
        ref[:, at : at + size] = value[j * rows : (j + 1) * rows].astype(BF16)


def route_kernel(slots, split, direct, ids_ref, weight_ref, tokens_ref, mix_ref, *block_refs):
    tokens, top = ids_ref.shape
    full = mix_ref.shape[1] // 3
    rows = full // split
    ids = ids_ref[...]
    weight = weight_ref[...]

    def named(count, per):
        expert = lax.broadcasted_iota(jnp.int32, (tokens, count), 1) // per
        if direct:
            expert = expert ^ lax.axis_index("expert")
        hit = jnp.zeros((tokens, count), F32)
        scale = jnp.zeros((tokens, count), F32)
        for k in range(top):
            same = ids[:, k : k + 1] == expert
            hit = jnp.where(same, 1.0, hit)
            scale = jnp.where(same, weight[:, k : k + 1], scale)
        earlier = lax.broadcasted_iota(jnp.int32, (tokens, tokens), 1) < lax.broadcasted_iota(
            jnp.int32, (tokens, tokens), 0
        )
        before = jnp.dot(
            earlier.astype(F32).astype(BF16), hit.astype(BF16), preferred_element_type=F32
        ).astype(jnp.int32)
        slot = lax.broadcasted_iota(jnp.int32, (tokens, count), 1) % slots
        return jnp.where(before == slot, hit, 0.0), scale

    chosen, scale = named(rows, slots)
    pick = chosen.astype(BF16)
    for at, size in tiles(tokens_ref.shape[1], 512):
        value = lax.dot_general(
            pick,
            tokens_ref[:, at : at + size],
            (((0,), (0,)), ((), ())),
            preferred_element_type=F32,
        )
        spread(block_refs, value, at, size)
    if split > 1:
        chosen, scale = named(full, slots * split)
    rest = chosen * scale
    for part in range(3):
        piece = rest.astype(BF16)
        mix_ref[:, part * full : (part + 1) * full] = piece
        rest = rest - piece.astype(F32)


def up_kernel(count, *refs):
    block_refs, (gate_ref, up_ref, own_ref, send_ref) = refs[:count], refs[count:]
    hidden = gate_ref.shape[1]
    rows = own_ref.shape[0]
    x = join([b[...] for b in block_refs])
    for low, high in tiles(rows, 256):
        for part, w_ref in enumerate((gate_ref, up_ref)):
            for at, size in tiles(hidden, 512):
                value = jnp.dot(
                    x[low : low + high], w_ref[:, at : at + size], preferred_element_type=F32
                )
                to = part * hidden + at
                own_ref[low : low + high, to : to + size] = value
                send_ref[low : low + high, to : to + size] = value.astype(BF16)


def down_kernel(own_ref, other_ref, down_ref, *block_refs):
    hidden = down_ref.shape[0]
    total = own_ref[...] + other_ref[...].astype(F32)
    gate, up = total[:, :hidden], total[:, hidden:]
    act = (gate / (1.0 + jnp.exp(-gate)) * up).astype(BF16)
    for at, size in tiles(down_ref.shape[1], 512):
        value = jnp.dot(act, down_ref[:, at : at + size], preferred_element_type=F32)
        spread(block_refs, value, at, size)


def mix_kernel(mix_ref, *refs):
    block_refs, out_ref = refs[:-1], refs[-1]
    full = mix_ref.shape[1] // 3
    for at, size in tiles(out_ref.shape[1], 512):
        part = join([b[:, at : at + size] for b in block_refs])
        value = jnp.zeros((out_ref.shape[0], size), F32)
        for low in (2, 1, 0):
            value += jnp.dot(
                mix_ref[:, low * full : (low + 1) * full], part, preferred_element_type=F32
            )
        out_ref[:, at : at + size] = value.astype(BF16)


def swap(blocks, devices):
    return [blocks[0]] + [
        lax.ppermute(blocks[j], "expert", [(i, i ^ j) for i in range(devices)])
        for j in range(1, devices)
    ]


def local(tokens, expert_ids, route_weight, gate_weight, up_weight, down_weight):
    devices = lax.axis_size("expert")
    split = HIDDEN_SIZE // gate_weight.shape[2]
    experts = devices // split
    count, width = tokens.shape
    top = expert_ids.shape[1]
    slots = min(max(4, 2 * count * top // ROUTED), count)
    hidden = gate_weight.shape[2]
    rows = devices * slots
    direct = split == 1 and devices <= DIRECT and devices & (devices - 1) == 0
    near = functools.partial(pltpu.with_memory_space_constraint, memory_space=pltpu.VMEM)

    parts = devices if direct else 1
    sent = experts * slots // parts
    mix, *send = pl.pallas_call(
        functools.partial(route_kernel, slots, split, direct),
        in_specs=[VMEM] * 3,
        out_specs=[VMEM] * (1 + parts),
        out_shape=[shape((count, 3 * rows), BF16)] + [shape((sent, width), BF16)] * parts,
        compiler_params=params(tokens, shape((count, 8 * rows), F32)),
        name="route",
    )(expert_ids, route_weight, tokens)
    if direct:
        arrived = swap(send, devices)
    else:
        spread_out = jnp.repeat(send[0].reshape(experts, slots, width), split, axis=0)
        arrived = [
            lax.all_to_all(spread_out, "expert", 0, 0, tiled=True).reshape(rows, width)
        ]

    own, give = pl.pallas_call(
        functools.partial(up_kernel, parts),
        in_specs=[VMEM] * (parts + 2),
        out_specs=[VMEM] * 2,
        out_shape=[shape((rows, 2 * hidden), F32), shape((rows, 2 * hidden), BF16)],
        compiler_params=params(shape((rows, width), F32), shape((rows, 2 * hidden), F32)),
        name="up",
    )(*arrived, near(gate_weight[0]), near(up_weight[0]))
    cores = lax.axis_size("tensor")
    other = lax.ppermute(give, "tensor", [(i, (i + 1) % cores) for i in range(cores)])
    answer = pl.pallas_call(
        down_kernel,
        in_specs=[VMEM] * 3,
        out_specs=[VMEM] * parts,
        out_shape=[shape((rows // parts, width), BF16)] * parts,
        compiler_params=params(shape((rows, 4 * hidden), F32), shape((rows, width), F32)),
        name="down",
    )(own, other, near(down_weight[0]))
    if direct:
        back = swap(answer, devices)
    else:
        back = [
            lax.all_to_all(
                answer[0].reshape(devices, slots, width), "expert", 0, 0, tiled=True
            ).reshape(rows, width)
        ]
    return pl.pallas_call(
        mix_kernel,
        in_specs=[VMEM] * (1 + parts),
        out_specs=VMEM,
        out_shape=shape((count, width), BF16),
        compiler_params=params(mix, tokens, shape((rows, width), BF16)),
        name="mix",
    )(mix, *back)


def solution(mesh):
    return jax.shard_map(
        local,
        mesh=mesh,
        in_specs=(
            P(("groups", "expert"), "tensor"),
            P(("groups", "expert"), None),
            P(("groups", "expert"), None),
            P("expert", "tensor", None),
            P("expert", "tensor", None),
            P("expert", None, "tensor"),
        ),
        out_specs=P(("groups", "expert"), "tensor"),
        check_vma=False,
    )
```

time: 151 us -> 59.8 us (0.40)
  local copies, waits for them, and re-layouts: 42.9 us -> 13.1 us
  matrix products: 25.9 us -> 0 us
  blocking collectives: 22.3 us -> 0 us
  starting transfers between devices: 5.8 us -> 23.8 us
  other arithmetic: 16.8 us -> 0 us
  between operations: 13.5 us -> 0.05 us
  waiting for transfers between devices: 23.2 us -> 12.3 us
  Pallas kernels: 0 us -> 10.3 us
    scatter x1 -> x0, local copies, waits for them, and re-layouts: 32.1 us -> none  [local(): send = send.at[position].set(tokens[source_row])[:dump_row]]
    dot_general x3 -> x0, matrix products: 25.9 us -> none  [the longest x1 8.75 us: local(): up = jnp.dot(flat, up_local, preferred_element_type=jnp.float32)]
    ppermute x0 -> x15, starting transfers between devices: none -> 23.8 us  [the longest x14 23.7 us: swap(): lax.ppermute(blocks[j], 'expert', [(i, i ^ j) for i in range(devices)])]
    all_to_all x1 -> x0, blocking collectives: 20.3 us -> none  [local(): lax.all_to_all(send, 'expert', split_axis=0, concat_axis=0, tiled=True)]
    all_to_all x1 -> x0, waiting for transfers between devices: 13.4 us -> none  [local(): lax.all_to_all(answer, 'expert', split_axis=0, concat_axis=0, tiled=True)]
    ppermute x0 -> x15, waiting for transfers between devices: none -> 12.3 us  [the longest x14 10.4 us: swap(): lax.ppermute(blocks[j], 'expert', [(i, i ^ j) for i in range(devices)])]
    unnamed x6 -> x10, local copies, waits for them, and re-layouts: 0.98 us -> 13.1 us
    reduce_sum x2 -> x0, other arithmetic: 11.7 us -> none  [the longest x1 11.7 us: local(): result = jnp.sum(picked.reshape(tokens.shape[0], top_count, width), axis=1)]
  transfers between devices with their start and end apart: 3 -> 15, of which waited for: 2 -> 4; matrix products, arithmetic and copies ran while one was open for 6% -> 0% of each run, Pallas kernels for 0% -> 0%
where the time goes in v1:
time: 59.8 us; the launch traced here: 59.6 us
  starting transfers between devices  23.8 us (40%)
  local copies, waits for them, and re-layouts  13.1 us (22%)
  waiting for transfers between devices  12.3 us (21%)
  Pallas kernels  10.3 us (17%)
    ppermute x14, starting transfers between devices, swap(): lax.ppermute(blocks[j], 'expert', [(i, i ^ j) for i in range(devices)])  23.7 us
    unnamed x10, local copies, waits for them, and re-layouts  13.1 us
    ppermute x14, waiting for transfers between devices, swap(): lax.ppermute(blocks[j], 'expert', [(i, i ^ j) for i in range(devices)])  10.4 us
    pallas_call x1, Pallas kernels, local(): pl.pallas_call(functools.partial(up_kernel, parts), in_specs=[VMEM] * (pa...  5.19 us
    pallas_call x1, Pallas kernels, local(): pl.pallas_call(down_kernel, in_specs=[VMEM] * 3, out_specs=[VMEM] * parts...  2.59 us
    ppermute x1, waiting for transfers between devices, local(): lax.ppermute(give, 'tensor', [(i, (i + 1) % cores) for i in range(cores)])  1.9 us
    pallas_call x1, Pallas kernels, local(): pl.pallas_call(mix_kernel, in_specs=[VMEM] * (1 + parts), out_specs=VMEM,...  1.83 us
  transfers between devices with their start and end apart: 15, of which 4 were waited for; matrix products, arithmetic and copies ran while one was open for 0% of the time, Pallas kernels for 0%

profile of v1, /device:TPU:0, one launch (start us, length us, event | category | flops | bytes accessed | tf_op | source)
XLA Modules:
  0.0 59.6 jit_solution(6234199274949105007)
XLA Ops:
  0.0 0.8 %copy.7.ids_ref = s32[128,8]{1,0:T(8,128)S(1)} copy(s32[128,8]{0,1:T(8,128)} %param.7) | data formatting | bytes 8192 | tf_op args[1]
  0.8 0.8 %copy.8.weight_ref = f32[128,8]{1,0:T(8,128)S(1)} copy(f32[128,8]{0,1:T(8,128)} %param.8) | data formatting | bytes 8192 | tf_op args[2]
  1.6 1.2 %copy-done.3 = bf16[128,3584]{1,0:T(8,128)(2,1)S(1)} copy-done((bf16[128,3584]{1,0:T(8,128)(2,1)S(1)}, bf16[128,3584]{1,0:T(8,128)(2,1)}, u32[]{:S(2)}) %copy-start.3) | copy-done | bytes 917528
  2.8 0.7 %route.1 = (bf16[128,192]{1,0:T(8,128)(2,1)S(1)}, bf16[8,3584]{1,0:T(8,128)(2,1)S(1)}, bf16[8,3584]{1,0:T(8,128)(2,1)S(1)}, bf16[8,3584]{1,0:T(8,128)(2,1)S(1)},...) custom-call(s32[128,8]{1,0:T(8,128)S(1)} %copy.7.ids_ref, ...), custom_call_target="tpu_custom_call" | custom-call | tf_op jit(solution)/shard_map/route/pallas_call | solution.py:148
  3.5 3.0 %collective-permute-start = (bf16[8,3584]{1,0:T(8,128)(2,1)S(1)}, bf16[8,3584]{1,0:T(8,128)(2,1)S(1)}, u32[]{:S(2)}, u32[]{:S(2)}) collective-permute-start(bf16[8,3584]{1,0:T(8,128)(2,1)S(1)} %get-tuple-element.26), channel_id=1, source_target_pairs={{0,2},{2,0},{4,6},{6,4},{8,10},{10,8},{12,14},{14,12},{1,3},{3,1},... | collective-permute-start | bytes 172040 | tf_op jit(solution)/shard_map/ppermute | solution.py:129
  6.5 1.6 %collective-permute-start.1 = (bf16[8,3584]{1,0:T(8,128)(2,1)S(1)}, bf16[8,3584]{1,0:T(8,128)(2,1)S(1)}, u32[]{:S(2)}, u32[]{:S(2)}) collective-permute-start(bf16[8,3584]{1,0:T(8,128)(2,1)S(1)} %get-tuple-element.27), channel_id=1, source_target_pairs={{0,4},{2,6},{4,0},{6,2},{8,12},{10,14},{12,8},{14,10},{1,5},{3,7},... | collective-permute-start | bytes 172040 | tf_op jit(solution)/shard_map/ppermute | solution.py:129
  8.1 3.0 %collective-permute-start.3 = (bf16[8,3584]{1,0:T(8,128)(2,1)S(1)}, bf16[8,3584]{1,0:T(8,128)(2,1)S(1)}, u32[]{:S(2)}, u32[]{:S(2)}) collective-permute-start(bf16[8,3584]{1,0:T(8,128)(2,1)S(1)} %get-tuple-element.29), channel_id=1, source_target_pairs={{0,8},{2,10},{4,12},{6,14},{8,0},{10,2},{12,4},{14,6},{1,9},{3,11}... | collective-permute-start | bytes 172040 | tf_op jit(solution)/shard_map/ppermute | solution.py:129
  11.1 1.3 %collective-permute-start.4 = (bf16[8,3584]{1,0:T(8,128)(2,1)S(1)}, bf16[8,3584]{1,0:T(8,128)(2,1)S(1)}, u32[]{:S(2)}, u32[]{:S(2)}) collective-permute-start(bf16[8,3584]{1,0:T(8,128)(2,1)S(1)} %get-tuple-element.30), channel_id=1, source_target_pairs={{0,10},{2,8},{4,14},{6,12},{8,2},{10,0},{12,6},{14,4},{1,11},{3,9}... | collective-permute-start | bytes 172040 | tf_op jit(solution)/shard_map/ppermute | solution.py:129
  12.4 3.6 %collective-permute-start.5 = (bf16[8,3584]{1,0:T(8,128)(2,1)S(1)}, bf16[8,3584]{1,0:T(8,128)(2,1)S(1)}, u32[]{:S(2)}, u32[]{:S(2)}) collective-permute-start(bf16[8,3584]{1,0:T(8,128)(2,1)S(1)} %get-tuple-element.31), channel_id=1, source_target_pairs={{0,12},{2,14},{4,8},{6,10},{8,4},{10,6},{12,0},{14,2},{1,13},{3,15... | collective-permute-start | bytes 172040 | tf_op jit(solution)/shard_map/ppermute | solution.py:129
  16.0 4.2 %collective-permute-done.4.refs_5_ = bf16[8,3584]{1,0:T(8,128)(2,1)S(1)} collective-permute-done((bf16[8,3584]{1,0:T(8,128)(2,1)S(1)}, bf16[8,3584]{1,0:T(8,128)(2,1)S(1)}, u32[]{:S(2)}, u32[]{:S(2)}) %collective-permute-start.4) | collective-permute-done | bytes 57376 | tf_op jit(solution)/shard_map/ppermute | solution.py:129
  20.3 2.6 %collective-permute-done.6.refs_7_ = bf16[8,3584]{1,0:T(8,128)(2,1)S(1)} collective-permute-done((bf16[8,3584]{1,0:T(8,128)(2,1)S(1)}, bf16[8,3584]{1,0:T(8,128)(2,1)S(1)}, u32[]{:S(2)}, u32[]{:S(2)}) %collective-permute-start.6) | collective-permute-done | bytes 57376 | tf_op jit(solution)/shard_map/ppermute | solution.py:129
  22.8 5.2 %copy-done = bf16[1,3584,2048]{2,1,0:T(8,128)(2,1)S(1)} copy-done((bf16[1,3584,2048]{2,1,0:T(8,128)(2,1)S(1)}, bf16[1,3584,2048]{2,1,0:T(8,128)(2,1)}, u32[]{:S(2)}) %copy-start) | copy-done | bytes 14680088
  28.0 5.2 %copy-done.1 = bf16[1,3584,2048]{2,1,0:T(8,128)(2,1)S(1)} copy-done((bf16[1,3584,2048]{2,1,0:T(8,128)(2,1)S(1)}, bf16[1,3584,2048]{2,1,0:T(8,128)(2,1)}, u32[]{:S(2)}) %copy-start.1) | copy-done | bytes 14680088
  33.2 5.2 %up.1 = (f32[64,4096]{1,0:T(8,128)S(1)}, bf16[64,4096]{1,0:T(8,128)(2,1)S(1)}) custom-call(bf16[8,3584]{1,0:T(8,128)(2,1)S(1)} %get-tuple-element.25.refs_0_, bf16[8,3584]{1,0:T(8,128)(2,1)S(1)} %collective-permute-done.refs_1_, bf16[8,3584]{1,0:T(8,128)(2,1)S(1)} %collective-permute-done.1.refs_2_, bf16[8,3584]{1,0:T(8,128)(2,1)S(1)} %collective-permute-done.2.refs_3_, ...), custom_call_target="tpu_custom_call" | custom-call | tf_op jit(solution)/shard_map/up/pallas_call | solution.py:164
  38.5 1.9 %collective-permute-done.7.other_ref = bf16[64,4096]{1,0:T(8,128)(2,1)S(1)} collective-permute-done((bf16[64,4096]{1,0:T(8,128)(2,1)S(1)}, bf16[64,4096]{1,0:T(8,128)(2,1)S(1)}, u32[]{:S(2)}, u32[]{:S(2)}) %collective-permute-start.7) | collective-permute-done | bytes 524320 | tf_op jit(solution)/shard_map/ppermute | solution.py:173
  40.4 2.6 %down.1 = (bf16[8,3584]{1,0:T(8,128)(2,1)S(1)}, bf16[8,3584]{1,0:T(8,128)(2,1)S(1)}, bf16[8,3584]{1,0:T(8,128)(2,1)S(1)}, bf16[8,3584]{1,0:T(8,128)(2,1)S(1)}, b...) custom-call(f32[64,4096]{1,0:T(8,128)S(1)} %get-tuple-element.33.own, ...), custom_call_target="tpu_custom_call" | custom-call | tf_op jit(solution)/shard_map/down/pallas_call | solution.py:174
  43.7 0.8 %collective-permute-start.9 = (bf16[8,3584]{1,0:T(8,128)(2,1)S(1)}, bf16[8,3584]{1,0:T(8,128)(2,1)S(1)}, u32[]{:S(2)}, u32[]{:S(2)}) collective-permute-start(bf16[8,3584]{1,0:T(8,128)(2,1)S(1)} %get-tuple-element.37), channel_id=1, source_target_pairs={{0,4},{2,6},{4,0},{6,2},{8,12},{10,14},{12,8},{14,10},{1,5},{3,7},... | collective-permute-start | bytes 172040 | tf_op jit(solution)/shard_map/ppermute | solution.py:129
  44.4 2.1 %collective-permute-start.10 = (bf16[8,3584]{1,0:T(8,128)(2,1)S(1)}, bf16[8,3584]{1,0:T(8,128)(2,1)S(1)}, u32[]{:S(2)}, u32[]{:S(2)}) collective-permute-start(bf16[8,3584]{1,0:T(8,128)(2,1)S(1)} %get-tuple-element.38), channel_id=1, source_target_pairs={{0,6},{2,4},{4,2},{6,0},{8,14},{10,12},{12,10},{14,8},{1,7},{3,5},... | collective-permute-start | bytes 172040 | tf_op jit(solution)/shard_map/ppermute | solution.py:129
  46.5 1.5 %collective-permute-start.11 = (bf16[8,3584]{1,0:T(8,128)(2,1)S(1)}, bf16[8,3584]{1,0:T(8,128)(2,1)S(1)}, u32[]{:S(2)}, u32[]{:S(2)}) collective-permute-start(bf16[8,3584]{1,0:T(8,128)(2,1)S(1)} %get-tuple-element.39), channel_id=1, source_target_pairs={{0,8},{2,10},{4,12},{6,14},{8,0},{10,2},{12,4},{14,6},{1,9},{3,11}... | collective-permute-start | bytes 172040 | tf_op jit(solution)/shard_map/ppermute | solution.py:129
  48.0 1.5 %collective-permute-start.12 = (bf16[8,3584]{1,0:T(8,128)(2,1)S(1)}, bf16[8,3584]{1,0:T(8,128)(2,1)S(1)}, u32[]{:S(2)}, u32[]{:S(2)}) collective-permute-start(bf16[8,3584]{1,0:T(8,128)(2,1)S(1)} %get-tuple-element.40), channel_id=1, source_target_pairs={{0,10},{2,8},{4,14},{6,12},{8,2},{10,0},{12,6},{14,4},{1,11},{3,9}... | collective-permute-start | bytes 172040 | tf_op jit(solution)/shard_map/ppermute | solution.py:129
  49.5 0.9 %collective-permute-start.13 = (bf16[8,3584]{1,0:T(8,128)(2,1)S(1)}, bf16[8,3584]{1,0:T(8,128)(2,1)S(1)}, u32[]{:S(2)}, u32[]{:S(2)}) collective-permute-start(bf16[8,3584]{1,0:T(8,128)(2,1)S(1)} %get-tuple-element.41), channel_id=1, source_target_pairs={{0,12},{2,14},{4,8},{6,10},{8,4},{10,6},{12,0},{14,2},{1,13},{3,15... | collective-permute-start | bytes 172040 | tf_op jit(solution)/shard_map/ppermute | solution.py:129
  50.4 3.8 %collective-permute-start.14 = (bf16[8,3584]{1,0:T(8,128)(2,1)S(1)}, bf16[8,3584]{1,0:T(8,128)(2,1)S(1)}, u32[]{:S(2)}, u32[]{:S(2)}) collective-permute-start(bf16[8,3584]{1,0:T(8,128)(2,1)S(1)} %get-tuple-element.42), channel_id=1, source_target_pairs={{0,14},{2,12},{4,10},{6,8},{8,6},{10,4},{12,2},{14,0},{1,15},{3,13... | collective-permute-start | bytes 172040 | tf_op jit(solution)/shard_map/ppermute | solution.py:129
  54.2 3.5 %collective-permute-done.12.refs_5_ = bf16[8,3584]{1,0:T(8,128)(2,1)S(1)} collective-permute-done((bf16[8,3584]{1,0:T(8,128)(2,1)S(1)}, bf16[8,3584]{1,0:T(8,128)(2,1)S(1)}, u32[]{:S(2)}, u32[]{:S(2)}) %collective-permute-start.12) | collective-permute-done | bytes 57376 | tf_op jit(solution)/shard_map/ppermute | solution.py:129
  57.7 1.8 %mix.1 = bf16[128,3584]{1,0:T(8,128)(2,1)} custom-call(bf16[128,192]{1,0:T(8,128)(2,1)S(1)} %get-tuple-element.24.mix_ref, bf16[8,3584]{1,0:T(8,128)(2,1)S(1)} %get-tuple-element.35.refs_0_, bf16[8,3584]{1,0:T(8,128)(2,1)S(1)} %collective-permute-done.8.refs_1_, bf16[8,3584]{1,0:T(8,128)(2,1)S(1)} %collective-permute-done.9.refs_2_, ...), custom_call_target="tpu_custom_call" | custom-call | tf_op jit(solution)/shard_map/mix/pallas_call | solution.py:190
  (20 shorter events, 0.9 us)
Async XLA Ops:
  1.6 1.2 %copy-start.3 = (bf16[128,3584]{1,0:T(8,128)(2,1)S(1)}, bf16[128,3584]{1,0:T(8,128)(2,1)}, u32[]{:S(2)}) copy-start(bf16[128,3584]{1,0:T(8,128)(2,1)} %tokens_ref.1) | copy-start | bytes 2752516
  3.5 8.9 %collective-permute-start = (bf16[8,3584]{1,0:T(8,128)(2,1)S(1)}, bf16[8,3584]{1,0:T(8,128)(2,1)S(1)}, u32[]{:S(2)}, u32[]{:S(2)}) collective-permute-start(bf16[8,3584]{1,0:T(8,128)(2,1)S(1)} %get-tuple-element.26), channel_id=1, source_target_pairs={{0,2},{2,0},{4,6},{6,4},{8,10},{10,8},{12,14},{14,12},{1,3},{3,1},... | collective-permute-start | bytes 172040 | tf_op jit(solution)/shard_map/ppermute | solution.py:129
  6.5 9.5 %collective-permute-start.1 = (bf16[8,3584]{1,0:T(8,128)(2,1)S(1)}, bf16[8,3584]{1,0:T(8,128)(2,1)S(1)}, u32[]{:S(2)}, u32[]{:S(2)}) collective-permute-start(bf16[8,3584]{1,0:T(8,128)(2,1)S(1)} %get-tuple-element.27), channel_id=1, source_target_pairs={{0,4},{2,6},{4,0},{6,2},{8,12},{10,14},{12,8},{14,10},{1,5},{3,7},... | collective-permute-start | bytes 172040 | tf_op jit(solution)/shard_map/ppermute | solution.py:129
  8.1 7.9 %collective-permute-start.2 = (bf16[8,3584]{1,0:T(8,128)(2,1)S(1)}, bf16[8,3584]{1,0:T(8,128)(2,1)S(1)}, u32[]{:S(2)}, u32[]{:S(2)}) collective-permute-start(bf16[8,3584]{1,0:T(8,128)(2,1)S(1)} %get-tuple-element.28), channel_id=1, source_target_pairs={{0,6},{2,4},{4,2},{6,0},{8,14},{10,12},{12,10},{14,8},{1,7},{3,5},... | collective-permute-start | bytes 172040 | tf_op jit(solution)/shard_map/ppermute | solution.py:129
  8.1 7.9 %collective-permute-start.3 = (bf16[8,3584]{1,0:T(8,128)(2,1)S(1)}, bf16[8,3584]{1,0:T(8,128)(2,1)S(1)}, u32[]{:S(2)}, u32[]{:S(2)}) collective-permute-start(bf16[8,3584]{1,0:T(8,128)(2,1)S(1)} %get-tuple-element.29), channel_id=1, source_target_pairs={{0,8},{2,10},{4,12},{6,14},{8,0},{10,2},{12,4},{14,6},{1,9},{3,11}... | collective-permute-start | bytes 172040 | tf_op jit(solution)/shard_map/ppermute | solution.py:129
  11.1 9.2 %collective-permute-start.4 = (bf16[8,3584]{1,0:T(8,128)(2,1)S(1)}, bf16[8,3584]{1,0:T(8,128)(2,1)S(1)}, u32[]{:S(2)}, u32[]{:S(2)}) collective-permute-start(bf16[8,3584]{1,0:T(8,128)(2,1)S(1)} %get-tuple-element.30), channel_id=1, source_target_pairs={{0,10},{2,8},{4,14},{6,12},{8,2},{10,0},{12,6},{14,4},{1,11},{3,9}... | collective-permute-start | bytes 172040 | tf_op jit(solution)/shard_map/ppermute | solution.py:129
  12.4 7.9 %collective-permute-start.5 = (bf16[8,3584]{1,0:T(8,128)(2,1)S(1)}, bf16[8,3584]{1,0:T(8,128)(2,1)S(1)}, u32[]{:S(2)}, u32[]{:S(2)}) collective-permute-start(bf16[8,3584]{1,0:T(8,128)(2,1)S(1)} %get-tuple-element.31), channel_id=1, source_target_pairs={{0,12},{2,14},{4,8},{6,10},{8,4},{10,6},{12,0},{14,2},{1,13},{3,15... | collective-permute-start | bytes 172040 | tf_op jit(solution)/shard_map/ppermute | solution.py:129
  16.0 6.9 %collective-permute-start.6 = (bf16[8,3584]{1,0:T(8,128)(2,1)S(1)}, bf16[8,3584]{1,0:T(8,128)(2,1)S(1)}, u32[]{:S(2)}, u32[]{:S(2)}) collective-permute-start(bf16[8,3584]{1,0:T(8,128)(2,1)S(1)} %get-tuple-element.32), channel_id=1, source_target_pairs={{0,14},{2,12},{4,10},{6,8},{8,6},{10,4},{12,2},{14,0},{1,15},{3,13... | collective-permute-start | bytes 172040 | tf_op jit(solution)/shard_map/ppermute | solution.py:129
  22.8 5.2 %copy-start = (bf16[1,3584,2048]{2,1,0:T(8,128)(2,1)S(1)}, bf16[1,3584,2048]{2,1,0:T(8,128)(2,1)}, u32[]{:S(2)}) copy-start(bf16[1,3584,2048]{2,1,0:T(8,128)(2,1)} %param.9) | copy-start | bytes 44040196
  28.0 5.2 %copy-start.1 = (bf16[1,3584,2048]{2,1,0:T(8,128)(2,1)S(1)}, bf16[1,3584,2048]{2,1,0:T(8,128)(2,1)}, u32[]{:S(2)}) copy-start(bf16[1,3584,2048]{2,1,0:T(8,128)(2,1)} %param.10) | copy-start | bytes 44040196
  33.2 7.2 %copy-start.2 = (bf16[1,2048,3584]{2,1,0:T(8,128)(2,1)S(1)}, bf16[1,2048,3584]{2,1,0:T(8,128)(2,1)}, u32[]{:S(2)}) copy-start(bf16[1,2048,3584]{2,1,0:T(8,128)(2,1)} %param.11) | copy-start | bytes 44040196
  38.4 2.0 %collective-permute-start.7 = (bf16[64,4096]{1,0:T(8,128)(2,1)S(1)}, bf16[64,4096]{1,0:T(8,128)(2,1)S(1)}, u32[]{:S(2)}, u32[]{:S(2)}) collective-permute-start(bf16[64,4096]{1,0:T(8,128)(2,1)S(1)} %get-tuple-element.34), channel_id=1, source_target_pairs={{0,1},{1,0},{2,3},{3,2},{4,5},{5,4},{6,7},{7,6},{8,9},{9,8},{10,11... | collective-permute-start | bytes 1572872 | tf_op jit(solution)/shard_map/ppermute | solution.py:173
  42.9 6.6 %collective-permute-start.8 = (bf16[8,3584]{1,0:T(8,128)(2,1)S(1)}, bf16[8,3584]{1,0:T(8,128)(2,1)S(1)}, u32[]{:S(2)}, u32[]{:S(2)}) collective-permute-start(bf16[8,3584]{1,0:T(8,128)(2,1)S(1)} %get-tuple-element.36), channel_id=1, source_target_pairs={{0,2},{2,0},{4,6},{6,4},{8,10},{10,8},{12,14},{14,12},{1,3},{3,1},... | collective-permute-start | bytes 172040 | tf_op jit(solution)/shard_map/ppermute | solution.py:129
  43.7 6.8 %collective-permute-start.9 = (bf16[8,3584]{1,0:T(8,128)(2,1)S(1)}, bf16[8,3584]{1,0:T(8,128)(2,1)S(1)}, u32[]{:S(2)}, u32[]{:S(2)}) collective-permute-start(bf16[8,3584]{1,0:T(8,128)(2,1)S(1)} %get-tuple-element.37), channel_id=1, source_target_pairs={{0,4},{2,6},{4,0},{6,2},{8,12},{10,14},{12,8},{14,10},{1,5},{3,7},... | collective-permute-start | bytes 172040 | tf_op jit(solution)/shard_map/ppermute | solution.py:129
  44.4 9.7 %collective-permute-start.10 = (bf16[8,3584]{1,0:T(8,128)(2,1)S(1)}, bf16[8,3584]{1,0:T(8,128)(2,1)S(1)}, u32[]{:S(2)}, u32[]{:S(2)}) collective-permute-start(bf16[8,3584]{1,0:T(8,128)(2,1)S(1)} %get-tuple-element.38), channel_id=1, source_target_pairs={{0,6},{2,4},{4,2},{6,0},{8,14},{10,12},{12,10},{14,8},{1,7},{3,5},... | collective-permute-start | bytes 172040 | tf_op jit(solution)/shard_map/ppermute | solution.py:129
  46.5 7.7 %collective-permute-start.11 = (bf16[8,3584]{1,0:T(8,128)(2,1)S(1)}, bf16[8,3584]{1,0:T(8,128)(2,1)S(1)}, u32[]{:S(2)}, u32[]{:S(2)}) collective-permute-start(bf16[8,3584]{1,0:T(8,128)(2,1)S(1)} %get-tuple-element.39), channel_id=1, source_target_pairs={{0,8},{2,10},{4,12},{6,14},{8,0},{10,2},{12,4},{14,6},{1,9},{3,11}... | collective-permute-start | bytes 172040 | tf_op jit(solution)/shard_map/ppermute | solution.py:129
  48.0 9.7 %collective-permute-start.12 = (bf16[8,3584]{1,0:T(8,128)(2,1)S(1)}, bf16[8,3584]{1,0:T(8,128)(2,1)S(1)}, u32[]{:S(2)}, u32[]{:S(2)}) collective-permute-start(bf16[8,3584]{1,0:T(8,128)(2,1)S(1)} %get-tuple-element.40), channel_id=1, source_target_pairs={{0,10},{2,8},{4,14},{6,12},{8,2},{10,0},{12,6},{14,4},{1,11},{3,9}... | collective-permute-start | bytes 172040 | tf_op jit(solution)/shard_map/ppermute | solution.py:129
  49.5 8.2 %collective-permute-start.13 = (bf16[8,3584]{1,0:T(8,128)(2,1)S(1)}, bf16[8,3584]{1,0:T(8,128)(2,1)S(1)}, u32[]{:S(2)}, u32[]{:S(2)}) collective-permute-start(bf16[8,3584]{1,0:T(8,128)(2,1)S(1)} %get-tuple-element.41), channel_id=1, source_target_pairs={{0,12},{2,14},{4,8},{6,10},{8,4},{10,6},{12,0},{14,2},{1,13},{3,15... | collective-permute-start | bytes 172040 | tf_op jit(solution)/shard_map/ppermute | solution.py:129
  50.4 7.3 %collective-permute-start.14 = (bf16[8,3584]{1,0:T(8,128)(2,1)S(1)}, bf16[8,3584]{1,0:T(8,128)(2,1)S(1)}, u32[]{:S(2)}, u32[]{:S(2)}) collective-permute-start(bf16[8,3584]{1,0:T(8,128)(2,1)S(1)} %get-tuple-element.42), channel_id=1, source_target_pairs={{0,14},{2,12},{4,10},{6,8},{8,6},{10,4},{12,2},{14,0},{1,15},{3,13... | collective-permute-start | bytes 172040 | tf_op jit(solution)/shard_map/ppermute | solution.py:129

commit v2 on v1

v2 whole, which is shorter than its diff:
```python
import functools

import jax
import jax.numpy as jnp
from jax import lax
from jax.experimental import pallas as pl
from jax.experimental.pallas import tpu as pltpu
from jax.sharding import PartitionSpec as P

HIDDEN_SIZE = 2048
ROUTED = 256
ORDER = (0, 4, 5, 6, 7, 2, 3, 1)
BF16 = jnp.bfloat16
F32 = jnp.float32
VMEM = pl.BlockSpec(memory_space=pltpu.VMEM)


def params(*arrays):
    size = sum(a.size * a.dtype.itemsize for a in arrays)
    return pltpu.CompilerParams(vmem_limit_bytes=int(2 * size) + (6 << 20))


def shape(dims, dtype):
    return jax.ShapeDtypeStruct(dims, dtype)


def tiles(total, size):
    return [(at, min(size, total - at)) for at in range(0, total, size)]


def join(blocks):
    if len(blocks) == 1:
        return blocks[0]
    return jnp.concatenate([b.astype(F32) for b in blocks], axis=0).astype(BF16)


def padded(x):
    short = 128 - x.shape[0]
    return x if short <= 0 else jnp.concatenate([x, jnp.zeros((short, x.shape[1]), x.dtype)], axis=0)


def partner(place):
    return sum(jnp.where(place == at, j, 0) for at, j in enumerate(ORDER) if j)


def spread(refs, value, at, size):
    rows = value.shape[0] // len(refs)
    for j, ref in enumerate(refs):
        ref[:, at : at + size] = value[j * rows : (j + 1) * rows].astype(BF16)


def route_kernel(slots, split, direct, ids_hbm, weight_hbm, tokens_hbm, share_ref, *rest_refs):
    *block_refs, ids_ref, weight_ref, tokens_ref, sems = rest_refs
    top, tokens = ids_ref.shape
    columns = tiles(tokens_ref.shape[1], 512)
    copies = [
        pltpu.make_async_copy(ids_hbm, ids_ref, sems.at[0]),
        pltpu.make_async_copy(weight_hbm, weight_ref, sems.at[1]),
    ] + [
        pltpu.make_async_copy(
            tokens_hbm.at[:, at : at + size], tokens_ref.at[:, at : at + size], sems.at[2 + i]
        )
        for i, (at, size) in enumerate(columns)
    ]
    for copy in copies:
        copy.start()
    copies[0].wait()
    copies[1].wait()
    full = share_ref.shape[0]
    rows = full // split

    def named(count, per):
        expert = lax.broadcasted_iota(jnp.int32, (count, tokens), 0) // per
        if direct:
            expert = partner(expert) ^ lax.axis_index("expert")
        hit = jnp.zeros((count, tokens), F32)
        scale = jnp.zeros((count, tokens), F32)
        for k in range(top):
            same = ids_ref[k : k + 1, :] == expert
            hit = jnp.where(same, 1.0, hit)
            scale = jnp.where(same, weight_ref[k : k + 1, :], scale)
        earlier = lax.broadcasted_iota(jnp.int32, (tokens, tokens), 0) < lax.broadcasted_iota(
            jnp.int32, (tokens, tokens), 1
        )
        before = jnp.dot(
            hit.astype(BF16), earlier.astype(F32).astype(BF16), preferred_element_type=F32
        ).astype(jnp.int32)
        slot = lax.broadcasted_iota(jnp.int32, (count, tokens), 0) % slots
        return jnp.where(before == slot, hit, 0.0), scale

    chosen, scale = named(rows, slots)
    pick = chosen.astype(BF16)
    for i, (at, size) in enumerate(columns):
        copies[2 + i].wait()
        value = jnp.dot(pick, tokens_ref[:, at : at + size], preferred_element_type=F32)
        spread(block_refs, value, at, size)
    if split > 1:
        chosen, scale = named(full, slots * split)
    share_ref[...] = chosen * scale


def split_weights(share_ref, mix_ref):
    full = share_ref.shape[0]
    rest = share_ref[...].T
    for part in range(3):
        piece = rest.astype(BF16)
        mix_ref[:, part * full : (part + 1) * full] = piece
        rest = rest - piece.astype(F32)


def up_kernel(count, *refs):
    block_refs = refs[:count]
    share_ref, gate_ref, up_ref, own_ref, send_ref, mix_ref = refs[count:]
    split_weights(share_ref, mix_ref)
    hidden = gate_ref.shape[1]
    rows = own_ref.shape[0]
    x = padded(join([b[...] for b in block_refs]))
    for low, high in tiles(x.shape[0], 256):
        for part, w_ref in enumerate((gate_ref, up_ref)):
            for at, size in tiles(hidden, 512):
                value = jnp.dot(
                    x[low : low + high], w_ref[:, at : at + size], preferred_element_type=F32
                )[: min(high, rows)]
                to = part * hidden + at
                own_ref[low : low + value.shape[0], to : to + size] = value
                send_ref[low : low + value.shape[0], to : to + size] = value.astype(BF16)


def down_kernel(own_ref, other_ref, down_ref, *block_refs):
    rows, hidden = own_ref.shape[0], down_ref.shape[0]
    total = own_ref[...] + other_ref[...].astype(F32)
    gate, up = total[:, :hidden], total[:, hidden:]
    act = padded((gate / (1.0 + jnp.exp(-gate)) * up).astype(BF16))
    for at, size in tiles(down_ref.shape[1], 512):
        value = jnp.dot(act, down_ref[:, at : at + size], preferred_element_type=F32)[:rows]
        spread(block_refs, value, at, size)


def mix_kernel(count, mix_ref, *refs):
    block_refs, (out_hbm, out_ref, sems) = refs[:count], refs[count:]
    mix = mix_ref[...]
    copies = []
    for i, (at, size) in enumerate(tiles(out_ref.shape[1], 512)):
        part = join([b[:, at : at + size] for b in block_refs])
        value = jnp.dot(
            mix, jnp.concatenate([part] * 3, axis=0), preferred_element_type=F32
        )
        out_ref[:, at : at + size] = value.astype(BF16)
        copy = pltpu.make_async_copy(
            out_ref.at[:, at : at + size], out_hbm.at[:, at : at + size], sems.at[i]
        )
        copy.start()
        copies.append(copy)
    for copy in copies:
        copy.wait()


def swap(blocks, devices):
    return [
        lax.ppermute(block, "expert", [(i, i ^ j) for i in range(devices)]) if j else block
        for block, j in zip(blocks, ORDER)
    ]


def local(tokens, expert_ids, route_weight, gate_weight, up_weight, down_weight):
    devices = lax.axis_size("expert")
    split = HIDDEN_SIZE // gate_weight.shape[2]
    experts = devices // split
    count, width = tokens.shape
    top = expert_ids.shape[1]
    slots = min(max(4, 2 * count * top // ROUTED), count)
    hidden = gate_weight.shape[2]
    rows = devices * slots
    direct = split == 1 and devices == len(ORDER)
    near = functools.partial(pltpu.with_memory_space_constraint, memory_space=pltpu.VMEM)
    far = functools.partial(pltpu.with_memory_space_constraint, memory_space=pltpu.HBM)

    parts = devices if direct else 1
    sent = experts * slots // parts
    share, *send = pl.pallas_call(
        functools.partial(route_kernel, slots, split, direct),
        in_specs=[pl.BlockSpec(memory_space=pltpu.HBM)] * 3,
        out_specs=[VMEM] * (1 + parts),
        out_shape=[shape((rows, count), F32)] + [shape((sent, width), BF16)] * parts,
        scratch_shapes=[
            pltpu.VMEM((top, count), jnp.int32),
            pltpu.VMEM((top, count), F32),
            pltpu.VMEM((count, width), BF16),
            pltpu.SemaphoreType.DMA((2 + pl.cdiv(width, 512),)),
        ],
        compiler_params=params(tokens, shape((count, 8 * rows), F32)),
        cost_estimate=pl.CostEstimate(flops=int(3e10), bytes_accessed=0, transcendentals=0),
        name="route",
    )(far(expert_ids.T), far(route_weight.T), far(tokens))
    if direct:
        arrived = swap(send, devices)
    else:
        spread_out = jnp.repeat(send[0].reshape(experts, slots, width), split, axis=0)
        arrived = [
            lax.all_to_all(spread_out, "expert", 0, 0, tiled=True).reshape(rows, width)
        ]

    own, give, mix = pl.pallas_call(
        functools.partial(up_kernel, parts),
        in_specs=[VMEM] * (parts + 3),
        out_specs=[VMEM] * 3,
        out_shape=[
            shape((rows, 2 * hidden), F32),
            shape((rows, 2 * hidden), BF16),
            shape((count, 3 * rows), BF16),
        ],
        compiler_params=params(shape((rows, width), F32), shape((rows, 2 * hidden), F32)),
        name="up",
    )(*arrived, share, near(gate_weight[0]), near(up_weight[0]))
    cores = lax.axis_size("tensor")
    other = lax.ppermute(give, "tensor", [(i, (i + 1) % cores) for i in range(cores)])
    answer = pl.pallas_call(
        down_kernel,
        in_specs=[VMEM] * 3,
        out_specs=[VMEM] * parts,
        out_shape=[shape((rows // parts, width), BF16)] * parts,
        compiler_params=params(shape((rows, 4 * hidden), F32), shape((rows, width), F32)),
        name="down",
    )(own, other, near(down_weight[0]))
    if direct:
        back = swap(answer, devices)
    else:
        back = [
            lax.all_to_all(
                answer[0].reshape(devices, slots, width), "expert", 0, 0, tiled=True
            ).reshape(rows, width)
        ]
    return pl.pallas_call(
        functools.partial(mix_kernel, parts),
        in_specs=[VMEM] * (1 + parts),
        out_specs=pl.BlockSpec(memory_space=pltpu.HBM),
        scratch_shapes=[
            pltpu.VMEM((count, width), BF16),
            pltpu.SemaphoreType.DMA((pl.cdiv(width, 512),)),
        ],
        out_shape=shape((count, width), BF16),
        compiler_params=params(mix, tokens, shape((rows, width), BF16)),
        name="mix",
    )(mix, *back)


def solution(mesh):
    return jax.shard_map(
        local,
        mesh=mesh,
        in_specs=(
            P(("groups", "expert"), "tensor"),
            P(("groups", "expert"), None),
            P(("groups", "expert"), None),
            P("expert", "tensor", None),
            P("expert", "tensor", None),
            P("expert", None, "tensor"),
        ),
        out_specs=P(("groups", "expert"), "tensor"),
        check_vma=False,
    )
```

time: 59.8 us -> 45.2 us (0.76)
  local copies, waits for them, and re-layouts: 13.1 us -> 0.01 us
  waiting for transfers between devices: 12.3 us -> 9.72 us
  starting transfers between devices: 23.8 us -> 25.7 us
  Pallas kernels: 10.3 us -> 9.49 us
    unnamed x10 -> x6, local copies, waits for them, and re-layouts: 13.1 us -> 0.01 us
    ppermute x14, waiting for transfers between devices: 10.4 us -> 7.82 us  [swap(): lax.ppermute(block, 'expert', [(i, i ^ j) for i in range(devices)])]
    ppermute x14, starting transfers between devices: 23.7 us -> 25.7 us  [swap(): lax.ppermute(block, 'expert', [(i, i ^ j) for i in range(devices)])]
    pallas_call x1, Pallas kernels: 0.73 us -> 2.24 us  [local(): pl.pallas_call(functools.partial(route_kernel, slots, split, direct), in_...]
    pallas_call x1, Pallas kernels: 5.19 us -> 3.99 us  [local(): pl.pallas_call(functools.partial(up_kernel, parts), in_specs=[VMEM] * (pa...]
    pallas_call x1, Pallas kernels: 1.83 us -> 1.17 us  [local(): pl.pallas_call(functools.partial(mix_kernel, parts), in_specs=[VMEM] * (1...]
  transfers between devices with their start and end apart: 15 -> 15, of which waited for: 4 -> 8; matrix products, arithmetic and copies ran while one was open for 0% -> 0% of each run, Pallas kernels for 0% -> 0%
where the time goes in v2:
time: 45.2 us; the launch traced here: 45 us
  starting transfers between devices  25.7 us (57%)
  waiting for transfers between devices  9.72 us (22%)
  Pallas kernels  9.49 us (21%)
    ppermute x14, starting transfers between devices, swap(): lax.ppermute(block, 'expert', [(i, i ^ j) for i in range(devices)])  25.7 us
    ppermute x14, waiting for transfers between devices, swap(): lax.ppermute(block, 'expert', [(i, i ^ j) for i in range(devices)])  7.82 us
    pallas_call x1, Pallas kernels, local(): pl.pallas_call(functools.partial(up_kernel, parts), in_specs=[VMEM] * (pa...  3.99 us
    pallas_call x1, Pallas kernels, local(): pl.pallas_call(functools.partial(route_kernel, slots, split, direct), in_...  2.24 us
    pallas_call x1, Pallas kernels, local(): pl.pallas_call(down_kernel, in_specs=[VMEM] * 3, out_specs=[VMEM] * parts...  2.09 us
    ppermute x1, waiting for transfers between devices, local(): lax.ppermute(give, 'tensor', [(i, (i + 1) % cores) for i in range(cores)])  1.9 us
    pallas_call x1, Pallas kernels, local(): pl.pallas_call(functools.partial(mix_kernel, parts), in_specs=[VMEM] * (1...  1.17 us
  transfers between devices with their start and end apart: 15, of which 8 were waited for; matrix products, arithmetic and copies ran while one was open for 0% of the time, Pallas kernels for 0%

profile of v2, /device:TPU:0, one launch (start us, length us, event | category | flops | bytes accessed | tf_op | source)
XLA Modules:
  0.0 45.0 jit_solution(3963754097392135243)
XLA Ops:
  0.0 2.2 %route.1 = (f32[64,128]{1,0:T(8,128)S(1)}, bf16[8,3584]{1,0:T(8,128)(2,1)S(1)}, bf16[8,3584]{1,0:T(8,128)(2,1)S(1)}, bf16[8,3584]{1,0:T(8,128)(2,1)S(1)}, bf16[8...) custom-call(s32[8,128]{1,0:T(8,128)} %bitcast.8, ...), custom_call_target="tpu_custom_call" | custom-call | flops 30000001024 | tf_op jit(solution)/shard_map/route/pallas_call | solution.py:180
  2.3 4.1 %collective-permute-start = (bf16[8,3584]{1,0:T(8,128)(2,1)S(1)}, bf16[8,3584]{1,0:T(8,128)(2,1)S(1)}, u32[]{:S(2)}, u32[]{:S(2)}) collective-permute-start(bf16[8,3584]{1,0:T(8,128)(2,1)S(1)} %get-tuple-element.26), channel_id=1, source_target_pairs={{0,8},{2,10},{4,12},{6,14},{8,0},{10,2},{12,4},{14,6},{1,9},{3,11}... | collective-permute-start | bytes 172040 | tf_op jit(solution)/shard_map/ppermute | solution.py:160
  6.4 1.3 %collective-permute-start.1 = (bf16[8,3584]{1,0:T(8,128)(2,1)S(1)}, bf16[8,3584]{1,0:T(8,128)(2,1)S(1)}, u32[]{:S(2)}, u32[]{:S(2)}) collective-permute-start(bf16[8,3584]{1,0:T(8,128)(2,1)S(1)} %get-tuple-element.27), channel_id=1, source_target_pairs={{0,10},{2,8},{4,14},{6,12},{8,2},{10,0},{12,6},{14,4},{1,11},{3,9}... | collective-permute-start | bytes 172040 | tf_op jit(solution)/shard_map/ppermute | solution.py:160
  7.6 3.6 %collective-permute-start.2 = (bf16[8,3584]{1,0:T(8,128)(2,1)S(1)}, bf16[8,3584]{1,0:T(8,128)(2,1)S(1)}, u32[]{:S(2)}, u32[]{:S(2)}) collective-permute-start(bf16[8,3584]{1,0:T(8,128)(2,1)S(1)} %get-tuple-element.28), channel_id=1, source_target_pairs={{0,12},{2,14},{4,8},{6,10},{8,4},{10,6},{12,0},{14,2},{1,13},{3,15... | collective-permute-start | bytes 172040 | tf_op jit(solution)/shard_map/ppermute | solution.py:160
  11.2 3.1 %collective-permute-start.5 = (bf16[8,3584]{1,0:T(8,128)(2,1)S(1)}, bf16[8,3584]{1,0:T(8,128)(2,1)S(1)}, u32[]{:S(2)}, u32[]{:S(2)}) collective-permute-start(bf16[8,3584]{1,0:T(8,128)(2,1)S(1)} %get-tuple-element.31), channel_id=1, source_target_pairs={{0,6},{2,4},{4,2},{6,0},{8,14},{10,12},{12,10},{14,8},{1,7},{3,5},... | collective-permute-start | bytes 172040 | tf_op jit(solution)/shard_map/ppermute | solution.py:160
  14.4 0.7 %collective-permute-done.1.refs_2_ = bf16[8,3584]{1,0:T(8,128)(2,1)S(1)} collective-permute-done((bf16[8,3584]{1,0:T(8,128)(2,1)S(1)}, bf16[8,3584]{1,0:T(8,128)(2,1)S(1)}, u32[]{:S(2)}, u32[]{:S(2)}) %collective-permute-start.1) | collective-permute-done | bytes 57376 | tf_op jit(solution)/shard_map/ppermute | solution.py:160
  15.1 2.3 %collective-permute-start.6 = (bf16[8,3584]{1,0:T(8,128)(2,1)S(1)}, bf16[8,3584]{1,0:T(8,128)(2,1)S(1)}, u32[]{:S(2)}, u32[]{:S(2)}) collective-permute-start(bf16[8,3584]{1,0:T(8,128)(2,1)S(1)} %get-tuple-element.32), channel_id=1, source_target_pairs={{0,2},{2,0},{4,6},{6,4},{8,10},{10,8},{12,14},{14,12},{1,3},{3,1},... | collective-permute-start | bytes 172040 | tf_op jit(solution)/shard_map/ppermute | solution.py:160
  17.3 1.0 %collective-permute-done.3.refs_4_ = bf16[8,3584]{1,0:T(8,128)(2,1)S(1)} collective-permute-done((bf16[8,3584]{1,0:T(8,128)(2,1)S(1)}, bf16[8,3584]{1,0:T(8,128)(2,1)S(1)}, u32[]{:S(2)}, u32[]{:S(2)}) %collective-permute-start.3) | collective-permute-done | bytes 57376 | tf_op jit(solution)/shard_map/ppermute | solution.py:160
  18.4 1.1 %collective-permute-done.6.refs_7_ = bf16[8,3584]{1,0:T(8,128)(2,1)S(1)} collective-permute-done((bf16[8,3584]{1,0:T(8,128)(2,1)S(1)}, bf16[8,3584]{1,0:T(8,128)(2,1)S(1)}, u32[]{:S(2)}, u32[]{:S(2)}) %collective-permute-start.6) | collective-permute-done | bytes 57376 | tf_op jit(solution)/shard_map/ppermute | solution.py:160
  19.5 4.0 %up.1 = (f32[64,4096]{1,0:T(8,128)S(1)}, bf16[64,4096]{1,0:T(8,128)(2,1)S(1)}, bf16[128,192]{1,0:T(8,128)(2,1)S(1)}) custom-call(bf16[8,3584]{1,0:T(8,128)(2,1)S(1)} %get-tuple-element.25.refs_0_, bf16[8,3584]{1,0:T(8,128)(2,1)S(1)} %collective-permute-done.refs_1_, bf16[8,3584]{1,0:T(8,128)(2,1)S(1)} %collective-permute-done.1.refs_2_, ...), custom_call_target="tpu_custom_call" | custom-call | tf_op jit(solution)/shard_map/up/pallas_call | solution.py:203
  23.5 0.1 collective-permute-start.7
  23.6 1.9 %collective-permute-done.7.other_ref = bf16[64,4096]{1,0:T(8,128)(2,1)S(1)} collective-permute-done((bf16[64,4096]{1,0:T(8,128)(2,1)S(1)}, bf16[64,4096]{1,0:T(8,128)(2,1)S(1)}, u32[]{:S(2)}, u32[]{:S(2)}) %collective-permute-start.7) | collective-permute-done | bytes 524320 | tf_op jit(solution)/shard_map/ppermute | solution.py:216
  25.5 2.1 %down.1 = (bf16[8,3584]{1,0:T(8,128)(2,1)S(1)}, bf16[8,3584]{1,0:T(8,128)(2,1)S(1)}, bf16[8,3584]{1,0:T(8,128)(2,1)S(1)}, bf16[8,3584]{1,0:T(8,128)(2,1)S(1)}, b...) custom-call(f32[64,4096]{1,0:T(8,128)S(1)} %get-tuple-element.35.own, ...), custom_call_target="tpu_custom_call" | custom-call | tf_op jit(solution)/shard_map/down/pallas_call | solution.py:217
  27.6 2.4 %collective-permute-start.8 = (bf16[8,3584]{1,0:T(8,128)(2,1)S(1)}, bf16[8,3584]{1,0:T(8,128)(2,1)S(1)}, u32[]{:S(2)}, u32[]{:S(2)}) collective-permute-start(bf16[8,3584]{1,0:T(8,128)(2,1)S(1)} %get-tuple-element.38), channel_id=1, source_target_pairs={{0,8},{2,10},{4,12},{6,14},{8,0},{10,2},{12,4},{14,6},{1,9},{3,11}... | collective-permute-start | bytes 172040 | tf_op jit(solution)/shard_map/ppermute | solution.py:160
  29.9 2.1 %collective-permute-start.9 = (bf16[8,3584]{1,0:T(8,128)(2,1)S(1)}, bf16[8,3584]{1,0:T(8,128)(2,1)S(1)}, u32[]{:S(2)}, u32[]{:S(2)}) collective-permute-start(bf16[8,3584]{1,0:T(8,128)(2,1)S(1)} %get-tuple-element.39), channel_id=1, source_target_pairs={{0,10},{2,8},{4,14},{6,12},{8,2},{10,0},{12,6},{14,4},{1,11},{3,9}... | collective-permute-start | bytes 172040 | tf_op jit(solution)/shard_map/ppermute | solution.py:160
  32.0 2.1 %collective-permute-start.10 = (bf16[8,3584]{1,0:T(8,128)(2,1)S(1)}, bf16[8,3584]{1,0:T(8,128)(2,1)S(1)}, u32[]{:S(2)}, u32[]{:S(2)}) collective-permute-start(bf16[8,3584]{1,0:T(8,128)(2,1)S(1)} %get-tuple-element.40), channel_id=1, source_target_pairs={{0,12},{2,14},{4,8},{6,10},{8,4},{10,6},{12,0},{14,2},{1,13},{3,15... | collective-permute-start | bytes 172040 | tf_op jit(solution)/shard_map/ppermute | solution.py:160
  34.1 1.2 %collective-permute-start.11 = (bf16[8,3584]{1,0:T(8,128)(2,1)S(1)}, bf16[8,3584]{1,0:T(8,128)(2,1)S(1)}, u32[]{:S(2)}, u32[]{:S(2)}) collective-permute-start(bf16[8,3584]{1,0:T(8,128)(2,1)S(1)} %get-tuple-element.41), channel_id=1, source_target_pairs={{0,14},{2,12},{4,10},{6,8},{8,6},{10,4},{12,2},{14,0},{1,15},{3,13... | collective-permute-start | bytes 172040 | tf_op jit(solution)/shard_map/ppermute | solution.py:160
  35.3 3.5 %collective-permute-start.13 = (bf16[8,3584]{1,0:T(8,128)(2,1)S(1)}, bf16[8,3584]{1,0:T(8,128)(2,1)S(1)}, u32[]{:S(2)}, u32[]{:S(2)}) collective-permute-start(bf16[8,3584]{1,0:T(8,128)(2,1)S(1)} %get-tuple-element.43), channel_id=1, source_target_pairs={{0,6},{2,4},{4,2},{6,0},{8,14},{10,12},{12,10},{14,8},{1,7},{3,5},... | collective-permute-start | bytes 172040 | tf_op jit(solution)/shard_map/ppermute | solution.py:160
  38.8 0.9 %collective-permute-done.9.refs_2_ = bf16[8,3584]{1,0:T(8,128)(2,1)S(1)} collective-permute-done((bf16[8,3584]{1,0:T(8,128)(2,1)S(1)}, bf16[8,3584]{1,0:T(8,128)(2,1)S(1)}, u32[]{:S(2)}, u32[]{:S(2)}) %collective-permute-start.9) | collective-permute-done | bytes 57376 | tf_op jit(solution)/shard_map/ppermute | solution.py:160
  39.7 0.1 collective-permute-start.14
  39.8 1.4 %collective-permute-done.11.refs_4_ = bf16[8,3584]{1,0:T(8,128)(2,1)S(1)} collective-permute-done((bf16[8,3584]{1,0:T(8,128)(2,1)S(1)}, bf16[8,3584]{1,0:T(8,128)(2,1)S(1)}, u32[]{:S(2)}, u32[]{:S(2)}) %collective-permute-start.11) | collective-permute-done | bytes 57376 | tf_op jit(solution)/shard_map/ppermute | solution.py:160
  41.1 1.3 %collective-permute-done.13.refs_6_ = bf16[8,3584]{1,0:T(8,128)(2,1)S(1)} collective-permute-done((bf16[8,3584]{1,0:T(8,128)(2,1)S(1)}, bf16[8,3584]{1,0:T(8,128)(2,1)S(1)}, u32[]{:S(2)}, u32[]{:S(2)}) %collective-permute-start.13) | collective-permute-done | bytes 57376 | tf_op jit(solution)/shard_map/ppermute | solution.py:160
  42.4 1.4 %collective-permute-done.14.refs_7_ = bf16[8,3584]{1,0:T(8,128)(2,1)S(1)} collective-permute-done((bf16[8,3584]{1,0:T(8,128)(2,1)S(1)}, bf16[8,3584]{1,0:T(8,128)(2,1)S(1)}, u32[]{:S(2)}, u32[]{:S(2)}) %collective-permute-start.14) | collective-permute-done | bytes 57376 | tf_op jit(solution)/shard_map/ppermute | solution.py:160
  43.8 1.2 %mix.1 = bf16[128,3584]{1,0:T(8,128)(2,1)} custom-call(bf16[128,192]{1,0:T(8,128)(2,1)S(1)} %get-tuple-element.34.mix_ref, bf16[8,3584]{1,0:T(8,128)(2,1)S(1)} %get-tuple-element.37.refs_0_, bf16[8,3584]{1,0:T(8,128)(2,1)S(1)} %collective-permute-done.8.refs_1_, bf16[8,3584]{1,0:T(8,128)(2,1)S(1)} %collective-permute-done.9.refs_2_, ...), custom_call_target="tpu_custom_call" | custom-call | tf_op jit(solution)/shard_map/mix/pallas_call | solution.py:233
  (16 shorter events, 0.1 us)
Async XLA Ops:
  0.0 19.5 %copy-start = (bf16[1,3584,2048]{2,1,0:T(8,128)(2,1)S(1)}, bf16[1,3584,2048]{2,1,0:T(8,128)(2,1)}, u32[]{:S(2)}) copy-start(bf16[1,3584,2048]{2,1,0:T(8,128)(2,1)} %param.9) | copy-start | bytes 44040196
  0.0 19.5 %copy-start.1 = (bf16[1,3584,2048]{2,1,0:T(8,128)(2,1)S(1)}, bf16[1,3584,2048]{2,1,0:T(8,128)(2,1)}, u32[]{:S(2)}) copy-start(bf16[1,3584,2048]{2,1,0:T(8,128)(2,1)} %param.10) | copy-start | bytes 44040196
  2.3 9.0 %collective-permute-start = (bf16[8,3584]{1,0:T(8,128)(2,1)S(1)}, bf16[8,3584]{1,0:T(8,128)(2,1)S(1)}, u32[]{:S(2)}, u32[]{:S(2)}) collective-permute-start(bf16[8,3584]{1,0:T(8,128)(2,1)S(1)} %get-tuple-element.26), channel_id=1, source_target_pairs={{0,8},{2,10},{4,12},{6,14},{8,0},{10,2},{12,4},{14,6},{1,9},{3,11}... | collective-permute-start | bytes 172040 | tf_op jit(solution)/shard_map/ppermute | solution.py:160
  6.4 8.7 %collective-permute-start.1 = (bf16[8,3584]{1,0:T(8,128)(2,1)S(1)}, bf16[8,3584]{1,0:T(8,128)(2,1)S(1)}, u32[]{:S(2)}, u32[]{:S(2)}) collective-permute-start(bf16[8,3584]{1,0:T(8,128)(2,1)S(1)} %get-tuple-element.27), channel_id=1, source_target_pairs={{0,10},{2,8},{4,14},{6,12},{8,2},{10,0},{12,6},{14,4},{1,11},{3,9}... | collective-permute-start | bytes 172040 | tf_op jit(solution)/shard_map/ppermute | solution.py:160
  7.6 9.7 %collective-permute-start.2 = (bf16[8,3584]{1,0:T(8,128)(2,1)S(1)}, bf16[8,3584]{1,0:T(8,128)(2,1)S(1)}, u32[]{:S(2)}, u32[]{:S(2)}) collective-permute-start(bf16[8,3584]{1,0:T(8,128)(2,1)S(1)} %get-tuple-element.28), channel_id=1, source_target_pairs={{0,12},{2,14},{4,8},{6,10},{8,4},{10,6},{12,0},{14,2},{1,13},{3,15... | collective-permute-start | bytes 172040 | tf_op jit(solution)/shard_map/ppermute | solution.py:160
  11.2 7.1 %collective-permute-start.3 = (bf16[8,3584]{1,0:T(8,128)(2,1)S(1)}, bf16[8,3584]{1,0:T(8,128)(2,1)S(1)}, u32[]{:S(2)}, u32[]{:S(2)}) collective-permute-start(bf16[8,3584]{1,0:T(8,128)(2,1)S(1)} %get-tuple-element.29), channel_id=1, source_target_pairs={{0,14},{2,12},{4,10},{6,8},{8,6},{10,4},{12,2},{14,0},{1,15},{3,13... | collective-permute-start | bytes 172040 | tf_op jit(solution)/shard_map/ppermute | solution.py:160
  11.2 7.1 %collective-permute-start.4 = (bf16[8,3584]{1,0:T(8,128)(2,1)S(1)}, bf16[8,3584]{1,0:T(8,128)(2,1)S(1)}, u32[]{:S(2)}, u32[]{:S(2)}) collective-permute-start(bf16[8,3584]{1,0:T(8,128)(2,1)S(1)} %get-tuple-element.30), channel_id=1, source_target_pairs={{0,4},{2,6},{4,0},{6,2},{8,12},{10,14},{12,8},{14,10},{1,5},{3,7},... | collective-permute-start | bytes 172040 | tf_op jit(solution)/shard_map/ppermute | solution.py:160
  11.2 7.1 %collective-permute-start.5 = (bf16[8,3584]{1,0:T(8,128)(2,1)S(1)}, bf16[8,3584]{1,0:T(8,128)(2,1)S(1)}, u32[]{:S(2)}, u32[]{:S(2)}) collective-permute-start(bf16[8,3584]{1,0:T(8,128)(2,1)S(1)} %get-tuple-element.31), channel_id=1, source_target_pairs={{0,6},{2,4},{4,2},{6,0},{8,14},{10,12},{12,10},{14,8},{1,7},{3,5},... | collective-permute-start | bytes 172040 | tf_op jit(solution)/shard_map/ppermute | solution.py:160
  15.1 4.4 %collective-permute-start.6 = (bf16[8,3584]{1,0:T(8,128)(2,1)S(1)}, bf16[8,3584]{1,0:T(8,128)(2,1)S(1)}, u32[]{:S(2)}, u32[]{:S(2)}) collective-permute-start(bf16[8,3584]{1,0:T(8,128)(2,1)S(1)} %get-tuple-element.32), channel_id=1, source_target_pairs={{0,2},{2,0},{4,6},{6,4},{8,10},{10,8},{12,14},{14,12},{1,3},{3,1},... | collective-permute-start | bytes 172040 | tf_op jit(solution)/shard_map/ppermute | solution.py:160
  19.5 6.0 %copy-start.2 = (bf16[1,2048,3584]{2,1,0:T(8,128)(2,1)S(1)}, bf16[1,2048,3584]{2,1,0:T(8,128)(2,1)}, u32[]{:S(2)}) copy-start(bf16[1,2048,3584]{2,1,0:T(8,128)(2,1)} %param.11) | copy-start | bytes 44040196
  23.5 2.0 %collective-permute-start.7 = (bf16[64,4096]{1,0:T(8,128)(2,1)S(1)}, bf16[64,4096]{1,0:T(8,128)(2,1)S(1)}, u32[]{:S(2)}, u32[]{:S(2)}) collective-permute-start(bf16[64,4096]{1,0:T(8,128)(2,1)S(1)} %get-tuple-element.36), channel_id=1, source_target_pairs={{0,1},{1,0},{2,3},{3,2},{4,5},{5,4},{6,7},{7,6},{8,9},{9,8},{10,11... | collective-permute-start | bytes 1572872 | tf_op jit(solution)/shard_map/ppermute | solution.py:216
  27.6 7.7 %collective-permute-start.8 = (bf16[8,3584]{1,0:T(8,128)(2,1)S(1)}, bf16[8,3584]{1,0:T(8,128)(2,1)S(1)}, u32[]{:S(2)}, u32[]{:S(2)}) collective-permute-start(bf16[8,3584]{1,0:T(8,128)(2,1)S(1)} %get-tuple-element.38), channel_id=1, source_target_pairs={{0,8},{2,10},{4,12},{6,14},{8,0},{10,2},{12,4},{14,6},{1,9},{3,11}... | collective-permute-start | bytes 172040 | tf_op jit(solution)/shard_map/ppermute | solution.py:160
  29.9 9.7 %collective-permute-start.9 = (bf16[8,3584]{1,0:T(8,128)(2,1)S(1)}, bf16[8,3584]{1,0:T(8,128)(2,1)S(1)}, u32[]{:S(2)}, u32[]{:S(2)}) collective-permute-start(bf16[8,3584]{1,0:T(8,128)(2,1)S(1)} %get-tuple-element.39), channel_id=1, source_target_pairs={{0,10},{2,8},{4,14},{6,12},{8,2},{10,0},{12,6},{14,4},{1,11},{3,9}... | collective-permute-start | bytes 172040 | tf_op jit(solution)/shard_map/ppermute | solution.py:160
  32.0 7.7 %collective-permute-start.10 = (bf16[8,3584]{1,0:T(8,128)(2,1)S(1)}, bf16[8,3584]{1,0:T(8,128)(2,1)S(1)}, u32[]{:S(2)}, u32[]{:S(2)}) collective-permute-start(bf16[8,3584]{1,0:T(8,128)(2,1)S(1)} %get-tuple-element.40), channel_id=1, source_target_pairs={{0,12},{2,14},{4,8},{6,10},{8,4},{10,6},{12,0},{14,2},{1,13},{3,15... | collective-permute-start | bytes 172040 | tf_op jit(solution)/shard_map/ppermute | solution.py:160
  34.1 7.0 %collective-permute-start.11 = (bf16[8,3584]{1,0:T(8,128)(2,1)S(1)}, bf16[8,3584]{1,0:T(8,128)(2,1)S(1)}, u32[]{:S(2)}, u32[]{:S(2)}) collective-permute-start(bf16[8,3584]{1,0:T(8,128)(2,1)S(1)} %get-tuple-element.41), channel_id=1, source_target_pairs={{0,14},{2,12},{4,10},{6,8},{8,6},{10,4},{12,2},{14,0},{1,15},{3,13... | collective-permute-start | bytes 172040 | tf_op jit(solution)/shard_map/ppermute | solution.py:160
  35.3 5.8 %collective-permute-start.12 = (bf16[8,3584]{1,0:T(8,128)(2,1)S(1)}, bf16[8,3584]{1,0:T(8,128)(2,1)S(1)}, u32[]{:S(2)}, u32[]{:S(2)}) collective-permute-start(bf16[8,3584]{1,0:T(8,128)(2,1)S(1)} %get-tuple-element.42), channel_id=1, source_target_pairs={{0,4},{2,6},{4,0},{6,2},{8,12},{10,14},{12,8},{14,10},{1,5},{3,7},... | collective-permute-start | bytes 172040 | tf_op jit(solution)/shard_map/ppermute | solution.py:160
  35.3 7.1 %collective-permute-start.13 = (bf16[8,3584]{1,0:T(8,128)(2,1)S(1)}, bf16[8,3584]{1,0:T(8,128)(2,1)S(1)}, u32[]{:S(2)}, u32[]{:S(2)}) collective-permute-start(bf16[8,3584]{1,0:T(8,128)(2,1)S(1)} %get-tuple-element.43), channel_id=1, source_target_pairs={{0,6},{2,4},{4,2},{6,0},{8,14},{10,12},{12,10},{14,8},{1,7},{3,5},... | collective-permute-start | bytes 172040 | tf_op jit(solution)/shard_map/ppermute | solution.py:160
  39.7 4.2 %collective-permute-start.14 = (bf16[8,3584]{1,0:T(8,128)(2,1)S(1)}, bf16[8,3584]{1,0:T(8,128)(2,1)S(1)}, u32[]{:S(2)}, u32[]{:S(2)}) collective-permute-start(bf16[8,3584]{1,0:T(8,128)(2,1)S(1)} %get-tuple-element.44), channel_id=1, source_target_pairs={{0,2},{2,0},{4,6},{6,4},{8,10},{10,8},{12,14},{14,12},{1,3},{3,1},... | collective-permute-start | bytes 172040 | tf_op jit(solution)/shard_map/ppermute | solution.py:160

commit v3 on v2

--- a/solution.py
+++ b/solution.py
@@ -9,7 +9,7 @@
 
 HIDDEN_SIZE = 2048
 ROUTED = 256
-ORDER = (0, 4, 5, 6, 7, 2, 3, 1)
+ORDER = (0, 7, 6, 5, 3, 4, 2, 1)
 BF16 = jnp.bfloat16
 F32 = jnp.float32
 VMEM = pl.BlockSpec(memory_space=pltpu.VMEM)

time: 45.2 us -> 42.5 us (0.940)
  starting transfers between devices: 25.7 us -> 23.8 us
  waiting for transfers between devices: 9.72 us -> 9.01 us
    ppermute x14, starting transfers between devices: 25.7 us -> 23.7 us  [swap(): lax.ppermute(block, 'expert', [(i, i ^ j) for i in range(devices)])]
    ppermute x14, waiting for transfers between devices: 7.82 us -> 7.11 us  [swap(): lax.ppermute(block, 'expert', [(i, i ^ j) for i in range(devices)])]
  transfers between devices with their start and end apart: 15 -> 15, of which waited for: 8 -> 9; matrix products, arithmetic and copies ran while one was open for 0% -> 0% of each run, Pallas kernels for 0% -> 0%
where the time goes in v3:
time: 42.5 us; the launch traced here: 42.4 us
  starting transfers between devices  23.8 us (56%)
  Pallas kernels  9.49 us (22%)
  waiting for transfers between devices  9.01 us (21%)
    ppermute x14, starting transfers between devices, swap(): lax.ppermute(block, 'expert', [(i, i ^ j) for i in range(devices)])  23.7 us
    ppermute x14, waiting for transfers between devices, swap(): lax.ppermute(block, 'expert', [(i, i ^ j) for i in range(devices)])  7.11 us
    pallas_call x1, Pallas kernels, local(): pl.pallas_call(functools.partial(up_kernel, parts), in_specs=[VMEM] * (pa...  4 us
    pallas_call x1, Pallas kernels, local(): pl.pallas_call(functools.partial(route_kernel, slots, split, direct), in_...  2.24 us
    pallas_call x1, Pallas kernels, local(): pl.pallas_call(down_kernel, in_specs=[VMEM] * 3, out_specs=[VMEM] * parts...  2.09 us
    ppermute x1, waiting for transfers between devices, local(): lax.ppermute(give, 'tensor', [(i, (i + 1) % cores) for i in range(cores)])  1.9 us
    pallas_call x1, Pallas kernels, local(): pl.pallas_call(functools.partial(mix_kernel, parts), in_specs=[VMEM] * (1...  1.17 us
  transfers between devices with their start and end apart: 15, of which 9 were waited for; matrix products, arithmetic and copies ran while one was open for 0% of the time, Pallas kernels for 0%

profile of v3, /device:TPU:0, one launch (start us, length us, event | category | flops | bytes accessed | tf_op | source)
XLA Modules:
  0.0 42.4 jit_solution(2747036398898180911)
XLA Ops:
  0.0 2.2 %route.1 = (f32[64,128]{1,0:T(8,128)S(1)}, bf16[8,3584]{1,0:T(8,128)(2,1)S(1)}, bf16[8,3584]{1,0:T(8,128)(2,1)S(1)}, bf16[8,3584]{1,0:T(8,128)(2,1)S(1)}, bf16[8...) custom-call(s32[8,128]{1,0:T(8,128)} %bitcast.8, ...), custom_call_target="tpu_custom_call" | custom-call | flops 30000001024 | tf_op jit(solution)/shard_map/route/pallas_call | solution.py:180
  2.3 6.0 %collective-permute-start = (bf16[8,3584]{1,0:T(8,128)(2,1)S(1)}, bf16[8,3584]{1,0:T(8,128)(2,1)S(1)}, u32[]{:S(2)}, u32[]{:S(2)}) collective-permute-start(bf16[8,3584]{1,0:T(8,128)(2,1)S(1)} %get-tuple-element.26), channel_id=1, source_target_pairs={{0,14},{2,12},{4,10},{6,8},{8,6},{10,4},{12,2},{14,0},{1,15},{3,13... | collective-permute-start | bytes 172040 | tf_op jit(solution)/shard_map/ppermute | solution.py:160
  8.3 0.2 collective-permute-start.1
  8.5 0.8 %collective-permute-start.2 = (bf16[8,3584]{1,0:T(8,128)(2,1)S(1)}, bf16[8,3584]{1,0:T(8,128)(2,1)S(1)}, u32[]{:S(2)}, u32[]{:S(2)}) collective-permute-start(bf16[8,3584]{1,0:T(8,128)(2,1)S(1)} %get-tuple-element.28), channel_id=1, source_target_pairs={{0,10},{2,8},{4,14},{6,12},{8,2},{10,0},{12,6},{14,4},{1,11},{3,9}... | collective-permute-start | bytes 172040 | tf_op jit(solution)/shard_map/ppermute | solution.py:160
  9.3 4.3 %collective-permute-start.3 = (bf16[8,3584]{1,0:T(8,128)(2,1)S(1)}, bf16[8,3584]{1,0:T(8,128)(2,1)S(1)}, u32[]{:S(2)}, u32[]{:S(2)}) collective-permute-start(bf16[8,3584]{1,0:T(8,128)(2,1)S(1)} %get-tuple-element.29), channel_id=1, source_target_pairs={{0,6},{2,4},{4,2},{6,0},{8,14},{10,12},{12,10},{14,8},{1,7},{3,5},... | collective-permute-start | bytes 172040 | tf_op jit(solution)/shard_map/ppermute | solution.py:160
  13.6 0.8 %collective-permute-start.5 = (bf16[8,3584]{1,0:T(8,128)(2,1)S(1)}, bf16[8,3584]{1,0:T(8,128)(2,1)S(1)}, u32[]{:S(2)}, u32[]{:S(2)}) collective-permute-start(bf16[8,3584]{1,0:T(8,128)(2,1)S(1)} %get-tuple-element.31), channel_id=1, source_target_pairs={{0,4},{2,6},{4,0},{6,2},{8,12},{10,14},{12,8},{14,10},{1,5},{3,7},... | collective-permute-start | bytes 172040 | tf_op jit(solution)/shard_map/ppermute | solution.py:160
  14.4 0.6 %collective-permute-done.1.refs_2_ = bf16[8,3584]{1,0:T(8,128)(2,1)S(1)} collective-permute-done((bf16[8,3584]{1,0:T(8,128)(2,1)S(1)}, bf16[8,3584]{1,0:T(8,128)(2,1)S(1)}, u32[]{:S(2)}, u32[]{:S(2)}) %collective-permute-start.1) | collective-permute-done | bytes 57376 | tf_op jit(solution)/shard_map/ppermute | solution.py:160
  14.9 0.4 collective-permute-start.6
  15.4 1.5 %collective-permute-done.2.refs_3_ = bf16[8,3584]{1,0:T(8,128)(2,1)S(1)} collective-permute-done((bf16[8,3584]{1,0:T(8,128)(2,1)S(1)}, bf16[8,3584]{1,0:T(8,128)(2,1)S(1)}, u32[]{:S(2)}, u32[]{:S(2)}) %collective-permute-start.2) | collective-permute-done | bytes 57376 | tf_op jit(solution)/shard_map/ppermute | solution.py:160
  16.8 0.8 %collective-permute-done.3.refs_4_ = bf16[8,3584]{1,0:T(8,128)(2,1)S(1)} collective-permute-done((bf16[8,3584]{1,0:T(8,128)(2,1)S(1)}, bf16[8,3584]{1,0:T(8,128)(2,1)S(1)}, u32[]{:S(2)}, u32[]{:S(2)}) %collective-permute-start.3) | collective-permute-done | bytes 57376 | tf_op jit(solution)/shard_map/ppermute | solution.py:160
  17.6 1.0 %collective-permute-done.4.refs_5_ = bf16[8,3584]{1,0:T(8,128)(2,1)S(1)} collective-permute-done((bf16[8,3584]{1,0:T(8,128)(2,1)S(1)}, bf16[8,3584]{1,0:T(8,128)(2,1)S(1)}, u32[]{:S(2)}, u32[]{:S(2)}) %collective-permute-start.4) | collective-permute-done | bytes 57376 | tf_op jit(solution)/shard_map/ppermute | solution.py:160
  18.7 0.4 %collective-permute-done.6.refs_7_ = bf16[8,3584]{1,0:T(8,128)(2,1)S(1)} collective-permute-done((bf16[8,3584]{1,0:T(8,128)(2,1)S(1)}, bf16[8,3584]{1,0:T(8,128)(2,1)S(1)}, u32[]{:S(2)}, u32[]{:S(2)}) %collective-permute-start.6) | collective-permute-done | bytes 57376 | tf_op jit(solution)/shard_map/ppermute | solution.py:160
  19.1 4.0 %up.1 = (f32[64,4096]{1,0:T(8,128)S(1)}, bf16[64,4096]{1,0:T(8,128)(2,1)S(1)}, bf16[128,192]{1,0:T(8,128)(2,1)S(1)}) custom-call(bf16[8,3584]{1,0:T(8,128)(2,1)S(1)} %get-tuple-element.25.refs_0_, bf16[8,3584]{1,0:T(8,128)(2,1)S(1)} %collective-permute-done.refs_1_, bf16[8,3584]{1,0:T(8,128)(2,1)S(1)} %collective-permute-done.1.refs_2_, ...), custom_call_target="tpu_custom_call" | custom-call | tf_op jit(solution)/shard_map/up/pallas_call | solution.py:203
  23.2 1.9 %collective-permute-done.7.other_ref = bf16[64,4096]{1,0:T(8,128)(2,1)S(1)} collective-permute-done((bf16[64,4096]{1,0:T(8,128)(2,1)S(1)}, bf16[64,4096]{1,0:T(8,128)(2,1)S(1)}, u32[]{:S(2)}, u32[]{:S(2)}) %collective-permute-start.7) | collective-permute-done | bytes 524320 | tf_op jit(solution)/shard_map/ppermute | solution.py:216
  25.1 2.1 %down.1 = (bf16[8,3584]{1,0:T(8,128)(2,1)S(1)}, bf16[8,3584]{1,0:T(8,128)(2,1)S(1)}, bf16[8,3584]{1,0:T(8,128)(2,1)S(1)}, bf16[8,3584]{1,0:T(8,128)(2,1)S(1)}, b...) custom-call(f32[64,4096]{1,0:T(8,128)S(1)} %get-tuple-element.35.own, ...), custom_call_target="tpu_custom_call" | custom-call | tf_op jit(solution)/shard_map/down/pallas_call | solution.py:217
  27.2 3.1 %collective-permute-start.8 = (bf16[8,3584]{1,0:T(8,128)(2,1)S(1)}, bf16[8,3584]{1,0:T(8,128)(2,1)S(1)}, u32[]{:S(2)}, u32[]{:S(2)}) collective-permute-start(bf16[8,3584]{1,0:T(8,128)(2,1)S(1)} %get-tuple-element.38), channel_id=1, source_target_pairs={{0,14},{2,12},{4,10},{6,8},{8,6},{10,4},{12,2},{14,0},{1,15},{3,13... | collective-permute-start | bytes 172040 | tf_op jit(solution)/shard_map/ppermute | solution.py:160
  30.3 0.7 %collective-permute-start.9 = (bf16[8,3584]{1,0:T(8,128)(2,1)S(1)}, bf16[8,3584]{1,0:T(8,128)(2,1)S(1)}, u32[]{:S(2)}, u32[]{:S(2)}) collective-permute-start(bf16[8,3584]{1,0:T(8,128)(2,1)S(1)} %get-tuple-element.39), channel_id=1, source_target_pairs={{0,12},{2,14},{4,8},{6,10},{8,4},{10,6},{12,0},{14,2},{1,13},{3,15... | collective-permute-start | bytes 172040 | tf_op jit(solution)/shard_map/ppermute | solution.py:160
  30.9 0.9 %collective-permute-start.10 = (bf16[8,3584]{1,0:T(8,128)(2,1)S(1)}, bf16[8,3584]{1,0:T(8,128)(2,1)S(1)}, u32[]{:S(2)}, u32[]{:S(2)}) collective-permute-start(bf16[8,3584]{1,0:T(8,128)(2,1)S(1)} %get-tuple-element.40), channel_id=1, source_target_pairs={{0,10},{2,8},{4,14},{6,12},{8,2},{10,0},{12,6},{14,4},{1,11},{3,9}... | collective-permute-start | bytes 172040 | tf_op jit(solution)/shard_map/ppermute | solution.py:160
  31.8 3.7 %collective-permute-start.11 = (bf16[8,3584]{1,0:T(8,128)(2,1)S(1)}, bf16[8,3584]{1,0:T(8,128)(2,1)S(1)}, u32[]{:S(2)}, u32[]{:S(2)}) collective-permute-start(bf16[8,3584]{1,0:T(8,128)(2,1)S(1)} %get-tuple-element.41), channel_id=1, source_target_pairs={{0,6},{2,4},{4,2},{6,0},{8,14},{10,12},{12,10},{14,8},{1,7},{3,5},... | collective-permute-start | bytes 172040 | tf_op jit(solution)/shard_map/ppermute | solution.py:160
  35.6 1.2 %collective-permute-start.13 = (bf16[8,3584]{1,0:T(8,128)(2,1)S(1)}, bf16[8,3584]{1,0:T(8,128)(2,1)S(1)}, u32[]{:S(2)}, u32[]{:S(2)}) collective-permute-start(bf16[8,3584]{1,0:T(8,128)(2,1)S(1)} %get-tuple-element.43), channel_id=1, source_target_pairs={{0,4},{2,6},{4,0},{6,2},{8,12},{10,14},{12,8},{14,10},{1,5},{3,7},... | collective-permute-start | bytes 172040 | tf_op jit(solution)/shard_map/ppermute | solution.py:160
  36.8 1.6 %collective-permute-start.14 = (bf16[8,3584]{1,0:T(8,128)(2,1)S(1)}, bf16[8,3584]{1,0:T(8,128)(2,1)S(1)}, u32[]{:S(2)}, u32[]{:S(2)}) collective-permute-start(bf16[8,3584]{1,0:T(8,128)(2,1)S(1)} %get-tuple-element.44), channel_id=1, source_target_pairs={{0,2},{2,0},{4,6},{6,4},{8,10},{10,8},{12,14},{14,12},{1,3},{3,1},... | collective-permute-start | bytes 172040 | tf_op jit(solution)/shard_map/ppermute | solution.py:160
  38.4 0.6 %collective-permute-done.10.refs_3_ = bf16[8,3584]{1,0:T(8,128)(2,1)S(1)} collective-permute-done((bf16[8,3584]{1,0:T(8,128)(2,1)S(1)}, bf16[8,3584]{1,0:T(8,128)(2,1)S(1)}, u32[]{:S(2)}, u32[]{:S(2)}) %collective-permute-start.10) | collective-permute-done | bytes 57376 | tf_op jit(solution)/shard_map/ppermute | solution.py:160
  39.0 2.1 %collective-permute-done.12.refs_5_ = bf16[8,3584]{1,0:T(8,128)(2,1)S(1)} collective-permute-done((bf16[8,3584]{1,0:T(8,128)(2,1)S(1)}, bf16[8,3584]{1,0:T(8,128)(2,1)S(1)}, u32[]{:S(2)}, u32[]{:S(2)}) %collective-permute-start.12) | collective-permute-done | bytes 57376 | tf_op jit(solution)/shard_map/ppermute | solution.py:160
  41.2 1.2 %mix.1 = bf16[128,3584]{1,0:T(8,128)(2,1)} custom-call(bf16[128,192]{1,0:T(8,128)(2,1)S(1)} %get-tuple-element.34.mix_ref, bf16[8,3584]{1,0:T(8,128)(2,1)S(1)} %get-tuple-element.37.refs_0_, bf16[8,3584]{1,0:T(8,128)(2,1)S(1)} %collective-permute-done.8.refs_1_, bf16[8,3584]{1,0:T(8,128)(2,1)S(1)} %collective-permute-done.9.refs_2_, ...), custom_call_target="tpu_custom_call" | custom-call | tf_op jit(solution)/shard_map/mix/pallas_call | solution.py:233
  (16 shorter events, 0.3 us)
Async XLA Ops:
  0.0 19.1 %copy-start = (bf16[1,3584,2048]{2,1,0:T(8,128)(2,1)S(1)}, bf16[1,3584,2048]{2,1,0:T(8,128)(2,1)}, u32[]{:S(2)}) copy-start(bf16[1,3584,2048]{2,1,0:T(8,128)(2,1)} %param.9) | copy-start | bytes 44040196
  0.0 19.1 %copy-start.1 = (bf16[1,3584,2048]{2,1,0:T(8,128)(2,1)S(1)}, bf16[1,3584,2048]{2,1,0:T(8,128)(2,1)}, u32[]{:S(2)}) copy-start(bf16[1,3584,2048]{2,1,0:T(8,128)(2,1)} %param.10) | copy-start | bytes 44040196
  2.3 11.3 %collective-permute-start = (bf16[8,3584]{1,0:T(8,128)(2,1)S(1)}, bf16[8,3584]{1,0:T(8,128)(2,1)S(1)}, u32[]{:S(2)}, u32[]{:S(2)}) collective-permute-start(bf16[8,3584]{1,0:T(8,128)(2,1)S(1)} %get-tuple-element.26), channel_id=1, source_target_pairs={{0,14},{2,12},{4,10},{6,8},{8,6},{10,4},{12,2},{14,0},{1,15},{3,13... | collective-permute-start | bytes 172040 | tf_op jit(solution)/shard_map/ppermute | solution.py:160
  8.3 6.6 %collective-permute-start.1 = (bf16[8,3584]{1,0:T(8,128)(2,1)S(1)}, bf16[8,3584]{1,0:T(8,128)(2,1)S(1)}, u32[]{:S(2)}, u32[]{:S(2)}) collective-permute-start(bf16[8,3584]{1,0:T(8,128)(2,1)S(1)} %get-tuple-element.27), channel_id=1, source_target_pairs={{0,12},{2,14},{4,8},{6,10},{8,4},{10,6},{12,0},{14,2},{1,13},{3,15... | collective-permute-start | bytes 172040 | tf_op jit(solution)/shard_map/ppermute | solution.py:160
  8.5 8.3 %collective-permute-start.2 = (bf16[8,3584]{1,0:T(8,128)(2,1)S(1)}, bf16[8,3584]{1,0:T(8,128)(2,1)S(1)}, u32[]{:S(2)}, u32[]{:S(2)}) collective-permute-start(bf16[8,3584]{1,0:T(8,128)(2,1)S(1)} %get-tuple-element.28), channel_id=1, source_target_pairs={{0,10},{2,8},{4,14},{6,12},{8,2},{10,0},{12,6},{14,4},{1,11},{3,9}... | collective-permute-start | bytes 172040 | tf_op jit(solution)/shard_map/ppermute | solution.py:160
  9.3 8.3 %collective-permute-start.3 = (bf16[8,3584]{1,0:T(8,128)(2,1)S(1)}, bf16[8,3584]{1,0:T(8,128)(2,1)S(1)}, u32[]{:S(2)}, u32[]{:S(2)}) collective-permute-start(bf16[8,3584]{1,0:T(8,128)(2,1)S(1)} %get-tuple-element.29), channel_id=1, source_target_pairs={{0,6},{2,4},{4,2},{6,0},{8,14},{10,12},{12,10},{14,8},{1,7},{3,5},... | collective-permute-start | bytes 172040 | tf_op jit(solution)/shard_map/ppermute | solution.py:160
  13.6 5.1 %collective-permute-start.4 = (bf16[8,3584]{1,0:T(8,128)(2,1)S(1)}, bf16[8,3584]{1,0:T(8,128)(2,1)S(1)}, u32[]{:S(2)}, u32[]{:S(2)}) collective-permute-start(bf16[8,3584]{1,0:T(8,128)(2,1)S(1)} %get-tuple-element.30), channel_id=1, source_target_pairs={{0,8},{2,10},{4,12},{6,14},{8,0},{10,2},{12,4},{14,6},{1,9},{3,11}... | collective-permute-start | bytes 172040 | tf_op jit(solution)/shard_map/ppermute | solution.py:160
  13.6 5.1 %collective-permute-start.5 = (bf16[8,3584]{1,0:T(8,128)(2,1)S(1)}, bf16[8,3584]{1,0:T(8,128)(2,1)S(1)}, u32[]{:S(2)}, u32[]{:S(2)}) collective-permute-start(bf16[8,3584]{1,0:T(8,128)(2,1)S(1)} %get-tuple-element.31), channel_id=1, source_target_pairs={{0,4},{2,6},{4,0},{6,2},{8,12},{10,14},{12,8},{14,10},{1,5},{3,7},... | collective-permute-start | bytes 172040 | tf_op jit(solution)/shard_map/ppermute | solution.py:160
  14.9 4.2 %collective-permute-start.6 = (bf16[8,3584]{1,0:T(8,128)(2,1)S(1)}, bf16[8,3584]{1,0:T(8,128)(2,1)S(1)}, u32[]{:S(2)}, u32[]{:S(2)}) collective-permute-start(bf16[8,3584]{1,0:T(8,128)(2,1)S(1)} %get-tuple-element.32), channel_id=1, source_target_pairs={{0,2},{2,0},{4,6},{6,4},{8,10},{10,8},{12,14},{14,12},{1,3},{3,1},... | collective-permute-start | bytes 172040 | tf_op jit(solution)/shard_map/ppermute | solution.py:160
  19.1 6.0 %copy-start.2 = (bf16[1,2048,3584]{2,1,0:T(8,128)(2,1)S(1)}, bf16[1,2048,3584]{2,1,0:T(8,128)(2,1)}, u32[]{:S(2)}) copy-start(bf16[1,2048,3584]{2,1,0:T(8,128)(2,1)} %param.11) | copy-start | bytes 44040196
  23.1 2.0 %collective-permute-start.7 = (bf16[64,4096]{1,0:T(8,128)(2,1)S(1)}, bf16[64,4096]{1,0:T(8,128)(2,1)S(1)}, u32[]{:S(2)}, u32[]{:S(2)}) collective-permute-start(bf16[64,4096]{1,0:T(8,128)(2,1)S(1)} %get-tuple-element.36), channel_id=1, source_target_pairs={{0,1},{1,0},{2,3},{3,2},{4,5},{5,4},{6,7},{7,6},{8,9},{9,8},{10,11... | collective-permute-start | bytes 1572872 | tf_op jit(solution)/shard_map/ppermute | solution.py:216
  27.2 8.4 %collective-permute-start.8 = (bf16[8,3584]{1,0:T(8,128)(2,1)S(1)}, bf16[8,3584]{1,0:T(8,128)(2,1)S(1)}, u32[]{:S(2)}, u32[]{:S(2)}) collective-permute-start(bf16[8,3584]{1,0:T(8,128)(2,1)S(1)} %get-tuple-element.38), channel_id=1, source_target_pairs={{0,14},{2,12},{4,10},{6,8},{8,6},{10,4},{12,2},{14,0},{1,15},{3,13... | collective-permute-start | bytes 172040 | tf_op jit(solution)/shard_map/ppermute | solution.py:160
  30.3 6.5 %collective-permute-start.9 = (bf16[8,3584]{1,0:T(8,128)(2,1)S(1)}, bf16[8,3584]{1,0:T(8,128)(2,1)S(1)}, u32[]{:S(2)}, u32[]{:S(2)}) collective-permute-start(bf16[8,3584]{1,0:T(8,128)(2,1)S(1)} %get-tuple-element.39), channel_id=1, source_target_pairs={{0,12},{2,14},{4,8},{6,10},{8,4},{10,6},{12,0},{14,2},{1,13},{3,15... | collective-permute-start | bytes 172040 | tf_op jit(solution)/shard_map/ppermute | solution.py:160
  30.9 8.0 %collective-permute-start.10 = (bf16[8,3584]{1,0:T(8,128)(2,1)S(1)}, bf16[8,3584]{1,0:T(8,128)(2,1)S(1)}, u32[]{:S(2)}, u32[]{:S(2)}) collective-permute-start(bf16[8,3584]{1,0:T(8,128)(2,1)S(1)} %get-tuple-element.40), channel_id=1, source_target_pairs={{0,10},{2,8},{4,14},{6,12},{8,2},{10,0},{12,6},{14,4},{1,11},{3,9}... | collective-permute-start | bytes 172040 | tf_op jit(solution)/shard_map/ppermute | solution.py:160
  31.8 7.1 %collective-permute-start.11 = (bf16[8,3584]{1,0:T(8,128)(2,1)S(1)}, bf16[8,3584]{1,0:T(8,128)(2,1)S(1)}, u32[]{:S(2)}, u32[]{:S(2)}) collective-permute-start(bf16[8,3584]{1,0:T(8,128)(2,1)S(1)} %get-tuple-element.41), channel_id=1, source_target_pairs={{0,6},{2,4},{4,2},{6,0},{8,14},{10,12},{12,10},{14,8},{1,7},{3,5},... | collective-permute-start | bytes 172040 | tf_op jit(solution)/shard_map/ppermute | solution.py:160
  35.6 5.5 %collective-permute-start.12 = (bf16[8,3584]{1,0:T(8,128)(2,1)S(1)}, bf16[8,3584]{1,0:T(8,128)(2,1)S(1)}, u32[]{:S(2)}, u32[]{:S(2)}) collective-permute-start(bf16[8,3584]{1,0:T(8,128)(2,1)S(1)} %get-tuple-element.42), channel_id=1, source_target_pairs={{0,8},{2,10},{4,12},{6,14},{8,0},{10,2},{12,4},{14,6},{1,9},{3,11}... | collective-permute-start | bytes 172040 | tf_op jit(solution)/shard_map/ppermute | solution.py:160
  35.6 5.6 %collective-permute-start.13 = (bf16[8,3584]{1,0:T(8,128)(2,1)S(1)}, bf16[8,3584]{1,0:T(8,128)(2,1)S(1)}, u32[]{:S(2)}, u32[]{:S(2)}) collective-permute-start(bf16[8,3584]{1,0:T(8,128)(2,1)S(1)} %get-tuple-element.43), channel_id=1, source_target_pairs={{0,4},{2,6},{4,0},{6,2},{8,12},{10,14},{12,8},{14,10},{1,5},{3,7},... | collective-permute-start | bytes 172040 | tf_op jit(solution)/shard_map/ppermute | solution.py:160
  36.8 4.4 %collective-permute-start.14 = (bf16[8,3584]{1,0:T(8,128)(2,1)S(1)}, bf16[8,3584]{1,0:T(8,128)(2,1)S(1)}, u32[]{:S(2)}, u32[]{:S(2)}) collective-permute-start(bf16[8,3584]{1,0:T(8,128)(2,1)S(1)} %get-tuple-element.44), channel_id=1, source_target_pairs={{0,2},{2,0},{4,6},{6,4},{8,10},{10,8},{12,14},{14,12},{1,3},{3,1},... | collective-permute-start | bytes 172040 | tf_op jit(solution)/shard_map/ppermute | solution.py:160

commit v4 on v3

--- a/solution.py
+++ b/solution.py
@@ -17,7 +17,7 @@
 
 def params(*arrays):
     size = sum(a.size * a.dtype.itemsize for a in arrays)
-    return pltpu.CompilerParams(vmem_limit_bytes=int(2 * size) + (6 << 20))
+    return pltpu.CompilerParams(vmem_limit_bytes=int(1.25 * size) + (3 << 20))
 
 
 def shape(dims, dtype):
@@ -49,25 +49,22 @@
         ref[:, at : at + size] = value[j * rows : (j + 1) * rows].astype(BF16)
 
 
-def route_kernel(slots, split, direct, ids_hbm, weight_hbm, tokens_hbm, share_ref, *rest_refs):
-    *block_refs, ids_ref, weight_ref, tokens_ref, sems = rest_refs
+def route_kernel(
+    slots, split, direct, ids_hbm, weight_hbm, tokens_hbm, pick_ref, share_ref, tokens_ref, *rest
+):
+    ids_ref, weight_ref, sems = rest
     top, tokens = ids_ref.shape
-    columns = tiles(tokens_ref.shape[1], 512)
+    full = share_ref.shape[0]
+    rows = full // split
     copies = [
         pltpu.make_async_copy(ids_hbm, ids_ref, sems.at[0]),
         pltpu.make_async_copy(weight_hbm, weight_ref, sems.at[1]),
-    ] + [
-        pltpu.make_async_copy(
-            tokens_hbm.at[:, at : at + size], tokens_ref.at[:, at : at + size], sems.at[2 + i]
-        )
-        for i, (at, size) in enumerate(columns)
+        pltpu.make_async_copy(tokens_hbm, tokens_ref, sems.at[2]),
     ]
     for copy in copies:
         copy.start()
     copies[0].wait()
     copies[1].wait()
-    full = share_ref.shape[0]
-    rows = full // split
 
     def named(count, per):
         expert = lax.broadcasted_iota(jnp.int32, (count, tokens), 0) // per
@@ -89,14 +86,18 @@
         return jnp.where(before == slot, hit, 0.0), scale
 
     chosen, scale = named(rows, slots)
-    pick = chosen.astype(BF16)
-    for i, (at, size) in enumerate(columns):
-        copies[2 + i].wait()
-        value = jnp.dot(pick, tokens_ref[:, at : at + size], preferred_element_type=F32)
-        spread(block_refs, value, at, size)
+    pick_ref[...] = chosen.astype(BF16)
     if split > 1:
         chosen, scale = named(full, slots * split)
     share_ref[...] = chosen * scale
+    copies[2].wait()
+
+
+def send_kernel(pick_ref, tokens_ref, *block_refs):
+    pick = pick_ref[...]
+    for at, size in tiles(tokens_ref.shape[1], 512):
+        value = jnp.dot(pick, tokens_ref[:, at : at + size], preferred_element_type=F32)
+        spread(block_refs, value, at, size)
 
 
 def split_weights(share_ref, mix_ref):
@@ -177,21 +178,33 @@
 
     parts = devices if direct else 1
     sent = experts * slots // parts
-    share, *send = pl.pallas_call(
+    pick, share, held = pl.pallas_call(
         functools.partial(route_kernel, slots, split, direct),
         in_specs=[pl.BlockSpec(memory_space=pltpu.HBM)] * 3,
-        out_specs=[VMEM] * (1 + parts),
-        out_shape=[shape((rows, count), F32)] + [shape((sent, width), BF16)] * parts,
+        out_specs=[VMEM] * 3,
+        out_shape=[
+            shape((experts * slots, count), BF16),
+            shape((rows, count), F32),
+            shape((count, width), BF16),
+        ],
         scratch_shapes=[
             pltpu.VMEM((top, count), jnp.int32),
             pltpu.VMEM((top, count), F32),
-            pltpu.VMEM((count, width), BF16),
-            pltpu.SemaphoreType.DMA((2 + pl.cdiv(width, 512),)),
+            pltpu.SemaphoreType.DMA((3,)),
         ],
         compiler_params=params(tokens, shape((count, 8 * rows), F32)),
-        cost_estimate=pl.CostEstimate(flops=int(3e10), bytes_accessed=0, transcendentals=0),
+        cost_estimate=pl.CostEstimate(flops=int(1e6), bytes_accessed=0, transcendentals=0),
         name="route",
     )(far(expert_ids.T), far(route_weight.T), far(tokens))
+    send = pl.pallas_call(
+        send_kernel,
+        in_specs=[VMEM] * 2,
+        out_specs=[VMEM] * parts,
+        out_shape=[shape((sent, width), BF16)] * parts,
+        compiler_params=params(tokens, tokens),
+        cost_estimate=pl.CostEstimate(flops=int(3e10), bytes_accessed=0, transcendentals=0),
+        name="send",
+    )(pick, held)
     if direct:
         arrived = swap(send, devices)
     else:

time: 42.5 us -> 41.8 us (0.984)
  Pallas kernels: 9.49 us -> 8.76 us
    pallas_call x1, Pallas kernels: 2.24 us -> 1.24 us  [local(): pl.pallas_call(functools.partial(route_kernel, slots, split, direct), in_...]
where the time goes in v4:
time: 41.8 us; the launch traced here: 41.7 us
  starting transfers between devices  23.8 us (57%)
  waiting for transfers between devices  8.99 us (22%)
  Pallas kernels  8.76 us (21%)
    ppermute x14, starting transfers between devices, swap(): lax.ppermute(block, 'expert', [(i, i ^ j) for i in range(devices)])  23.8 us
    ppermute x14, waiting for transfers between devices, swap(): lax.ppermute(block, 'expert', [(i, i ^ j) for i in range(devices)])  7.09 us
    pallas_call x1, Pallas kernels, local(): pl.pallas_call(functools.partial(up_kernel, parts), in_specs=[VMEM] * (pa...  4 us
    pallas_call x1, Pallas kernels, local(): pl.pallas_call(down_kernel, in_specs=[VMEM] * 3, out_specs=[VMEM] * parts...  2.09 us
    ppermute x1, waiting for transfers between devices, local(): lax.ppermute(give, 'tensor', [(i, (i + 1) % cores) for i in range(cores)])  1.9 us
    pallas_call x1, Pallas kernels, local(): pl.pallas_call(functools.partial(route_kernel, slots, split, direct), in_...  1.24 us
    pallas_call x1, Pallas kernels, local(): pl.pallas_call(functools.partial(mix_kernel, parts), in_specs=[VMEM] * (1...  1.17 us
  transfers between devices with their start and end apart: 15, of which 9 were waited for; matrix products, arithmetic and copies ran while one was open for 0% of the time, Pallas kernels for 0%

profile of v4, /device:TPU:0, one launch (start us, length us, event | category | flops | bytes accessed | tf_op | source)
XLA Modules:
  0.0 41.7 jit_solution(15564671845485433093)
XLA Ops:
  0.0 1.2 %route.1 = (bf16[64,128]{1,0:T(8,128)(2,1)S(1)}, f32[64,128]{1,0:T(8,128)S(1)}, bf16[128,3584]{1,0:T(8,128)(2,1)S(1)}) custom-call(s32[8,128]{1,0:T(8,128)} %bitcast.8, f32[8,128]{1,0:T(8,128)} %bitcast.9, bf16[128,3584]{1,0:T(8,128)(2,1)} %tokens_hbm.1), custom_call_target="tpu_custom_call" | custom-call | flops 1000000 | tf_op jit(solution)/shard_map/route/pallas_call | solution.py:181
  1.3 0.3 send.1
  1.5 6.0 %collective-permute-start = (bf16[8,3584]{1,0:T(8,128)(2,1)S(1)}, bf16[8,3584]{1,0:T(8,128)(2,1)S(1)}, u32[]{:S(2)}, u32[]{:S(2)}) collective-permute-start(bf16[8,3584]{1,0:T(8,128)(2,1)S(1)} %get-tuple-element.30), channel_id=1, source_target_pairs={{0,14},{2,12},{4,10},{6,8},{8,6},{10,4},{12,2},{14,0},{1,15},{3,13... | collective-permute-start | bytes 172040 | tf_op jit(solution)/shard_map/ppermute | solution.py:161
  7.8 0.8 %collective-permute-start.2 = (bf16[8,3584]{1,0:T(8,128)(2,1)S(1)}, bf16[8,3584]{1,0:T(8,128)(2,1)S(1)}, u32[]{:S(2)}, u32[]{:S(2)}) collective-permute-start(bf16[8,3584]{1,0:T(8,128)(2,1)S(1)} %get-tuple-element.32), channel_id=1, source_target_pairs={{0,10},{2,8},{4,14},{6,12},{8,2},{10,0},{12,6},{14,4},{1,11},{3,9}... | collective-permute-start | bytes 172040 | tf_op jit(solution)/shard_map/ppermute | solution.py:161
  8.6 4.3 %collective-permute-start.3 = (bf16[8,3584]{1,0:T(8,128)(2,1)S(1)}, bf16[8,3584]{1,0:T(8,128)(2,1)S(1)}, u32[]{:S(2)}, u32[]{:S(2)}) collective-permute-start(bf16[8,3584]{1,0:T(8,128)(2,1)S(1)} %get-tuple-element.33), channel_id=1, source_target_pairs={{0,6},{2,4},{4,2},{6,0},{8,14},{10,12},{12,10},{14,8},{1,7},{3,5},... | collective-permute-start | bytes 172040 | tf_op jit(solution)/shard_map/ppermute | solution.py:161
  12.9 0.8 %collective-permute-start.5 = (bf16[8,3584]{1,0:T(8,128)(2,1)S(1)}, bf16[8,3584]{1,0:T(8,128)(2,1)S(1)}, u32[]{:S(2)}, u32[]{:S(2)}) collective-permute-start(bf16[8,3584]{1,0:T(8,128)(2,1)S(1)} %get-tuple-element.35), channel_id=1, source_target_pairs={{0,4},{2,6},{4,0},{6,2},{8,12},{10,14},{12,8},{14,10},{1,5},{3,7},... | collective-permute-start | bytes 172040 | tf_op jit(solution)/shard_map/ppermute | solution.py:161
  13.7 0.5 %collective-permute-done.1.refs_2_ = bf16[8,3584]{1,0:T(8,128)(2,1)S(1)} collective-permute-done((bf16[8,3584]{1,0:T(8,128)(2,1)S(1)}, bf16[8,3584]{1,0:T(8,128)(2,1)S(1)}, u32[]{:S(2)}, u32[]{:S(2)}) %collective-permute-start.1) | collective-permute-done | bytes 57376 | tf_op jit(solution)/shard_map/ppermute | solution.py:161
  14.2 0.4 %collective-permute-start.6 = (bf16[8,3584]{1,0:T(8,128)(2,1)S(1)}, bf16[8,3584]{1,0:T(8,128)(2,1)S(1)}, u32[]{:S(2)}, u32[]{:S(2)}) collective-permute-start(bf16[8,3584]{1,0:T(8,128)(2,1)S(1)} %get-tuple-element.36), channel_id=1, source_target_pairs={{0,2},{2,0},{4,6},{6,4},{8,10},{10,8},{12,14},{14,12},{1,3},{3,1},... | collective-permute-start | bytes 172040 | tf_op jit(solution)/shard_map/ppermute | solution.py:161
  14.6 1.5 %collective-permute-done.2.refs_3_ = bf16[8,3584]{1,0:T(8,128)(2,1)S(1)} collective-permute-done((bf16[8,3584]{1,0:T(8,128)(2,1)S(1)}, bf16[8,3584]{1,0:T(8,128)(2,1)S(1)}, u32[]{:S(2)}, u32[]{:S(2)}) %collective-permute-start.2) | collective-permute-done | bytes 57376 | tf_op jit(solution)/shard_map/ppermute | solution.py:161
  16.1 0.8 %collective-permute-done.3.refs_4_ = bf16[8,3584]{1,0:T(8,128)(2,1)S(1)} collective-permute-done((bf16[8,3584]{1,0:T(8,128)(2,1)S(1)}, bf16[8,3584]{1,0:T(8,128)(2,1)S(1)}, u32[]{:S(2)}, u32[]{:S(2)}) %collective-permute-start.3) | collective-permute-done | bytes 57376 | tf_op jit(solution)/shard_map/ppermute | solution.py:161
  16.9 1.0 %collective-permute-done.4.refs_5_ = bf16[8,3584]{1,0:T(8,128)(2,1)S(1)} collective-permute-done((bf16[8,3584]{1,0:T(8,128)(2,1)S(1)}, bf16[8,3584]{1,0:T(8,128)(2,1)S(1)}, u32[]{:S(2)}, u32[]{:S(2)}) %collective-permute-start.4) | collective-permute-done | bytes 57376 | tf_op jit(solution)/shard_map/ppermute | solution.py:161
  18.0 0.4 %collective-permute-done.6.refs_7_ = bf16[8,3584]{1,0:T(8,128)(2,1)S(1)} collective-permute-done((bf16[8,3584]{1,0:T(8,128)(2,1)S(1)}, bf16[8,3584]{1,0:T(8,128)(2,1)S(1)}, u32[]{:S(2)}, u32[]{:S(2)}) %collective-permute-start.6) | collective-permute-done | bytes 57376 | tf_op jit(solution)/shard_map/ppermute | solution.py:161
  18.4 4.0 %up.1 = (f32[64,4096]{1,0:T(8,128)S(1)}, bf16[64,4096]{1,0:T(8,128)(2,1)S(1)}, bf16[128,192]{1,0:T(8,128)(2,1)S(1)}) custom-call(bf16[8,3584]{1,0:T(8,128)(2,1)S(1)} %get-tuple-element.29.refs_0_, bf16[8,3584]{1,0:T(8,128)(2,1)S(1)} %collective-permute-done.refs_1_, bf16[8,3584]{1,0:T(8,128)(2,1)S(1)} %collective-permute-done.1.refs_2_, ...), custom_call_target="tpu_custom_call" | custom-call | tf_op jit(solution)/shard_map/up/pallas_call | solution.py:216
  22.5 1.9 %collective-permute-done.7.other_ref = bf16[64,4096]{1,0:T(8,128)(2,1)S(1)} collective-permute-done((bf16[64,4096]{1,0:T(8,128)(2,1)S(1)}, bf16[64,4096]{1,0:T(8,128)(2,1)S(1)}, u32[]{:S(2)}, u32[]{:S(2)}) %collective-permute-start.7) | collective-permute-done | bytes 524320 | tf_op jit(solution)/shard_map/ppermute | solution.py:229
  24.4 2.1 %down.1 = (bf16[8,3584]{1,0:T(8,128)(2,1)S(1)}, bf16[8,3584]{1,0:T(8,128)(2,1)S(1)}, bf16[8,3584]{1,0:T(8,128)(2,1)S(1)}, bf16[8,3584]{1,0:T(8,128)(2,1)S(1)}, b...) custom-call(f32[64,4096]{1,0:T(8,128)S(1)} %get-tuple-element.39.own, ...), custom_call_target="tpu_custom_call" | custom-call | tf_op jit(solution)/shard_map/down/pallas_call | solution.py:230
  26.5 3.1 %collective-permute-start.8 = (bf16[8,3584]{1,0:T(8,128)(2,1)S(1)}, bf16[8,3584]{1,0:T(8,128)(2,1)S(1)}, u32[]{:S(2)}, u32[]{:S(2)}) collective-permute-start(bf16[8,3584]{1,0:T(8,128)(2,1)S(1)} %get-tuple-element.42), channel_id=1, source_target_pairs={{0,14},{2,12},{4,10},{6,8},{8,6},{10,4},{12,2},{14,0},{1,15},{3,13... | collective-permute-start | bytes 172040 | tf_op jit(solution)/shard_map/ppermute | solution.py:161
  29.6 0.7 %collective-permute-start.9 = (bf16[8,3584]{1,0:T(8,128)(2,1)S(1)}, bf16[8,3584]{1,0:T(8,128)(2,1)S(1)}, u32[]{:S(2)}, u32[]{:S(2)}) collective-permute-start(bf16[8,3584]{1,0:T(8,128)(2,1)S(1)} %get-tuple-element.43), channel_id=1, source_target_pairs={{0,12},{2,14},{4,8},{6,10},{8,4},{10,6},{12,0},{14,2},{1,13},{3,15... | collective-permute-start | bytes 172040 | tf_op jit(solution)/shard_map/ppermute | solution.py:161
  30.2 0.9 %collective-permute-start.10 = (bf16[8,3584]{1,0:T(8,128)(2,1)S(1)}, bf16[8,3584]{1,0:T(8,128)(2,1)S(1)}, u32[]{:S(2)}, u32[]{:S(2)}) collective-permute-start(bf16[8,3584]{1,0:T(8,128)(2,1)S(1)} %get-tuple-element.44), channel_id=1, source_target_pairs={{0,10},{2,8},{4,14},{6,12},{8,2},{10,0},{12,6},{14,4},{1,11},{3,9}... | collective-permute-start | bytes 172040 | tf_op jit(solution)/shard_map/ppermute | solution.py:161
  31.1 3.7 %collective-permute-start.11 = (bf16[8,3584]{1,0:T(8,128)(2,1)S(1)}, bf16[8,3584]{1,0:T(8,128)(2,1)S(1)}, u32[]{:S(2)}, u32[]{:S(2)}) collective-permute-start(bf16[8,3584]{1,0:T(8,128)(2,1)S(1)} %get-tuple-element.45), channel_id=1, source_target_pairs={{0,6},{2,4},{4,2},{6,0},{8,14},{10,12},{12,10},{14,8},{1,7},{3,5},... | collective-permute-start | bytes 172040 | tf_op jit(solution)/shard_map/ppermute | solution.py:161
  34.9 1.2 %collective-permute-start.13 = (bf16[8,3584]{1,0:T(8,128)(2,1)S(1)}, bf16[8,3584]{1,0:T(8,128)(2,1)S(1)}, u32[]{:S(2)}, u32[]{:S(2)}) collective-permute-start(bf16[8,3584]{1,0:T(8,128)(2,1)S(1)} %get-tuple-element.47), channel_id=1, source_target_pairs={{0,4},{2,6},{4,0},{6,2},{8,12},{10,14},{12,8},{14,10},{1,5},{3,7},... | collective-permute-start | bytes 172040 | tf_op jit(solution)/shard_map/ppermute | solution.py:161
  36.1 1.6 %collective-permute-start.14 = (bf16[8,3584]{1,0:T(8,128)(2,1)S(1)}, bf16[8,3584]{1,0:T(8,128)(2,1)S(1)}, u32[]{:S(2)}, u32[]{:S(2)}) collective-permute-start(bf16[8,3584]{1,0:T(8,128)(2,1)S(1)} %get-tuple-element.48), channel_id=1, source_target_pairs={{0,2},{2,0},{4,6},{6,4},{8,10},{10,8},{12,14},{14,12},{1,3},{3,1},... | collective-permute-start | bytes 172040 | tf_op jit(solution)/shard_map/ppermute | solution.py:161
  37.7 0.6 %collective-permute-done.10.refs_3_ = bf16[8,3584]{1,0:T(8,128)(2,1)S(1)} collective-permute-done((bf16[8,3584]{1,0:T(8,128)(2,1)S(1)}, bf16[8,3584]{1,0:T(8,128)(2,1)S(1)}, u32[]{:S(2)}, u32[]{:S(2)}) %collective-permute-start.10) | collective-permute-done | bytes 57376 | tf_op jit(solution)/shard_map/ppermute | solution.py:161
  38.3 2.1 %collective-permute-done.12.refs_5_ = bf16[8,3584]{1,0:T(8,128)(2,1)S(1)} collective-permute-done((bf16[8,3584]{1,0:T(8,128)(2,1)S(1)}, bf16[8,3584]{1,0:T(8,128)(2,1)S(1)}, u32[]{:S(2)}, u32[]{:S(2)}) %collective-permute-start.12) | collective-permute-done | bytes 57376 | tf_op jit(solution)/shard_map/ppermute | solution.py:161
  40.5 1.2 %mix.1 = bf16[128,3584]{1,0:T(8,128)(2,1)} custom-call(bf16[128,192]{1,0:T(8,128)(2,1)S(1)} %get-tuple-element.38.mix_ref, bf16[8,3584]{1,0:T(8,128)(2,1)S(1)} %get-tuple-element.41.refs_0_, bf16[8,3584]{1,0:T(8,128)(2,1)S(1)} %collective-permute-done.8.refs_1_, bf16[8,3584]{1,0:T(8,128)(2,1)S(1)} %collective-permute-done.9.refs_2_, ...), custom_call_target="tpu_custom_call" | custom-call | tf_op jit(solution)/shard_map/mix/pallas_call | solution.py:246
  (17 shorter events, 0.5 us)
Async XLA Ops:
  1.2 17.1 %copy-start = (bf16[1,3584,2048]{2,1,0:T(8,128)(2,1)S(1)}, bf16[1,3584,2048]{2,1,0:T(8,128)(2,1)}, u32[]{:S(2)}) copy-start(bf16[1,3584,2048]{2,1,0:T(8,128)(2,1)} %param.9) | copy-start | bytes 44040196
  1.3 17.1 %copy-start.1 = (bf16[1,3584,2048]{2,1,0:T(8,128)(2,1)S(1)}, bf16[1,3584,2048]{2,1,0:T(8,128)(2,1)}, u32[]{:S(2)}) copy-start(bf16[1,3584,2048]{2,1,0:T(8,128)(2,1)} %param.10) | copy-start | bytes 44040196
  1.5 11.3 %collective-permute-start = (bf16[8,3584]{1,0:T(8,128)(2,1)S(1)}, bf16[8,3584]{1,0:T(8,128)(2,1)S(1)}, u32[]{:S(2)}, u32[]{:S(2)}) collective-permute-start(bf16[8,3584]{1,0:T(8,128)(2,1)S(1)} %get-tuple-element.30), channel_id=1, source_target_pairs={{0,14},{2,12},{4,10},{6,8},{8,6},{10,4},{12,2},{14,0},{1,15},{3,13... | collective-permute-start | bytes 172040 | tf_op jit(solution)/shard_map/ppermute | solution.py:161
  7.6 6.6 %collective-permute-start.1 = (bf16[8,3584]{1,0:T(8,128)(2,1)S(1)}, bf16[8,3584]{1,0:T(8,128)(2,1)S(1)}, u32[]{:S(2)}, u32[]{:S(2)}) collective-permute-start(bf16[8,3584]{1,0:T(8,128)(2,1)S(1)} %get-tuple-element.31), channel_id=1, source_target_pairs={{0,12},{2,14},{4,8},{6,10},{8,4},{10,6},{12,0},{14,2},{1,13},{3,15... | collective-permute-start | bytes 172040 | tf_op jit(solution)/shard_map/ppermute | solution.py:161
  7.8 8.3 %collective-permute-start.2 = (bf16[8,3584]{1,0:T(8,128)(2,1)S(1)}, bf16[8,3584]{1,0:T(8,128)(2,1)S(1)}, u32[]{:S(2)}, u32[]{:S(2)}) collective-permute-start(bf16[8,3584]{1,0:T(8,128)(2,1)S(1)} %get-tuple-element.32), channel_id=1, source_target_pairs={{0,10},{2,8},{4,14},{6,12},{8,2},{10,0},{12,6},{14,4},{1,11},{3,9}... | collective-permute-start | bytes 172040 | tf_op jit(solution)/shard_map/ppermute | solution.py:161
  8.6 8.3 %collective-permute-start.3 = (bf16[8,3584]{1,0:T(8,128)(2,1)S(1)}, bf16[8,3584]{1,0:T(8,128)(2,1)S(1)}, u32[]{:S(2)}, u32[]{:S(2)}) collective-permute-start(bf16[8,3584]{1,0:T(8,128)(2,1)S(1)} %get-tuple-element.33), channel_id=1, source_target_pairs={{0,6},{2,4},{4,2},{6,0},{8,14},{10,12},{12,10},{14,8},{1,7},{3,5},... | collective-permute-start | bytes 172040 | tf_op jit(solution)/shard_map/ppermute | solution.py:161
  12.9 5.1 %collective-permute-start.4 = (bf16[8,3584]{1,0:T(8,128)(2,1)S(1)}, bf16[8,3584]{1,0:T(8,128)(2,1)S(1)}, u32[]{:S(2)}, u32[]{:S(2)}) collective-permute-start(bf16[8,3584]{1,0:T(8,128)(2,1)S(1)} %get-tuple-element.34), channel_id=1, source_target_pairs={{0,8},{2,10},{4,12},{6,14},{8,0},{10,2},{12,4},{14,6},{1,9},{3,11}... | collective-permute-start | bytes 172040 | tf_op jit(solution)/shard_map/ppermute | solution.py:161
  12.9 5.1 %collective-permute-start.5 = (bf16[8,3584]{1,0:T(8,128)(2,1)S(1)}, bf16[8,3584]{1,0:T(8,128)(2,1)S(1)}, u32[]{:S(2)}, u32[]{:S(2)}) collective-permute-start(bf16[8,3584]{1,0:T(8,128)(2,1)S(1)} %get-tuple-element.35), channel_id=1, source_target_pairs={{0,4},{2,6},{4,0},{6,2},{8,12},{10,14},{12,8},{14,10},{1,5},{3,7},... | collective-permute-start | bytes 172040 | tf_op jit(solution)/shard_map/ppermute | solution.py:161
  14.2 4.2 %collective-permute-start.6 = (bf16[8,3584]{1,0:T(8,128)(2,1)S(1)}, bf16[8,3584]{1,0:T(8,128)(2,1)S(1)}, u32[]{:S(2)}, u32[]{:S(2)}) collective-permute-start(bf16[8,3584]{1,0:T(8,128)(2,1)S(1)} %get-tuple-element.36), channel_id=1, source_target_pairs={{0,2},{2,0},{4,6},{6,4},{8,10},{10,8},{12,14},{14,12},{1,3},{3,1},... | collective-permute-start | bytes 172040 | tf_op jit(solution)/shard_map/ppermute | solution.py:161
  18.4 6.0 %copy-start.2 = (bf16[1,2048,3584]{2,1,0:T(8,128)(2,1)S(1)}, bf16[1,2048,3584]{2,1,0:T(8,128)(2,1)}, u32[]{:S(2)}) copy-start(bf16[1,2048,3584]{2,1,0:T(8,128)(2,1)} %param.11) | copy-start | bytes 44040196
  22.4 2.0 %collective-permute-start.7 = (bf16[64,4096]{1,0:T(8,128)(2,1)S(1)}, bf16[64,4096]{1,0:T(8,128)(2,1)S(1)}, u32[]{:S(2)}, u32[]{:S(2)}) collective-permute-start(bf16[64,4096]{1,0:T(8,128)(2,1)S(1)} %get-tuple-element.40), channel_id=1, source_target_pairs={{0,1},{1,0},{2,3},{3,2},{4,5},{5,4},{6,7},{7,6},{8,9},{9,8},{10,11... | collective-permute-start | bytes 1572872 | tf_op jit(solution)/shard_map/ppermute | solution.py:229
  26.5 8.4 %collective-permute-start.8 = (bf16[8,3584]{1,0:T(8,128)(2,1)S(1)}, bf16[8,3584]{1,0:T(8,128)(2,1)S(1)}, u32[]{:S(2)}, u32[]{:S(2)}) collective-permute-start(bf16[8,3584]{1,0:T(8,128)(2,1)S(1)} %get-tuple-element.42), channel_id=1, source_target_pairs={{0,14},{2,12},{4,10},{6,8},{8,6},{10,4},{12,2},{14,0},{1,15},{3,13... | collective-permute-start | bytes 172040 | tf_op jit(solution)/shard_map/ppermute | solution.py:161
  29.6 6.5 %collective-permute-start.9 = (bf16[8,3584]{1,0:T(8,128)(2,1)S(1)}, bf16[8,3584]{1,0:T(8,128)(2,1)S(1)}, u32[]{:S(2)}, u32[]{:S(2)}) collective-permute-start(bf16[8,3584]{1,0:T(8,128)(2,1)S(1)} %get-tuple-element.43), channel_id=1, source_target_pairs={{0,12},{2,14},{4,8},{6,10},{8,4},{10,6},{12,0},{14,2},{1,13},{3,15... | collective-permute-start | bytes 172040 | tf_op jit(solution)/shard_map/ppermute | solution.py:161
  30.2 8.0 %collective-permute-start.10 = (bf16[8,3584]{1,0:T(8,128)(2,1)S(1)}, bf16[8,3584]{1,0:T(8,128)(2,1)S(1)}, u32[]{:S(2)}, u32[]{:S(2)}) collective-permute-start(bf16[8,3584]{1,0:T(8,128)(2,1)S(1)} %get-tuple-element.44), channel_id=1, source_target_pairs={{0,10},{2,8},{4,14},{6,12},{8,2},{10,0},{12,6},{14,4},{1,11},{3,9}... | collective-permute-start | bytes 172040 | tf_op jit(solution)/shard_map/ppermute | solution.py:161
  31.1 7.1 %collective-permute-start.11 = (bf16[8,3584]{1,0:T(8,128)(2,1)S(1)}, bf16[8,3584]{1,0:T(8,128)(2,1)S(1)}, u32[]{:S(2)}, u32[]{:S(2)}) collective-permute-start(bf16[8,3584]{1,0:T(8,128)(2,1)S(1)} %get-tuple-element.45), channel_id=1, source_target_pairs={{0,6},{2,4},{4,2},{6,0},{8,14},{10,12},{12,10},{14,8},{1,7},{3,5},... | collective-permute-start | bytes 172040 | tf_op jit(solution)/shard_map/ppermute | solution.py:161
  34.9 5.5 %collective-permute-start.12 = (bf16[8,3584]{1,0:T(8,128)(2,1)S(1)}, bf16[8,3584]{1,0:T(8,128)(2,1)S(1)}, u32[]{:S(2)}, u32[]{:S(2)}) collective-permute-start(bf16[8,3584]{1,0:T(8,128)(2,1)S(1)} %get-tuple-element.46), channel_id=1, source_target_pairs={{0,8},{2,10},{4,12},{6,14},{8,0},{10,2},{12,4},{14,6},{1,9},{3,11}... | collective-permute-start | bytes 172040 | tf_op jit(solution)/shard_map/ppermute | solution.py:161
  34.9 5.6 %collective-permute-start.13 = (bf16[8,3584]{1,0:T(8,128)(2,1)S(1)}, bf16[8,3584]{1,0:T(8,128)(2,1)S(1)}, u32[]{:S(2)}, u32[]{:S(2)}) collective-permute-start(bf16[8,3584]{1,0:T(8,128)(2,1)S(1)} %get-tuple-element.47), channel_id=1, source_target_pairs={{0,4},{2,6},{4,0},{6,2},{8,12},{10,14},{12,8},{14,10},{1,5},{3,7},... | collective-permute-start | bytes 172040 | tf_op jit(solution)/shard_map/ppermute | solution.py:161
  36.1 4.4 %collective-permute-start.14 = (bf16[8,3584]{1,0:T(8,128)(2,1)S(1)}, bf16[8,3584]{1,0:T(8,128)(2,1)S(1)}, u32[]{:S(2)}, u32[]{:S(2)}) collective-permute-start(bf16[8,3584]{1,0:T(8,128)(2,1)S(1)} %get-tuple-element.48), channel_id=1, source_target_pairs={{0,2},{2,0},{4,6},{6,4},{8,10},{10,8},{12,14},{14,12},{1,3},{3,1},... | collective-permute-start | bytes 172040 | tf_op jit(solution)/shard_map/ppermute | solution.py:161

commit v5 on v4

--- a/solution.py
+++ b/solution.py
@@ -10,6 +10,7 @@
 HIDDEN_SIZE = 2048
 ROUTED = 256
 ORDER = (0, 7, 6, 5, 3, 4, 2, 1)
+RETURN = (0, 5, 6, 3, 7, 4, 2, 1)
 BF16 = jnp.bfloat16
 F32 = jnp.float32
 VMEM = pl.BlockSpec(memory_space=pltpu.VMEM)
@@ -134,7 +135,7 @@
     act = padded((gate / (1.0 + jnp.exp(-gate)) * up).astype(BF16))
     for at, size in tiles(down_ref.shape[1], 512):
         value = jnp.dot(act, down_ref[:, at : at + size], preferred_element_type=F32)[:rows]
-        spread(block_refs, value, at, size)
+        spread(sorted_as(block_refs, RETURN, ORDER), value, at, size)
 
 
 def mix_kernel(count, mix_ref, *refs):
@@ -142,7 +143,7 @@
     mix = mix_ref[...]
     copies = []
     for i, (at, size) in enumerate(tiles(out_ref.shape[1], 512)):
-        part = join([b[:, at : at + size] for b in block_refs])
+        part = join(sorted_as([b[:, at : at + size] for b in block_refs], RETURN, ORDER))
         value = jnp.dot(
             mix, jnp.concatenate([part] * 3, axis=0), preferred_element_type=F32
         )
@@ -156,11 +157,15 @@
         copy.wait()
 
 
-def swap(blocks, devices):
+def swap(blocks, order):
     return [
-        lax.ppermute(block, "expert", [(i, i ^ j) for i in range(devices)]) if j else block
-        for block, j in zip(blocks, ORDER)
+        lax.ppermute(block, "expert", [(i, i ^ j) for i in range(len(order))]) if j else block
+        for block, j in zip(blocks, order)
     ]
+
+
+def sorted_as(blocks, order, other):
+    return [blocks[order.index(j)] for j in other] if len(blocks) > 1 else list(blocks)
 
 
 def local(tokens, expert_ids, route_weight, gate_weight, up_weight, down_weight):
@@ -206,7 +211,7 @@
         name="send",
     )(pick, held)
     if direct:
-        arrived = swap(send, devices)
+        arrived = swap(send, ORDER)
     else:
         spread_out = jnp.repeat(send[0].reshape(experts, slots, width), split, axis=0)
         arrived = [
@@ -236,7 +241,7 @@
         name="down",
     )(own, other, near(down_weight[0]))
     if direct:
-        back = swap(answer, devices)
+        back = swap(answer, RETURN)
     else:
         back = [
             lax.all_to_all(

time: 41.8 us -> 41.2 us (0.986)
  starting transfers between devices: 23.8 us -> 22.8 us
  waiting for transfers between devices: 8.99 us -> 9.42 us
    ppermute x14, starting transfers between devices: 23.8 us -> 22.7 us  [swap(): lax.ppermute(block, 'expert', [(i, i ^ j) for i in range(len(order))])]
    ppermute x14, waiting for transfers between devices: 7.09 us -> 7.53 us  [swap(): lax.ppermute(block, 'expert', [(i, i ^ j) for i in range(len(order))])]
where the time goes in v5:
time: 41.2 us; the launch traced here: 41 us
  starting transfers between devices  22.8 us (55%)
  waiting for transfers between devices  9.42 us (23%)
  Pallas kernels  8.76 us (21%)
    ppermute x14, starting transfers between devices, swap(): lax.ppermute(block, 'expert', [(i, i ^ j) for i in range(len(order))])  22.7 us
    ppermute x14, waiting for transfers between devices, swap(): lax.ppermute(block, 'expert', [(i, i ^ j) for i in range(len(order))])  7.53 us
    pallas_call x1, Pallas kernels, local(): pl.pallas_call(functools.partial(up_kernel, parts), in_specs=[VMEM] * (pa...  4 us
    pallas_call x1, Pallas kernels, local(): pl.pallas_call(down_kernel, in_specs=[VMEM] * 3, out_specs=[VMEM] * parts...  2.09 us
    ppermute x1, waiting for transfers between devices, local(): lax.ppermute(give, 'tensor', [(i, (i + 1) % cores) for i in range(cores)])  1.9 us
    pallas_call x1, Pallas kernels, local(): pl.pallas_call(functools.partial(route_kernel, slots, split, direct), in_...  1.24 us
    pallas_call x1, Pallas kernels, local(): pl.pallas_call(functools.partial(mix_kernel, parts), in_specs=[VMEM] * (1...  1.17 us
  transfers between devices with their start and end apart: 15, of which 9 were waited for; matrix products, arithmetic and copies ran while one was open for 0% of the time, Pallas kernels for 0%

profile of v5, /device:TPU:0, one launch (start us, length us, event | category | flops | bytes accessed | tf_op | source)
XLA Modules:
  0.0 41.0 jit_solution(7215655108713894313)
XLA Ops:
  0.0 1.2 %route.1 = (bf16[64,128]{1,0:T(8,128)(2,1)S(1)}, f32[64,128]{1,0:T(8,128)S(1)}, bf16[128,3584]{1,0:T(8,128)(2,1)S(1)}) custom-call(s32[8,128]{1,0:T(8,128)} %bitcast.8, f32[8,128]{1,0:T(8,128)} %bitcast.9, bf16[128,3584]{1,0:T(8,128)(2,1)} %tokens_hbm.1), custom_call_target="tpu_custom_call" | custom-call | flops 1000000 | tf_op jit(solution)/shard_map/route/pallas_call | solution.py:186
  1.5 6.0 %collective-permute-start = (bf16[8,3584]{1,0:T(8,128)(2,1)S(1)}, bf16[8,3584]{1,0:T(8,128)(2,1)S(1)}, u32[]{:S(2)}, u32[]{:S(2)}) collective-permute-start(bf16[8,3584]{1,0:T(8,128)(2,1)S(1)} %get-tuple-element.30), channel_id=1, source_target_pairs={{0,14},{2,12},{4,10},{6,8},{8,6},{10,4},{12,2},{14,0},{1,15},{3,13... | collective-permute-start | bytes 172040 | tf_op jit(solution)/shard_map/ppermute | solution.py:162
  7.8 0.8 %collective-permute-start.2 = (bf16[8,3584]{1,0:T(8,128)(2,1)S(1)}, bf16[8,3584]{1,0:T(8,128)(2,1)S(1)}, u32[]{:S(2)}, u32[]{:S(2)}) collective-permute-start(bf16[8,3584]{1,0:T(8,128)(2,1)S(1)} %get-tuple-element.32), channel_id=1, source_target_pairs={{0,10},{2,8},{4,14},{6,12},{8,2},{10,0},{12,6},{14,4},{1,11},{3,9}... | collective-permute-start | bytes 172040 | tf_op jit(solution)/shard_map/ppermute | solution.py:162
  8.6 4.3 %collective-permute-start.3 = (bf16[8,3584]{1,0:T(8,128)(2,1)S(1)}, bf16[8,3584]{1,0:T(8,128)(2,1)S(1)}, u32[]{:S(2)}, u32[]{:S(2)}) collective-permute-start(bf16[8,3584]{1,0:T(8,128)(2,1)S(1)} %get-tuple-element.33), channel_id=1, source_target_pairs={{0,6},{2,4},{4,2},{6,0},{8,14},{10,12},{12,10},{14,8},{1,7},{3,5},... | collective-permute-start | bytes 172040 | tf_op jit(solution)/shard_map/ppermute | solution.py:162
  12.9 0.8 %collective-permute-start.5 = (bf16[8,3584]{1,0:T(8,128)(2,1)S(1)}, bf16[8,3584]{1,0:T(8,128)(2,1)S(1)}, u32[]{:S(2)}, u32[]{:S(2)}) collective-permute-start(bf16[8,3584]{1,0:T(8,128)(2,1)S(1)} %get-tuple-element.35), channel_id=1, source_target_pairs={{0,4},{2,6},{4,0},{6,2},{8,12},{10,14},{12,8},{14,10},{1,5},{3,7},... | collective-permute-start | bytes 172040 | tf_op jit(solution)/shard_map/ppermute | solution.py:162
  13.7 0.5 %collective-permute-done.1.refs_2_ = bf16[8,3584]{1,0:T(8,128)(2,1)S(1)} collective-permute-done((bf16[8,3584]{1,0:T(8,128)(2,1)S(1)}, bf16[8,3584]{1,0:T(8,128)(2,1)S(1)}, u32[]{:S(2)}, u32[]{:S(2)}) %collective-permute-start.1) | collective-permute-done | bytes 57376 | tf_op jit(solution)/shard_map/ppermute | solution.py:162
  14.2 0.4 %collective-permute-start.6 = (bf16[8,3584]{1,0:T(8,128)(2,1)S(1)}, bf16[8,3584]{1,0:T(8,128)(2,1)S(1)}, u32[]{:S(2)}, u32[]{:S(2)}) collective-permute-start(bf16[8,3584]{1,0:T(8,128)(2,1)S(1)} %get-tuple-element.36), channel_id=1, source_target_pairs={{0,2},{2,0},{4,6},{6,4},{8,10},{10,8},{12,14},{14,12},{1,3},{3,1},... | collective-permute-start | bytes 172040 | tf_op jit(solution)/shard_map/ppermute | solution.py:162
  14.6 1.5 %collective-permute-done.2.refs_3_ = bf16[8,3584]{1,0:T(8,128)(2,1)S(1)} collective-permute-done((bf16[8,3584]{1,0:T(8,128)(2,1)S(1)}, bf16[8,3584]{1,0:T(8,128)(2,1)S(1)}, u32[]{:S(2)}, u32[]{:S(2)}) %collective-permute-start.2) | collective-permute-done | bytes 57376 | tf_op jit(solution)/shard_map/ppermute | solution.py:162
  16.1 0.8 %collective-permute-done.3.refs_4_ = bf16[8,3584]{1,0:T(8,128)(2,1)S(1)} collective-permute-done((bf16[8,3584]{1,0:T(8,128)(2,1)S(1)}, bf16[8,3584]{1,0:T(8,128)(2,1)S(1)}, u32[]{:S(2)}, u32[]{:S(2)}) %collective-permute-start.3) | collective-permute-done | bytes 57376 | tf_op jit(solution)/shard_map/ppermute | solution.py:162
  16.9 1.0 %collective-permute-done.4.refs_5_ = bf16[8,3584]{1,0:T(8,128)(2,1)S(1)} collective-permute-done((bf16[8,3584]{1,0:T(8,128)(2,1)S(1)}, bf16[8,3584]{1,0:T(8,128)(2,1)S(1)}, u32[]{:S(2)}, u32[]{:S(2)}) %collective-permute-start.4) | collective-permute-done | bytes 57376 | tf_op jit(solution)/shard_map/ppermute | solution.py:162
  18.0 0.4 %collective-permute-done.6.refs_7_ = bf16[8,3584]{1,0:T(8,128)(2,1)S(1)} collective-permute-done((bf16[8,3584]{1,0:T(8,128)(2,1)S(1)}, bf16[8,3584]{1,0:T(8,128)(2,1)S(1)}, u32[]{:S(2)}, u32[]{:S(2)}) %collective-permute-start.6) | collective-permute-done | bytes 57376 | tf_op jit(solution)/shard_map/ppermute | solution.py:162
  18.4 4.0 %up.1 = (f32[64,4096]{1,0:T(8,128)S(1)}, bf16[64,4096]{1,0:T(8,128)(2,1)S(1)}, bf16[128,192]{1,0:T(8,128)(2,1)S(1)}) custom-call(bf16[8,3584]{1,0:T(8,128)(2,1)S(1)} %get-tuple-element.29.refs_0_, bf16[8,3584]{1,0:T(8,128)(2,1)S(1)} %collective-permute-done.refs_1_, bf16[8,3584]{1,0:T(8,128)(2,1)S(1)} %collective-permute-done.1.refs_2_, ...), custom_call_target="tpu_custom_call" | custom-call | tf_op jit(solution)/shard_map/up/pallas_call | solution.py:221
  22.5 1.9 %collective-permute-done.7.other_ref = bf16[64,4096]{1,0:T(8,128)(2,1)S(1)} collective-permute-done((bf16[64,4096]{1,0:T(8,128)(2,1)S(1)}, bf16[64,4096]{1,0:T(8,128)(2,1)S(1)}, u32[]{:S(2)}, u32[]{:S(2)}) %collective-permute-start.7) | collective-permute-done | bytes 524320 | tf_op jit(solution)/shard_map/ppermute | solution.py:234
  24.4 2.1 %down.1 = (bf16[8,3584]{1,0:T(8,128)(2,1)S(1)}, bf16[8,3584]{1,0:T(8,128)(2,1)S(1)}, bf16[8,3584]{1,0:T(8,128)(2,1)S(1)}, bf16[8,3584]{1,0:T(8,128)(2,1)S(1)}, b...) custom-call(f32[64,4096]{1,0:T(8,128)S(1)} %get-tuple-element.39.own, ...), custom_call_target="tpu_custom_call" | custom-call | tf_op jit(solution)/shard_map/down/pallas_call | solution.py:235
  26.5 1.7 %collective-permute-start.8 = (bf16[8,3584]{1,0:T(8,128)(2,1)S(1)}, bf16[8,3584]{1,0:T(8,128)(2,1)S(1)}, u32[]{:S(2)}, u32[]{:S(2)}) collective-permute-start(bf16[8,3584]{1,0:T(8,128)(2,1)S(1)} %get-tuple-element.42), channel_id=1, source_target_pairs={{0,10},{2,8},{4,14},{6,12},{8,2},{10,0},{12,6},{14,4},{1,11},{3,9}... | collective-permute-start | bytes 172040 | tf_op jit(solution)/shard_map/ppermute | solution.py:162
  28.2 1.5 %collective-permute-start.9 = (bf16[8,3584]{1,0:T(8,128)(2,1)S(1)}, bf16[8,3584]{1,0:T(8,128)(2,1)S(1)}, u32[]{:S(2)}, u32[]{:S(2)}) collective-permute-start(bf16[8,3584]{1,0:T(8,128)(2,1)S(1)} %get-tuple-element.43), channel_id=1, source_target_pairs={{0,12},{2,14},{4,8},{6,10},{8,4},{10,6},{12,0},{14,2},{1,13},{3,15... | collective-permute-start | bytes 172040 | tf_op jit(solution)/shard_map/ppermute | solution.py:162
  29.7 1.4 %collective-permute-start.10 = (bf16[8,3584]{1,0:T(8,128)(2,1)S(1)}, bf16[8,3584]{1,0:T(8,128)(2,1)S(1)}, u32[]{:S(2)}, u32[]{:S(2)}) collective-permute-start(bf16[8,3584]{1,0:T(8,128)(2,1)S(1)} %get-tuple-element.44), channel_id=1, source_target_pairs={{0,6},{2,4},{4,2},{6,0},{8,14},{10,12},{12,10},{14,8},{1,7},{3,5},... | collective-permute-start | bytes 172040 | tf_op jit(solution)/shard_map/ppermute | solution.py:162
  31.1 2.9 %collective-permute-start.11 = (bf16[8,3584]{1,0:T(8,128)(2,1)S(1)}, bf16[8,3584]{1,0:T(8,128)(2,1)S(1)}, u32[]{:S(2)}, u32[]{:S(2)}) collective-permute-start(bf16[8,3584]{1,0:T(8,128)(2,1)S(1)} %get-tuple-element.45), channel_id=1, source_target_pairs={{0,14},{2,12},{4,10},{6,8},{8,6},{10,4},{12,2},{14,0},{1,15},{3,13... | collective-permute-start | bytes 172040 | tf_op jit(solution)/shard_map/ppermute | solution.py:162
  34.1 0.3 collective-permute-done.8.refs_1_
  34.4 1.1 %collective-permute-start.13 = (bf16[8,3584]{1,0:T(8,128)(2,1)S(1)}, bf16[8,3584]{1,0:T(8,128)(2,1)S(1)}, u32[]{:S(2)}, u32[]{:S(2)}) collective-permute-start(bf16[8,3584]{1,0:T(8,128)(2,1)S(1)} %get-tuple-element.47), channel_id=1, source_target_pairs={{0,4},{2,6},{4,0},{6,2},{8,12},{10,14},{12,8},{14,10},{1,5},{3,7},... | collective-permute-start | bytes 172040 | tf_op jit(solution)/shard_map/ppermute | solution.py:162
  35.4 1.5 %collective-permute-start.14 = (bf16[8,3584]{1,0:T(8,128)(2,1)S(1)}, bf16[8,3584]{1,0:T(8,128)(2,1)S(1)}, u32[]{:S(2)}, u32[]{:S(2)}) collective-permute-start(bf16[8,3584]{1,0:T(8,128)(2,1)S(1)} %get-tuple-element.48), channel_id=1, source_target_pairs={{0,2},{2,0},{4,6},{6,4},{8,10},{10,8},{12,14},{14,12},{1,3},{3,1},... | collective-permute-start | bytes 172040 | tf_op jit(solution)/shard_map/ppermute | solution.py:162
  36.9 1.2 %collective-permute-done.11.refs_4_ = bf16[8,3584]{1,0:T(8,128)(2,1)S(1)} collective-permute-done((bf16[8,3584]{1,0:T(8,128)(2,1)S(1)}, bf16[8,3584]{1,0:T(8,128)(2,1)S(1)}, u32[]{:S(2)}, u32[]{:S(2)}) %collective-permute-start.11) | collective-permute-done | bytes 57376 | tf_op jit(solution)/shard_map/ppermute | solution.py:162
  38.1 1.7 %collective-permute-done.12.refs_5_ = bf16[8,3584]{1,0:T(8,128)(2,1)S(1)} collective-permute-done((bf16[8,3584]{1,0:T(8,128)(2,1)S(1)}, bf16[8,3584]{1,0:T(8,128)(2,1)S(1)}, u32[]{:S(2)}, u32[]{:S(2)}) %collective-permute-start.12) | collective-permute-done | bytes 57376 | tf_op jit(solution)/shard_map/ppermute | solution.py:162
  39.9 1.2 %mix.1 = bf16[128,3584]{1,0:T(8,128)(2,1)} custom-call(bf16[128,192]{1,0:T(8,128)(2,1)S(1)} %get-tuple-element.38.mix_ref, bf16[8,3584]{1,0:T(8,128)(2,1)S(1)} %get-tuple-element.41.refs_0_, bf16[8,3584]{1,0:T(8,128)(2,1)S(1)} %collective-permute-done.8.refs_1_, bf16[8,3584]{1,0:T(8,128)(2,1)S(1)} %collective-permute-done.9.refs_2_, ...), custom_call_target="tpu_custom_call" | custom-call | tf_op jit(solution)/shard_map/mix/pallas_call | solution.py:251
  (17 shorter events, 0.7 us)
Async XLA Ops:
  1.2 17.1 %copy-start = (bf16[1,3584,2048]{2,1,0:T(8,128)(2,1)S(1)}, bf16[1,3584,2048]{2,1,0:T(8,128)(2,1)}, u32[]{:S(2)}) copy-start(bf16[1,3584,2048]{2,1,0:T(8,128)(2,1)} %param.9) | copy-start | bytes 44040196
  1.3 17.1 %copy-start.1 = (bf16[1,3584,2048]{2,1,0:T(8,128)(2,1)S(1)}, bf16[1,3584,2048]{2,1,0:T(8,128)(2,1)}, u32[]{:S(2)}) copy-start(bf16[1,3584,2048]{2,1,0:T(8,128)(2,1)} %param.10) | copy-start | bytes 44040196
  1.5 11.3 %collective-permute-start = (bf16[8,3584]{1,0:T(8,128)(2,1)S(1)}, bf16[8,3584]{1,0:T(8,128)(2,1)S(1)}, u32[]{:S(2)}, u32[]{:S(2)}) collective-permute-start(bf16[8,3584]{1,0:T(8,128)(2,1)S(1)} %get-tuple-element.30), channel_id=1, source_target_pairs={{0,14},{2,12},{4,10},{6,8},{8,6},{10,4},{12,2},{14,0},{1,15},{3,13... | collective-permute-start | bytes 172040 | tf_op jit(solution)/shard_map/ppermute | solution.py:162
  7.6 6.6 %collective-permute-start.1 = (bf16[8,3584]{1,0:T(8,128)(2,1)S(1)}, bf16[8,3584]{1,0:T(8,128)(2,1)S(1)}, u32[]{:S(2)}, u32[]{:S(2)}) collective-permute-start(bf16[8,3584]{1,0:T(8,128)(2,1)S(1)} %get-tuple-element.31), channel_id=1, source_target_pairs={{0,12},{2,14},{4,8},{6,10},{8,4},{10,6},{12,0},{14,2},{1,13},{3,15... | collective-permute-start | bytes 172040 | tf_op jit(solution)/shard_map/ppermute | solution.py:162
  7.8 8.3 %collective-permute-start.2 = (bf16[8,3584]{1,0:T(8,128)(2,1)S(1)}, bf16[8,3584]{1,0:T(8,128)(2,1)S(1)}, u32[]{:S(2)}, u32[]{:S(2)}) collective-permute-start(bf16[8,3584]{1,0:T(8,128)(2,1)S(1)} %get-tuple-element.32), channel_id=1, source_target_pairs={{0,10},{2,8},{4,14},{6,12},{8,2},{10,0},{12,6},{14,4},{1,11},{3,9}... | collective-permute-start | bytes 172040 | tf_op jit(solution)/shard_map/ppermute | solution.py:162
  8.6 8.3 %collective-permute-start.3 = (bf16[8,3584]{1,0:T(8,128)(2,1)S(1)}, bf16[8,3584]{1,0:T(8,128)(2,1)S(1)}, u32[]{:S(2)}, u32[]{:S(2)}) collective-permute-start(bf16[8,3584]{1,0:T(8,128)(2,1)S(1)} %get-tuple-element.33), channel_id=1, source_target_pairs={{0,6},{2,4},{4,2},{6,0},{8,14},{10,12},{12,10},{14,8},{1,7},{3,5},... | collective-permute-start | bytes 172040 | tf_op jit(solution)/shard_map/ppermute | solution.py:162
  12.9 5.1 %collective-permute-start.4 = (bf16[8,3584]{1,0:T(8,128)(2,1)S(1)}, bf16[8,3584]{1,0:T(8,128)(2,1)S(1)}, u32[]{:S(2)}, u32[]{:S(2)}) collective-permute-start(bf16[8,3584]{1,0:T(8,128)(2,1)S(1)} %get-tuple-element.34), channel_id=1, source_target_pairs={{0,8},{2,10},{4,12},{6,14},{8,0},{10,2},{12,4},{14,6},{1,9},{3,11}... | collective-permute-start | bytes 172040 | tf_op jit(solution)/shard_map/ppermute | solution.py:162
  12.9 5.1 %collective-permute-start.5 = (bf16[8,3584]{1,0:T(8,128)(2,1)S(1)}, bf16[8,3584]{1,0:T(8,128)(2,1)S(1)}, u32[]{:S(2)}, u32[]{:S(2)}) collective-permute-start(bf16[8,3584]{1,0:T(8,128)(2,1)S(1)} %get-tuple-element.35), channel_id=1, source_target_pairs={{0,4},{2,6},{4,0},{6,2},{8,12},{10,14},{12,8},{14,10},{1,5},{3,7},... | collective-permute-start | bytes 172040 | tf_op jit(solution)/shard_map/ppermute | solution.py:162
  14.2 4.2 %collective-permute-start.6 = (bf16[8,3584]{1,0:T(8,128)(2,1)S(1)}, bf16[8,3584]{1,0:T(8,128)(2,1)S(1)}, u32[]{:S(2)}, u32[]{:S(2)}) collective-permute-start(bf16[8,3584]{1,0:T(8,128)(2,1)S(1)} %get-tuple-element.36), channel_id=1, source_target_pairs={{0,2},{2,0},{4,6},{6,4},{8,10},{10,8},{12,14},{14,12},{1,3},{3,1},... | collective-permute-start | bytes 172040 | tf_op jit(solution)/shard_map/ppermute | solution.py:162
  18.4 6.0 %copy-start.2 = (bf16[1,2048,3584]{2,1,0:T(8,128)(2,1)S(1)}, bf16[1,2048,3584]{2,1,0:T(8,128)(2,1)}, u32[]{:S(2)}) copy-start(bf16[1,2048,3584]{2,1,0:T(8,128)(2,1)} %param.11) | copy-start | bytes 44040196
  22.4 2.0 %collective-permute-start.7 = (bf16[64,4096]{1,0:T(8,128)(2,1)S(1)}, bf16[64,4096]{1,0:T(8,128)(2,1)S(1)}, u32[]{:S(2)}, u32[]{:S(2)}) collective-permute-start(bf16[64,4096]{1,0:T(8,128)(2,1)S(1)} %get-tuple-element.40), channel_id=1, source_target_pairs={{0,1},{1,0},{2,3},{3,2},{4,5},{5,4},{6,7},{7,6},{8,9},{9,8},{10,11... | collective-permute-start | bytes 1572872 | tf_op jit(solution)/shard_map/ppermute | solution.py:234
  26.5 7.9 %collective-permute-start.8 = (bf16[8,3584]{1,0:T(8,128)(2,1)S(1)}, bf16[8,3584]{1,0:T(8,128)(2,1)S(1)}, u32[]{:S(2)}, u32[]{:S(2)}) collective-permute-start(bf16[8,3584]{1,0:T(8,128)(2,1)S(1)} %get-tuple-element.42), channel_id=1, source_target_pairs={{0,10},{2,8},{4,14},{6,12},{8,2},{10,0},{12,6},{14,4},{1,11},{3,9}... | collective-permute-start | bytes 172040 | tf_op jit(solution)/shard_map/ppermute | solution.py:162
  28.2 7.3 %collective-permute-start.9 = (bf16[8,3584]{1,0:T(8,128)(2,1)S(1)}, bf16[8,3584]{1,0:T(8,128)(2,1)S(1)}, u32[]{:S(2)}, u32[]{:S(2)}) collective-permute-start(bf16[8,3584]{1,0:T(8,128)(2,1)S(1)} %get-tuple-element.43), channel_id=1, source_target_pairs={{0,12},{2,14},{4,8},{6,10},{8,4},{10,6},{12,0},{14,2},{1,13},{3,15... | collective-permute-start | bytes 172040 | tf_op jit(solution)/shard_map/ppermute | solution.py:162
  29.7 7.2 %collective-permute-start.10 = (bf16[8,3584]{1,0:T(8,128)(2,1)S(1)}, bf16[8,3584]{1,0:T(8,128)(2,1)S(1)}, u32[]{:S(2)}, u32[]{:S(2)}) collective-permute-start(bf16[8,3584]{1,0:T(8,128)(2,1)S(1)} %get-tuple-element.44), channel_id=1, source_target_pairs={{0,6},{2,4},{4,2},{6,0},{8,14},{10,12},{12,10},{14,8},{1,7},{3,5},... | collective-permute-start | bytes 172040 | tf_op jit(solution)/shard_map/ppermute | solution.py:162
  31.1 7.1 %collective-permute-start.11 = (bf16[8,3584]{1,0:T(8,128)(2,1)S(1)}, bf16[8,3584]{1,0:T(8,128)(2,1)S(1)}, u32[]{:S(2)}, u32[]{:S(2)}) collective-permute-start(bf16[8,3584]{1,0:T(8,128)(2,1)S(1)} %get-tuple-element.45), channel_id=1, source_target_pairs={{0,14},{2,12},{4,10},{6,8},{8,6},{10,4},{12,2},{14,0},{1,15},{3,13... | collective-permute-start | bytes 172040 | tf_op jit(solution)/shard_map/ppermute | solution.py:162
  34.0 5.9 %collective-permute-start.12 = (bf16[8,3584]{1,0:T(8,128)(2,1)S(1)}, bf16[8,3584]{1,0:T(8,128)(2,1)S(1)}, u32[]{:S(2)}, u32[]{:S(2)}) collective-permute-start(bf16[8,3584]{1,0:T(8,128)(2,1)S(1)} %get-tuple-element.46), channel_id=1, source_target_pairs={{0,8},{2,10},{4,12},{6,14},{8,0},{10,2},{12,4},{14,6},{1,9},{3,11}... | collective-permute-start | bytes 172040 | tf_op jit(solution)/shard_map/ppermute | solution.py:162
  34.4 5.5 %collective-permute-start.13 = (bf16[8,3584]{1,0:T(8,128)(2,1)S(1)}, bf16[8,3584]{1,0:T(8,128)(2,1)S(1)}, u32[]{:S(2)}, u32[]{:S(2)}) collective-permute-start(bf16[8,3584]{1,0:T(8,128)(2,1)S(1)} %get-tuple-element.47), channel_id=1, source_target_pairs={{0,4},{2,6},{4,0},{6,2},{8,12},{10,14},{12,8},{14,10},{1,5},{3,7},... | collective-permute-start | bytes 172040 | tf_op jit(solution)/shard_map/ppermute | solution.py:162
  35.4 4.4 %collective-permute-start.14 = (bf16[8,3584]{1,0:T(8,128)(2,1)S(1)}, bf16[8,3584]{1,0:T(8,128)(2,1)S(1)}, u32[]{:S(2)}, u32[]{:S(2)}) collective-permute-start(bf16[8,3584]{1,0:T(8,128)(2,1)S(1)} %get-tuple-element.48), channel_id=1, source_target_pairs={{0,2},{2,0},{4,6},{6,4},{8,10},{10,8},{12,14},{14,12},{1,3},{3,1},... | collective-permute-start | bytes 172040 | tf_op jit(solution)/shard_map/ppermute | solution.py:162

commit v6 on v5

--- a/solution.py
+++ b/solution.py
@@ -10,7 +10,7 @@
 HIDDEN_SIZE = 2048
 ROUTED = 256
 ORDER = (0, 7, 6, 5, 3, 4, 2, 1)
-RETURN = (0, 5, 6, 3, 7, 4, 2, 1)
+RETURN = (0, 5, 6, 3, 7, 2, 4, 1)
 BF16 = jnp.bfloat16
 F32 = jnp.float32
 VMEM = pl.BlockSpec(memory_space=pltpu.VMEM)

time: 41.2 us -> 41 us (level)
  transfers between devices with their start and end apart: 15 -> 15, of which waited for: 9 -> 11; matrix products, arithmetic and copies ran while one was open for 0% -> 0% of each run, Pallas kernels for 0% -> 0%
where the time goes in v6:
time: 41 us; the launch traced here: 40.8 us
  starting transfers between devices  22.7 us (55%)
  waiting for transfers between devices  9.2 us (22%)
  Pallas kernels  8.76 us (21%)
    ppermute x14, starting transfers between devices, swap(): lax.ppermute(block, 'expert', [(i, i ^ j) for i in range(len(order))])  22.7 us
    ppermute x14, waiting for transfers between devices, swap(): lax.ppermute(block, 'expert', [(i, i ^ j) for i in range(len(order))])  7.3 us
    pallas_call x1, Pallas kernels, local(): pl.pallas_call(functools.partial(up_kernel, parts), in_specs=[VMEM] * (pa...  4 us
    pallas_call x1, Pallas kernels, local(): pl.pallas_call(down_kernel, in_specs=[VMEM] * 3, out_specs=[VMEM] * parts...  2.09 us
    ppermute x1, waiting for transfers between devices, local(): lax.ppermute(give, 'tensor', [(i, (i + 1) % cores) for i in range(cores)])  1.9 us
    pallas_call x1, Pallas kernels, local(): pl.pallas_call(functools.partial(route_kernel, slots, split, direct), in_...  1.24 us
    pallas_call x1, Pallas kernels, local(): pl.pallas_call(functools.partial(mix_kernel, parts), in_specs=[VMEM] * (1...  1.17 us
  transfers between devices with their start and end apart: 15, of which 11 were waited for; matrix products, arithmetic and copies ran while one was open for 0% of the time, Pallas kernels for 0%

profile of v6, /device:TPU:0, one launch (start us, length us, event | category | flops | bytes accessed | tf_op | source)
XLA Modules:
  0.0 40.8 jit_solution(7838247232168447581)
XLA Ops:
  0.0 1.2 %route.1 = (bf16[64,128]{1,0:T(8,128)(2,1)S(1)}, f32[64,128]{1,0:T(8,128)S(1)}, bf16[128,3584]{1,0:T(8,128)(2,1)S(1)}) custom-call(s32[8,128]{1,0:T(8,128)} %bitcast.8, f32[8,128]{1,0:T(8,128)} %bitcast.9, bf16[128,3584]{1,0:T(8,128)(2,1)} %tokens_hbm.1), custom_call_target="tpu_custom_call" | custom-call | flops 1000000 | tf_op jit(solution)/shard_map/route/pallas_call | solution.py:186
  1.5 6.0 %collective-permute-start = (bf16[8,3584]{1,0:T(8,128)(2,1)S(1)}, bf16[8,3584]{1,0:T(8,128)(2,1)S(1)}, u32[]{:S(2)}, u32[]{:S(2)}) collective-permute-start(bf16[8,3584]{1,0:T(8,128)(2,1)S(1)} %get-tuple-element.30), channel_id=1, source_target_pairs={{0,14},{2,12},{4,10},{6,8},{8,6},{10,4},{12,2},{14,0},{1,15},{3,13... | collective-permute-start | bytes 172040 | tf_op jit(solution)/shard_map/ppermute | solution.py:162
  7.8 0.8 %collective-permute-start.2 = (bf16[8,3584]{1,0:T(8,128)(2,1)S(1)}, bf16[8,3584]{1,0:T(8,128)(2,1)S(1)}, u32[]{:S(2)}, u32[]{:S(2)}) collective-permute-start(bf16[8,3584]{1,0:T(8,128)(2,1)S(1)} %get-tuple-element.32), channel_id=1, source_target_pairs={{0,10},{2,8},{4,14},{6,12},{8,2},{10,0},{12,6},{14,4},{1,11},{3,9}... | collective-permute-start | bytes 172040 | tf_op jit(solution)/shard_map/ppermute | solution.py:162
  8.6 4.3 %collective-permute-start.3 = (bf16[8,3584]{1,0:T(8,128)(2,1)S(1)}, bf16[8,3584]{1,0:T(8,128)(2,1)S(1)}, u32[]{:S(2)}, u32[]{:S(2)}) collective-permute-start(bf16[8,3584]{1,0:T(8,128)(2,1)S(1)} %get-tuple-element.33), channel_id=1, source_target_pairs={{0,6},{2,4},{4,2},{6,0},{8,14},{10,12},{12,10},{14,8},{1,7},{3,5},... | collective-permute-start | bytes 172040 | tf_op jit(solution)/shard_map/ppermute | solution.py:162
  12.9 0.8 %collective-permute-start.5 = (bf16[8,3584]{1,0:T(8,128)(2,1)S(1)}, bf16[8,3584]{1,0:T(8,128)(2,1)S(1)}, u32[]{:S(2)}, u32[]{:S(2)}) collective-permute-start(bf16[8,3584]{1,0:T(8,128)(2,1)S(1)} %get-tuple-element.35), channel_id=1, source_target_pairs={{0,4},{2,6},{4,0},{6,2},{8,12},{10,14},{12,8},{14,10},{1,5},{3,7},... | collective-permute-start | bytes 172040 | tf_op jit(solution)/shard_map/ppermute | solution.py:162
  13.7 0.5 %collective-permute-done.1.refs_2_ = bf16[8,3584]{1,0:T(8,128)(2,1)S(1)} collective-permute-done((bf16[8,3584]{1,0:T(8,128)(2,1)S(1)}, bf16[8,3584]{1,0:T(8,128)(2,1)S(1)}, u32[]{:S(2)}, u32[]{:S(2)}) %collective-permute-start.1) | collective-permute-done | bytes 57376 | tf_op jit(solution)/shard_map/ppermute | solution.py:162
  14.2 0.4 %collective-permute-start.6 = (bf16[8,3584]{1,0:T(8,128)(2,1)S(1)}, bf16[8,3584]{1,0:T(8,128)(2,1)S(1)}, u32[]{:S(2)}, u32[]{:S(2)}) collective-permute-start(bf16[8,3584]{1,0:T(8,128)(2,1)S(1)} %get-tuple-element.36), channel_id=1, source_target_pairs={{0,2},{2,0},{4,6},{6,4},{8,10},{10,8},{12,14},{14,12},{1,3},{3,1},... | collective-permute-start | bytes 172040 | tf_op jit(solution)/shard_map/ppermute | solution.py:162
  14.6 1.5 %collective-permute-done.2.refs_3_ = bf16[8,3584]{1,0:T(8,128)(2,1)S(1)} collective-permute-done((bf16[8,3584]{1,0:T(8,128)(2,1)S(1)}, bf16[8,3584]{1,0:T(8,128)(2,1)S(1)}, u32[]{:S(2)}, u32[]{:S(2)}) %collective-permute-start.2) | collective-permute-done | bytes 57376 | tf_op jit(solution)/shard_map/ppermute | solution.py:162
  16.1 0.8 %collective-permute-done.3.refs_4_ = bf16[8,3584]{1,0:T(8,128)(2,1)S(1)} collective-permute-done((bf16[8,3584]{1,0:T(8,128)(2,1)S(1)}, bf16[8,3584]{1,0:T(8,128)(2,1)S(1)}, u32[]{:S(2)}, u32[]{:S(2)}) %collective-permute-start.3) | collective-permute-done | bytes 57376 | tf_op jit(solution)/shard_map/ppermute | solution.py:162
  16.9 1.0 %collective-permute-done.4.refs_5_ = bf16[8,3584]{1,0:T(8,128)(2,1)S(1)} collective-permute-done((bf16[8,3584]{1,0:T(8,128)(2,1)S(1)}, bf16[8,3584]{1,0:T(8,128)(2,1)S(1)}, u32[]{:S(2)}, u32[]{:S(2)}) %collective-permute-start.4) | collective-permute-done | bytes 57376 | tf_op jit(solution)/shard_map/ppermute | solution.py:162
  18.0 0.4 %collective-permute-done.6.refs_7_ = bf16[8,3584]{1,0:T(8,128)(2,1)S(1)} collective-permute-done((bf16[8,3584]{1,0:T(8,128)(2,1)S(1)}, bf16[8,3584]{1,0:T(8,128)(2,1)S(1)}, u32[]{:S(2)}, u32[]{:S(2)}) %collective-permute-start.6) | collective-permute-done | bytes 57376 | tf_op jit(solution)/shard_map/ppermute | solution.py:162
  18.4 4.0 %up.1 = (f32[64,4096]{1,0:T(8,128)S(1)}, bf16[64,4096]{1,0:T(8,128)(2,1)S(1)}, bf16[128,192]{1,0:T(8,128)(2,1)S(1)}) custom-call(bf16[8,3584]{1,0:T(8,128)(2,1)S(1)} %get-tuple-element.29.refs_0_, bf16[8,3584]{1,0:T(8,128)(2,1)S(1)} %collective-permute-done.refs_1_, bf16[8,3584]{1,0:T(8,128)(2,1)S(1)} %collective-permute-done.1.refs_2_, ...), custom_call_target="tpu_custom_call" | custom-call | tf_op jit(solution)/shard_map/up/pallas_call | solution.py:221
  22.5 1.9 %collective-permute-done.7.other_ref = bf16[64,4096]{1,0:T(8,128)(2,1)S(1)} collective-permute-done((bf16[64,4096]{1,0:T(8,128)(2,1)S(1)}, bf16[64,4096]{1,0:T(8,128)(2,1)S(1)}, u32[]{:S(2)}, u32[]{:S(2)}) %collective-permute-start.7) | collective-permute-done | bytes 524320 | tf_op jit(solution)/shard_map/ppermute | solution.py:234
  24.4 2.1 %down.1 = (bf16[8,3584]{1,0:T(8,128)(2,1)S(1)}, bf16[8,3584]{1,0:T(8,128)(2,1)S(1)}, bf16[8,3584]{1,0:T(8,128)(2,1)S(1)}, bf16[8,3584]{1,0:T(8,128)(2,1)S(1)}, b...) custom-call(f32[64,4096]{1,0:T(8,128)S(1)} %get-tuple-element.39.own, ...), custom_call_target="tpu_custom_call" | custom-call | tf_op jit(solution)/shard_map/down/pallas_call | solution.py:235
  26.5 1.7 %collective-permute-start.8 = (bf16[8,3584]{1,0:T(8,128)(2,1)S(1)}, bf16[8,3584]{1,0:T(8,128)(2,1)S(1)}, u32[]{:S(2)}, u32[]{:S(2)}) collective-permute-start(bf16[8,3584]{1,0:T(8,128)(2,1)S(1)} %get-tuple-element.42), channel_id=1, source_target_pairs={{0,10},{2,8},{4,14},{6,12},{8,2},{10,0},{12,6},{14,4},{1,11},{3,9}... | collective-permute-start | bytes 172040 | tf_op jit(solution)/shard_map/ppermute | solution.py:162
  28.2 1.5 %collective-permute-start.9 = (bf16[8,3584]{1,0:T(8,128)(2,1)S(1)}, bf16[8,3584]{1,0:T(8,128)(2,1)S(1)}, u32[]{:S(2)}, u32[]{:S(2)}) collective-permute-start(bf16[8,3584]{1,0:T(8,128)(2,1)S(1)} %get-tuple-element.43), channel_id=1, source_target_pairs={{0,12},{2,14},{4,8},{6,10},{8,4},{10,6},{12,0},{14,2},{1,13},{3,15... | collective-permute-start | bytes 172040 | tf_op jit(solution)/shard_map/ppermute | solution.py:162
  29.7 1.4 %collective-permute-start.10 = (bf16[8,3584]{1,0:T(8,128)(2,1)S(1)}, bf16[8,3584]{1,0:T(8,128)(2,1)S(1)}, u32[]{:S(2)}, u32[]{:S(2)}) collective-permute-start(bf16[8,3584]{1,0:T(8,128)(2,1)S(1)} %get-tuple-element.44), channel_id=1, source_target_pairs={{0,6},{2,4},{4,2},{6,0},{8,14},{10,12},{12,10},{14,8},{1,7},{3,5},... | collective-permute-start | bytes 172040 | tf_op jit(solution)/shard_map/ppermute | solution.py:162
  31.1 2.9 %collective-permute-start.11 = (bf16[8,3584]{1,0:T(8,128)(2,1)S(1)}, bf16[8,3584]{1,0:T(8,128)(2,1)S(1)}, u32[]{:S(2)}, u32[]{:S(2)}) collective-permute-start(bf16[8,3584]{1,0:T(8,128)(2,1)S(1)} %get-tuple-element.45), channel_id=1, source_target_pairs={{0,14},{2,12},{4,10},{6,8},{8,6},{10,4},{12,2},{14,0},{1,15},{3,13... | collective-permute-start | bytes 172040 | tf_op jit(solution)/shard_map/ppermute | solution.py:162
  34.4 1.1 %collective-permute-start.13 = (bf16[8,3584]{1,0:T(8,128)(2,1)S(1)}, bf16[8,3584]{1,0:T(8,128)(2,1)S(1)}, u32[]{:S(2)}, u32[]{:S(2)}) collective-permute-start(bf16[8,3584]{1,0:T(8,128)(2,1)S(1)} %get-tuple-element.47), channel_id=1, source_target_pairs={{0,8},{2,10},{4,12},{6,14},{8,0},{10,2},{12,4},{14,6},{1,9},{3,11}... | collective-permute-start | bytes 172040 | tf_op jit(solution)/shard_map/ppermute | solution.py:162
  35.4 1.5 %collective-permute-start.14 = (bf16[8,3584]{1,0:T(8,128)(2,1)S(1)}, bf16[8,3584]{1,0:T(8,128)(2,1)S(1)}, u32[]{:S(2)}, u32[]{:S(2)}) collective-permute-start(bf16[8,3584]{1,0:T(8,128)(2,1)S(1)} %get-tuple-element.48), channel_id=1, source_target_pairs={{0,2},{2,0},{4,6},{6,4},{8,10},{10,8},{12,14},{14,12},{1,3},{3,1},... | collective-permute-start | bytes 172040 | tf_op jit(solution)/shard_map/ppermute | solution.py:162
  36.9 1.1 %collective-permute-done.11.refs_4_ = bf16[8,3584]{1,0:T(8,128)(2,1)S(1)} collective-permute-done((bf16[8,3584]{1,0:T(8,128)(2,1)S(1)}, bf16[8,3584]{1,0:T(8,128)(2,1)S(1)}, u32[]{:S(2)}, u32[]{:S(2)}) %collective-permute-start.11) | collective-permute-done | bytes 57376 | tf_op jit(solution)/shard_map/ppermute | solution.py:162
  38.1 0.6 %collective-permute-done.12.refs_5_ = bf16[8,3584]{1,0:T(8,128)(2,1)S(1)} collective-permute-done((bf16[8,3584]{1,0:T(8,128)(2,1)S(1)}, bf16[8,3584]{1,0:T(8,128)(2,1)S(1)}, u32[]{:S(2)}, u32[]{:S(2)}) %collective-permute-start.12) | collective-permute-done | bytes 57376 | tf_op jit(solution)/shard_map/ppermute | solution.py:162
  38.6 0.8 %collective-permute-done.13.refs_6_ = bf16[8,3584]{1,0:T(8,128)(2,1)S(1)} collective-permute-done((bf16[8,3584]{1,0:T(8,128)(2,1)S(1)}, bf16[8,3584]{1,0:T(8,128)(2,1)S(1)}, u32[]{:S(2)}, u32[]{:S(2)}) %collective-permute-start.13) | collective-permute-done | bytes 57376 | tf_op jit(solution)/shard_map/ppermute | solution.py:162
  39.6 1.2 %mix.1 = bf16[128,3584]{1,0:T(8,128)(2,1)} custom-call(bf16[128,192]{1,0:T(8,128)(2,1)S(1)} %get-tuple-element.38.mix_ref, bf16[8,3584]{1,0:T(8,128)(2,1)S(1)} %get-tuple-element.41.refs_0_, bf16[8,3584]{1,0:T(8,128)(2,1)S(1)} %collective-permute-done.8.refs_1_, bf16[8,3584]{1,0:T(8,128)(2,1)S(1)} %collective-permute-done.9.refs_2_, ...), custom_call_target="tpu_custom_call" | custom-call | tf_op jit(solution)/shard_map/mix/pallas_call | solution.py:251
  (17 shorter events, 1.2 us)
Async XLA Ops:
  1.2 17.1 %copy-start = (bf16[1,3584,2048]{2,1,0:T(8,128)(2,1)S(1)}, bf16[1,3584,2048]{2,1,0:T(8,128)(2,1)}, u32[]{:S(2)}) copy-start(bf16[1,3584,2048]{2,1,0:T(8,128)(2,1)} %param.9) | copy-start | bytes 44040196
  1.3 17.1 %copy-start.1 = (bf16[1,3584,2048]{2,1,0:T(8,128)(2,1)S(1)}, bf16[1,3584,2048]{2,1,0:T(8,128)(2,1)}, u32[]{:S(2)}) copy-start(bf16[1,3584,2048]{2,1,0:T(8,128)(2,1)} %param.10) | copy-start | bytes 44040196
  1.5 11.3 %collective-permute-start = (bf16[8,3584]{1,0:T(8,128)(2,1)S(1)}, bf16[8,3584]{1,0:T(8,128)(2,1)S(1)}, u32[]{:S(2)}, u32[]{:S(2)}) collective-permute-start(bf16[8,3584]{1,0:T(8,128)(2,1)S(1)} %get-tuple-element.30), channel_id=1, source_target_pairs={{0,14},{2,12},{4,10},{6,8},{8,6},{10,4},{12,2},{14,0},{1,15},{3,13... | collective-permute-start | bytes 172040 | tf_op jit(solution)/shard_map/ppermute | solution.py:162
  7.6 6.6 %collective-permute-start.1 = (bf16[8,3584]{1,0:T(8,128)(2,1)S(1)}, bf16[8,3584]{1,0:T(8,128)(2,1)S(1)}, u32[]{:S(2)}, u32[]{:S(2)}) collective-permute-start(bf16[8,3584]{1,0:T(8,128)(2,1)S(1)} %get-tuple-element.31), channel_id=1, source_target_pairs={{0,12},{2,14},{4,8},{6,10},{8,4},{10,6},{12,0},{14,2},{1,13},{3,15... | collective-permute-start | bytes 172040 | tf_op jit(solution)/shard_map/ppermute | solution.py:162
  7.8 8.3 %collective-permute-start.2 = (bf16[8,3584]{1,0:T(8,128)(2,1)S(1)}, bf16[8,3584]{1,0:T(8,128)(2,1)S(1)}, u32[]{:S(2)}, u32[]{:S(2)}) collective-permute-start(bf16[8,3584]{1,0:T(8,128)(2,1)S(1)} %get-tuple-element.32), channel_id=1, source_target_pairs={{0,10},{2,8},{4,14},{6,12},{8,2},{10,0},{12,6},{14,4},{1,11},{3,9}... | collective-permute-start | bytes 172040 | tf_op jit(solution)/shard_map/ppermute | solution.py:162
  8.6 8.3 %collective-permute-start.3 = (bf16[8,3584]{1,0:T(8,128)(2,1)S(1)}, bf16[8,3584]{1,0:T(8,128)(2,1)S(1)}, u32[]{:S(2)}, u32[]{:S(2)}) collective-permute-start(bf16[8,3584]{1,0:T(8,128)(2,1)S(1)} %get-tuple-element.33), channel_id=1, source_target_pairs={{0,6},{2,4},{4,2},{6,0},{8,14},{10,12},{12,10},{14,8},{1,7},{3,5},... | collective-permute-start | bytes 172040 | tf_op jit(solution)/shard_map/ppermute | solution.py:162
  12.9 5.1 %collective-permute-start.4 = (bf16[8,3584]{1,0:T(8,128)(2,1)S(1)}, bf16[8,3584]{1,0:T(8,128)(2,1)S(1)}, u32[]{:S(2)}, u32[]{:S(2)}) collective-permute-start(bf16[8,3584]{1,0:T(8,128)(2,1)S(1)} %get-tuple-element.34), channel_id=1, source_target_pairs={{0,8},{2,10},{4,12},{6,14},{8,0},{10,2},{12,4},{14,6},{1,9},{3,11}... | collective-permute-start | bytes 172040 | tf_op jit(solution)/shard_map/ppermute | solution.py:162
  12.9 5.1 %collective-permute-start.5 = (bf16[8,3584]{1,0:T(8,128)(2,1)S(1)}, bf16[8,3584]{1,0:T(8,128)(2,1)S(1)}, u32[]{:S(2)}, u32[]{:S(2)}) collective-permute-start(bf16[8,3584]{1,0:T(8,128)(2,1)S(1)} %get-tuple-element.35), channel_id=1, source_target_pairs={{0,4},{2,6},{4,0},{6,2},{8,12},{10,14},{12,8},{14,10},{1,5},{3,7},... | collective-permute-start | bytes 172040 | tf_op jit(solution)/shard_map/ppermute | solution.py:162
  14.2 4.2 %collective-permute-start.6 = (bf16[8,3584]{1,0:T(8,128)(2,1)S(1)}, bf16[8,3584]{1,0:T(8,128)(2,1)S(1)}, u32[]{:S(2)}, u32[]{:S(2)}) collective-permute-start(bf16[8,3584]{1,0:T(8,128)(2,1)S(1)} %get-tuple-element.36), channel_id=1, source_target_pairs={{0,2},{2,0},{4,6},{6,4},{8,10},{10,8},{12,14},{14,12},{1,3},{3,1},... | collective-permute-start | bytes 172040 | tf_op jit(solution)/shard_map/ppermute | solution.py:162
  18.4 6.0 %copy-start.2 = (bf16[1,2048,3584]{2,1,0:T(8,128)(2,1)S(1)}, bf16[1,2048,3584]{2,1,0:T(8,128)(2,1)}, u32[]{:S(2)}) copy-start(bf16[1,2048,3584]{2,1,0:T(8,128)(2,1)} %param.11) | copy-start | bytes 44040196
  22.4 2.0 %collective-permute-start.7 = (bf16[64,4096]{1,0:T(8,128)(2,1)S(1)}, bf16[64,4096]{1,0:T(8,128)(2,1)S(1)}, u32[]{:S(2)}, u32[]{:S(2)}) collective-permute-start(bf16[64,4096]{1,0:T(8,128)(2,1)S(1)} %get-tuple-element.40), channel_id=1, source_target_pairs={{0,1},{1,0},{2,3},{3,2},{4,5},{5,4},{6,7},{7,6},{8,9},{9,8},{10,11... | collective-permute-start | bytes 1572872 | tf_op jit(solution)/shard_map/ppermute | solution.py:234
  26.5 7.9 %collective-permute-start.8 = (bf16[8,3584]{1,0:T(8,128)(2,1)S(1)}, bf16[8,3584]{1,0:T(8,128)(2,1)S(1)}, u32[]{:S(2)}, u32[]{:S(2)}) collective-permute-start(bf16[8,3584]{1,0:T(8,128)(2,1)S(1)} %get-tuple-element.42), channel_id=1, source_target_pairs={{0,10},{2,8},{4,14},{6,12},{8,2},{10,0},{12,6},{14,4},{1,11},{3,9}... | collective-permute-start | bytes 172040 | tf_op jit(solution)/shard_map/ppermute | solution.py:162
  28.2 7.3 %collective-permute-start.9 = (bf16[8,3584]{1,0:T(8,128)(2,1)S(1)}, bf16[8,3584]{1,0:T(8,128)(2,1)S(1)}, u32[]{:S(2)}, u32[]{:S(2)}) collective-permute-start(bf16[8,3584]{1,0:T(8,128)(2,1)S(1)} %get-tuple-element.43), channel_id=1, source_target_pairs={{0,12},{2,14},{4,8},{6,10},{8,4},{10,6},{12,0},{14,2},{1,13},{3,15... | collective-permute-start | bytes 172040 | tf_op jit(solution)/shard_map/ppermute | solution.py:162
  29.7 7.2 %collective-permute-start.10 = (bf16[8,3584]{1,0:T(8,128)(2,1)S(1)}, bf16[8,3584]{1,0:T(8,128)(2,1)S(1)}, u32[]{:S(2)}, u32[]{:S(2)}) collective-permute-start(bf16[8,3584]{1,0:T(8,128)(2,1)S(1)} %get-tuple-element.44), channel_id=1, source_target_pairs={{0,6},{2,4},{4,2},{6,0},{8,14},{10,12},{12,10},{14,8},{1,7},{3,5},... | collective-permute-start | bytes 172040 | tf_op jit(solution)/shard_map/ppermute | solution.py:162
  31.1 7.0 %collective-permute-start.11 = (bf16[8,3584]{1,0:T(8,128)(2,1)S(1)}, bf16[8,3584]{1,0:T(8,128)(2,1)S(1)}, u32[]{:S(2)}, u32[]{:S(2)}) collective-permute-start(bf16[8,3584]{1,0:T(8,128)(2,1)S(1)} %get-tuple-element.45), channel_id=1, source_target_pairs={{0,14},{2,12},{4,10},{6,8},{8,6},{10,4},{12,2},{14,0},{1,15},{3,13... | collective-permute-start | bytes 172040 | tf_op jit(solution)/shard_map/ppermute | solution.py:162
  34.0 4.7 %collective-permute-start.12 = (bf16[8,3584]{1,0:T(8,128)(2,1)S(1)}, bf16[8,3584]{1,0:T(8,128)(2,1)S(1)}, u32[]{:S(2)}, u32[]{:S(2)}) collective-permute-start(bf16[8,3584]{1,0:T(8,128)(2,1)S(1)} %get-tuple-element.46), channel_id=1, source_target_pairs={{0,4},{2,6},{4,0},{6,2},{8,12},{10,14},{12,8},{14,10},{1,5},{3,7},... | collective-permute-start | bytes 172040 | tf_op jit(solution)/shard_map/ppermute | solution.py:162
  34.4 5.1 %collective-permute-start.13 = (bf16[8,3584]{1,0:T(8,128)(2,1)S(1)}, bf16[8,3584]{1,0:T(8,128)(2,1)S(1)}, u32[]{:S(2)}, u32[]{:S(2)}) collective-permute-start(bf16[8,3584]{1,0:T(8,128)(2,1)S(1)} %get-tuple-element.47), channel_id=1, source_target_pairs={{0,8},{2,10},{4,12},{6,14},{8,0},{10,2},{12,4},{14,6},{1,9},{3,11}... | collective-permute-start | bytes 172040 | tf_op jit(solution)/shard_map/ppermute | solution.py:162
  35.4 4.2 %collective-permute-start.14 = (bf16[8,3584]{1,0:T(8,128)(2,1)S(1)}, bf16[8,3584]{1,0:T(8,128)(2,1)S(1)}, u32[]{:S(2)}, u32[]{:S(2)}) collective-permute-start(bf16[8,3584]{1,0:T(8,128)(2,1)S(1)} %get-tuple-element.48), channel_id=1, source_target_pairs={{0,2},{2,0},{4,6},{6,4},{8,10},{10,8},{12,14},{14,12},{1,3},{3,1},... | collective-permute-start | bytes 172040 | tf_op jit(solution)/shard_map/ppermute | solution.py:162

commit v7 on v6

--- a/solution.py
+++ b/solution.py
@@ -10,7 +10,7 @@
 HIDDEN_SIZE = 2048
 ROUTED = 256
 ORDER = (0, 7, 6, 5, 3, 4, 2, 1)
-RETURN = (0, 5, 6, 3, 7, 2, 4, 1)
+RETURN = (0, 5, 6, 7, 3, 4, 2, 1)
 BF16 = jnp.bfloat16
 F32 = jnp.float32
 VMEM = pl.BlockSpec(memory_space=pltpu.VMEM)

time: 41 us -> 41.2 us (level)
  transfers between devices with their start and end apart: 15 -> 15, of which waited for: 11 -> 10; matrix products, arithmetic and copies ran while one was open for 0% -> 0% of each run, Pallas kernels for 0% -> 0%
where the time goes in v7:
time: 41.2 us; the launch traced here: 41 us
  starting transfers between devices  22.6 us (55%)
  waiting for transfers between devices  9.6 us (23%)
  Pallas kernels  8.76 us (21%)
    ppermute x14, starting transfers between devices, swap(): lax.ppermute(block, 'expert', [(i, i ^ j) for i in range(len(order))])  22.5 us
    ppermute x14, waiting for transfers between devices, swap(): lax.ppermute(block, 'expert', [(i, i ^ j) for i in range(len(order))])  7.71 us
    pallas_call x1, Pallas kernels, local(): pl.pallas_call(functools.partial(up_kernel, parts), in_specs=[VMEM] * (pa...  4 us
    pallas_call x1, Pallas kernels, local(): pl.pallas_call(down_kernel, in_specs=[VMEM] * 3, out_specs=[VMEM] * parts...  2.09 us
    ppermute x1, waiting for transfers between devices, local(): lax.ppermute(give, 'tensor', [(i, (i + 1) % cores) for i in range(cores)])  1.9 us
    pallas_call x1, Pallas kernels, local(): pl.pallas_call(functools.partial(route_kernel, slots, split, direct), in_...  1.24 us
    pallas_call x1, Pallas kernels, local(): pl.pallas_call(functools.partial(mix_kernel, parts), in_specs=[VMEM] * (1...  1.17 us
  transfers between devices with their start and end apart: 15, of which 10 were waited for; matrix products, arithmetic and copies ran while one was open for 0% of the time, Pallas kernels for 0%

profile of v7, /device:TPU:0, one launch (start us, length us, event | category | flops | bytes accessed | tf_op | source)
XLA Modules:
  0.0 41.0 jit_solution(9559909248891943715)
XLA Ops:
  0.0 1.2 %route.1 = (bf16[64,128]{1,0:T(8,128)(2,1)S(1)}, f32[64,128]{1,0:T(8,128)S(1)}, bf16[128,3584]{1,0:T(8,128)(2,1)S(1)}) custom-call(s32[8,128]{1,0:T(8,128)} %bitcast.8, f32[8,128]{1,0:T(8,128)} %bitcast.9, bf16[128,3584]{1,0:T(8,128)(2,1)} %tokens_hbm.1), custom_call_target="tpu_custom_call" | custom-call | flops 1000000 | tf_op jit(solution)/shard_map/route/pallas_call | solution.py:186
  1.3 0.3 send.1
  1.5 6.0 %collective-permute-start = (bf16[8,3584]{1,0:T(8,128)(2,1)S(1)}, bf16[8,3584]{1,0:T(8,128)(2,1)S(1)}, u32[]{:S(2)}, u32[]{:S(2)}) collective-permute-start(bf16[8,3584]{1,0:T(8,128)(2,1)S(1)} %get-tuple-element.30), channel_id=1, source_target_pairs={{0,14},{2,12},{4,10},{6,8},{8,6},{10,4},{12,2},{14,0},{1,15},{3,13... | collective-permute-start | bytes 172040 | tf_op jit(solution)/shard_map/ppermute | solution.py:162
  7.8 0.8 %collective-permute-start.2 = (bf16[8,3584]{1,0:T(8,128)(2,1)S(1)}, bf16[8,3584]{1,0:T(8,128)(2,1)S(1)}, u32[]{:S(2)}, u32[]{:S(2)}) collective-permute-start(bf16[8,3584]{1,0:T(8,128)(2,1)S(1)} %get-tuple-element.32), channel_id=1, source_target_pairs={{0,10},{2,8},{4,14},{6,12},{8,2},{10,0},{12,6},{14,4},{1,11},{3,9}... | collective-permute-start | bytes 172040 | tf_op jit(solution)/shard_map/ppermute | solution.py:162
  8.6 4.3 %collective-permute-start.3 = (bf16[8,3584]{1,0:T(8,128)(2,1)S(1)}, bf16[8,3584]{1,0:T(8,128)(2,1)S(1)}, u32[]{:S(2)}, u32[]{:S(2)}) collective-permute-start(bf16[8,3584]{1,0:T(8,128)(2,1)S(1)} %get-tuple-element.33), channel_id=1, source_target_pairs={{0,6},{2,4},{4,2},{6,0},{8,14},{10,12},{12,10},{14,8},{1,7},{3,5},... | collective-permute-start | bytes 172040 | tf_op jit(solution)/shard_map/ppermute | solution.py:162
  12.9 0.8 %collective-permute-start.5 = (bf16[8,3584]{1,0:T(8,128)(2,1)S(1)}, bf16[8,3584]{1,0:T(8,128)(2,1)S(1)}, u32[]{:S(2)}, u32[]{:S(2)}) collective-permute-start(bf16[8,3584]{1,0:T(8,128)(2,1)S(1)} %get-tuple-element.35), channel_id=1, source_target_pairs={{0,4},{2,6},{4,0},{6,2},{8,12},{10,14},{12,8},{14,10},{1,5},{3,7},... | collective-permute-start | bytes 172040 | tf_op jit(solution)/shard_map/ppermute | solution.py:162
  13.7 0.5 %collective-permute-done.1.refs_2_ = bf16[8,3584]{1,0:T(8,128)(2,1)S(1)} collective-permute-done((bf16[8,3584]{1,0:T(8,128)(2,1)S(1)}, bf16[8,3584]{1,0:T(8,128)(2,1)S(1)}, u32[]{:S(2)}, u32[]{:S(2)}) %collective-permute-start.1) | collective-permute-done | bytes 57376 | tf_op jit(solution)/shard_map/ppermute | solution.py:162
  14.2 0.4 %collective-permute-start.6 = (bf16[8,3584]{1,0:T(8,128)(2,1)S(1)}, bf16[8,3584]{1,0:T(8,128)(2,1)S(1)}, u32[]{:S(2)}, u32[]{:S(2)}) collective-permute-start(bf16[8,3584]{1,0:T(8,128)(2,1)S(1)} %get-tuple-element.36), channel_id=1, source_target_pairs={{0,2},{2,0},{4,6},{6,4},{8,10},{10,8},{12,14},{14,12},{1,3},{3,1},... | collective-permute-start | bytes 172040 | tf_op jit(solution)/shard_map/ppermute | solution.py:162
  14.6 1.5 %collective-permute-done.2.refs_3_ = bf16[8,3584]{1,0:T(8,128)(2,1)S(1)} collective-permute-done((bf16[8,3584]{1,0:T(8,128)(2,1)S(1)}, bf16[8,3584]{1,0:T(8,128)(2,1)S(1)}, u32[]{:S(2)}, u32[]{:S(2)}) %collective-permute-start.2) | collective-permute-done | bytes 57376 | tf_op jit(solution)/shard_map/ppermute | solution.py:162
  16.1 0.8 %collective-permute-done.3.refs_4_ = bf16[8,3584]{1,0:T(8,128)(2,1)S(1)} collective-permute-done((bf16[8,3584]{1,0:T(8,128)(2,1)S(1)}, bf16[8,3584]{1,0:T(8,128)(2,1)S(1)}, u32[]{:S(2)}, u32[]{:S(2)}) %collective-permute-start.3) | collective-permute-done | bytes 57376 | tf_op jit(solution)/shard_map/ppermute | solution.py:162
  16.9 1.0 %collective-permute-done.4.refs_5_ = bf16[8,3584]{1,0:T(8,128)(2,1)S(1)} collective-permute-done((bf16[8,3584]{1,0:T(8,128)(2,1)S(1)}, bf16[8,3584]{1,0:T(8,128)(2,1)S(1)}, u32[]{:S(2)}, u32[]{:S(2)}) %collective-permute-start.4) | collective-permute-done | bytes 57376 | tf_op jit(solution)/shard_map/ppermute | solution.py:162
  18.0 0.4 %collective-permute-done.6.refs_7_ = bf16[8,3584]{1,0:T(8,128)(2,1)S(1)} collective-permute-done((bf16[8,3584]{1,0:T(8,128)(2,1)S(1)}, bf16[8,3584]{1,0:T(8,128)(2,1)S(1)}, u32[]{:S(2)}, u32[]{:S(2)}) %collective-permute-start.6) | collective-permute-done | bytes 57376 | tf_op jit(solution)/shard_map/ppermute | solution.py:162
  18.4 4.0 %up.1 = (f32[64,4096]{1,0:T(8,128)S(1)}, bf16[64,4096]{1,0:T(8,128)(2,1)S(1)}, bf16[128,192]{1,0:T(8,128)(2,1)S(1)}) custom-call(bf16[8,3584]{1,0:T(8,128)(2,1)S(1)} %get-tuple-element.29.refs_0_, bf16[8,3584]{1,0:T(8,128)(2,1)S(1)} %collective-permute-done.refs_1_, bf16[8,3584]{1,0:T(8,128)(2,1)S(1)} %collective-permute-done.1.refs_2_, ...), custom_call_target="tpu_custom_call" | custom-call | tf_op jit(solution)/shard_map/up/pallas_call | solution.py:221
  22.5 1.9 %collective-permute-done.7.other_ref = bf16[64,4096]{1,0:T(8,128)(2,1)S(1)} collective-permute-done((bf16[64,4096]{1,0:T(8,128)(2,1)S(1)}, bf16[64,4096]{1,0:T(8,128)(2,1)S(1)}, u32[]{:S(2)}, u32[]{:S(2)}) %collective-permute-start.7) | collective-permute-done | bytes 524320 | tf_op jit(solution)/shard_map/ppermute | solution.py:234
  24.4 2.1 %down.1 = (bf16[8,3584]{1,0:T(8,128)(2,1)S(1)}, bf16[8,3584]{1,0:T(8,128)(2,1)S(1)}, bf16[8,3584]{1,0:T(8,128)(2,1)S(1)}, bf16[8,3584]{1,0:T(8,128)(2,1)S(1)}, b...) custom-call(f32[64,4096]{1,0:T(8,128)S(1)} %get-tuple-element.39.own, ...), custom_call_target="tpu_custom_call" | custom-call | tf_op jit(solution)/shard_map/down/pallas_call | solution.py:235
  26.5 1.7 %collective-permute-start.8 = (bf16[8,3584]{1,0:T(8,128)(2,1)S(1)}, bf16[8,3584]{1,0:T(8,128)(2,1)S(1)}, u32[]{:S(2)}, u32[]{:S(2)}) collective-permute-start(bf16[8,3584]{1,0:T(8,128)(2,1)S(1)} %get-tuple-element.42), channel_id=1, source_target_pairs={{0,10},{2,8},{4,14},{6,12},{8,2},{10,0},{12,6},{14,4},{1,11},{3,9}... | collective-permute-start | bytes 172040 | tf_op jit(solution)/shard_map/ppermute | solution.py:162
  28.2 1.5 %collective-permute-start.9 = (bf16[8,3584]{1,0:T(8,128)(2,1)S(1)}, bf16[8,3584]{1,0:T(8,128)(2,1)S(1)}, u32[]{:S(2)}, u32[]{:S(2)}) collective-permute-start(bf16[8,3584]{1,0:T(8,128)(2,1)S(1)} %get-tuple-element.43), channel_id=1, source_target_pairs={{0,12},{2,14},{4,8},{6,10},{8,4},{10,6},{12,0},{14,2},{1,13},{3,15... | collective-permute-start | bytes 172040 | tf_op jit(solution)/shard_map/ppermute | solution.py:162
  29.7 3.3 %collective-permute-start.10 = (bf16[8,3584]{1,0:T(8,128)(2,1)S(1)}, bf16[8,3584]{1,0:T(8,128)(2,1)S(1)}, u32[]{:S(2)}, u32[]{:S(2)}) collective-permute-start(bf16[8,3584]{1,0:T(8,128)(2,1)S(1)} %get-tuple-element.44), channel_id=1, source_target_pairs={{0,14},{2,12},{4,10},{6,8},{8,6},{10,4},{12,2},{14,0},{1,15},{3,13... | collective-permute-start | bytes 172040 | tf_op jit(solution)/shard_map/ppermute | solution.py:162
  33.1 1.9 %collective-permute-start.12 = (bf16[8,3584]{1,0:T(8,128)(2,1)S(1)}, bf16[8,3584]{1,0:T(8,128)(2,1)S(1)}, u32[]{:S(2)}, u32[]{:S(2)}) collective-permute-start(bf16[8,3584]{1,0:T(8,128)(2,1)S(1)} %get-tuple-element.46), channel_id=1, source_target_pairs={{0,8},{2,10},{4,12},{6,14},{8,0},{10,2},{12,4},{14,6},{1,9},{3,11}... | collective-permute-start | bytes 172040 | tf_op jit(solution)/shard_map/ppermute | solution.py:162
  35.0 1.5 %collective-permute-start.14 = (bf16[8,3584]{1,0:T(8,128)(2,1)S(1)}, bf16[8,3584]{1,0:T(8,128)(2,1)S(1)}, u32[]{:S(2)}, u32[]{:S(2)}) collective-permute-start(bf16[8,3584]{1,0:T(8,128)(2,1)S(1)} %get-tuple-element.48), channel_id=1, source_target_pairs={{0,2},{2,0},{4,6},{6,4},{8,10},{10,8},{12,14},{14,12},{1,3},{3,1},... | collective-permute-start | bytes 172040 | tf_op jit(solution)/shard_map/ppermute | solution.py:162
  36.4 0.5 %collective-permute-done.10.refs_3_ = bf16[8,3584]{1,0:T(8,128)(2,1)S(1)} collective-permute-done((bf16[8,3584]{1,0:T(8,128)(2,1)S(1)}, bf16[8,3584]{1,0:T(8,128)(2,1)S(1)}, u32[]{:S(2)}, u32[]{:S(2)}) %collective-permute-start.10) | collective-permute-done | bytes 57376 | tf_op jit(solution)/shard_map/ppermute | solution.py:162
  37.0 1.4 %collective-permute-done.11.refs_4_ = bf16[8,3584]{1,0:T(8,128)(2,1)S(1)} collective-permute-done((bf16[8,3584]{1,0:T(8,128)(2,1)S(1)}, bf16[8,3584]{1,0:T(8,128)(2,1)S(1)}, u32[]{:S(2)}, u32[]{:S(2)}) %collective-permute-start.11) | collective-permute-done | bytes 57376 | tf_op jit(solution)/shard_map/ppermute | solution.py:162
  38.4 1.3 %collective-permute-done.12.refs_5_ = bf16[8,3584]{1,0:T(8,128)(2,1)S(1)} collective-permute-done((bf16[8,3584]{1,0:T(8,128)(2,1)S(1)}, bf16[8,3584]{1,0:T(8,128)(2,1)S(1)}, u32[]{:S(2)}, u32[]{:S(2)}) %collective-permute-start.12) | collective-permute-done | bytes 57376 | tf_op jit(solution)/shard_map/ppermute | solution.py:162
  39.9 1.2 %mix.1 = bf16[128,3584]{1,0:T(8,128)(2,1)} custom-call(bf16[128,192]{1,0:T(8,128)(2,1)S(1)} %get-tuple-element.38.mix_ref, bf16[8,3584]{1,0:T(8,128)(2,1)S(1)} %get-tuple-element.41.refs_0_, bf16[8,3584]{1,0:T(8,128)(2,1)S(1)} %collective-permute-done.8.refs_1_, bf16[8,3584]{1,0:T(8,128)(2,1)S(1)} %collective-permute-done.9.refs_2_, ...), custom_call_target="tpu_custom_call" | custom-call | tf_op jit(solution)/shard_map/mix/pallas_call | solution.py:251
  (17 shorter events, 0.7 us)
Async XLA Ops:
  1.2 17.1 %copy-start = (bf16[1,3584,2048]{2,1,0:T(8,128)(2,1)S(1)}, bf16[1,3584,2048]{2,1,0:T(8,128)(2,1)}, u32[]{:S(2)}) copy-start(bf16[1,3584,2048]{2,1,0:T(8,128)(2,1)} %param.9) | copy-start | bytes 44040196
  1.3 17.1 %copy-start.1 = (bf16[1,3584,2048]{2,1,0:T(8,128)(2,1)S(1)}, bf16[1,3584,2048]{2,1,0:T(8,128)(2,1)}, u32[]{:S(2)}) copy-start(bf16[1,3584,2048]{2,1,0:T(8,128)(2,1)} %param.10) | copy-start | bytes 44040196
  1.5 11.3 %collective-permute-start = (bf16[8,3584]{1,0:T(8,128)(2,1)S(1)}, bf16[8,3584]{1,0:T(8,128)(2,1)S(1)}, u32[]{:S(2)}, u32[]{:S(2)}) collective-permute-start(bf16[8,3584]{1,0:T(8,128)(2,1)S(1)} %get-tuple-element.30), channel_id=1, source_target_pairs={{0,14},{2,12},{4,10},{6,8},{8,6},{10,4},{12,2},{14,0},{1,15},{3,13... | collective-permute-start | bytes 172040 | tf_op jit(solution)/shard_map/ppermute | solution.py:162
  7.6 6.6 %collective-permute-start.1 = (bf16[8,3584]{1,0:T(8,128)(2,1)S(1)}, bf16[8,3584]{1,0:T(8,128)(2,1)S(1)}, u32[]{:S(2)}, u32[]{:S(2)}) collective-permute-start(bf16[8,3584]{1,0:T(8,128)(2,1)S(1)} %get-tuple-element.31), channel_id=1, source_target_pairs={{0,12},{2,14},{4,8},{6,10},{8,4},{10,6},{12,0},{14,2},{1,13},{3,15... | collective-permute-start | bytes 172040 | tf_op jit(solution)/shard_map/ppermute | solution.py:162
  7.8 8.3 %collective-permute-start.2 = (bf16[8,3584]{1,0:T(8,128)(2,1)S(1)}, bf16[8,3584]{1,0:T(8,128)(2,1)S(1)}, u32[]{:S(2)}, u32[]{:S(2)}) collective-permute-start(bf16[8,3584]{1,0:T(8,128)(2,1)S(1)} %get-tuple-element.32), channel_id=1, source_target_pairs={{0,10},{2,8},{4,14},{6,12},{8,2},{10,0},{12,6},{14,4},{1,11},{3,9}... | collective-permute-start | bytes 172040 | tf_op jit(solution)/shard_map/ppermute | solution.py:162
  8.6 8.3 %collective-permute-start.3 = (bf16[8,3584]{1,0:T(8,128)(2,1)S(1)}, bf16[8,3584]{1,0:T(8,128)(2,1)S(1)}, u32[]{:S(2)}, u32[]{:S(2)}) collective-permute-start(bf16[8,3584]{1,0:T(8,128)(2,1)S(1)} %get-tuple-element.33), channel_id=1, source_target_pairs={{0,6},{2,4},{4,2},{6,0},{8,14},{10,12},{12,10},{14,8},{1,7},{3,5},... | collective-permute-start | bytes 172040 | tf_op jit(solution)/shard_map/ppermute | solution.py:162
  12.9 5.1 %collective-permute-start.4 = (bf16[8,3584]{1,0:T(8,128)(2,1)S(1)}, bf16[8,3584]{1,0:T(8,128)(2,1)S(1)}, u32[]{:S(2)}, u32[]{:S(2)}) collective-permute-start(bf16[8,3584]{1,0:T(8,128)(2,1)S(1)} %get-tuple-element.34), channel_id=1, source_target_pairs={{0,8},{2,10},{4,12},{6,14},{8,0},{10,2},{12,4},{14,6},{1,9},{3,11}... | collective-permute-start | bytes 172040 | tf_op jit(solution)/shard_map/ppermute | solution.py:162
  12.9 5.1 %collective-permute-start.5 = (bf16[8,3584]{1,0:T(8,128)(2,1)S(1)}, bf16[8,3584]{1,0:T(8,128)(2,1)S(1)}, u32[]{:S(2)}, u32[]{:S(2)}) collective-permute-start(bf16[8,3584]{1,0:T(8,128)(2,1)S(1)} %get-tuple-element.35), channel_id=1, source_target_pairs={{0,4},{2,6},{4,0},{6,2},{8,12},{10,14},{12,8},{14,10},{1,5},{3,7},... | collective-permute-start | bytes 172040 | tf_op jit(solution)/shard_map/ppermute | solution.py:162
  14.2 4.2 %collective-permute-start.6 = (bf16[8,3584]{1,0:T(8,128)(2,1)S(1)}, bf16[8,3584]{1,0:T(8,128)(2,1)S(1)}, u32[]{:S(2)}, u32[]{:S(2)}) collective-permute-start(bf16[8,3584]{1,0:T(8,128)(2,1)S(1)} %get-tuple-element.36), channel_id=1, source_target_pairs={{0,2},{2,0},{4,6},{6,4},{8,10},{10,8},{12,14},{14,12},{1,3},{3,1},... | collective-permute-start | bytes 172040 | tf_op jit(solution)/shard_map/ppermute | solution.py:162
  18.4 6.0 %copy-start.2 = (bf16[1,2048,3584]{2,1,0:T(8,128)(2,1)S(1)}, bf16[1,2048,3584]{2,1,0:T(8,128)(2,1)}, u32[]{:S(2)}) copy-start(bf16[1,2048,3584]{2,1,0:T(8,128)(2,1)} %param.11) | copy-start | bytes 44040196
  22.4 2.0 %collective-permute-start.7 = (bf16[64,4096]{1,0:T(8,128)(2,1)S(1)}, bf16[64,4096]{1,0:T(8,128)(2,1)S(1)}, u32[]{:S(2)}, u32[]{:S(2)}) collective-permute-start(bf16[64,4096]{1,0:T(8,128)(2,1)S(1)} %get-tuple-element.40), channel_id=1, source_target_pairs={{0,1},{1,0},{2,3},{3,2},{4,5},{5,4},{6,7},{7,6},{8,9},{9,8},{10,11... | collective-permute-start | bytes 1572872 | tf_op jit(solution)/shard_map/ppermute | solution.py:234
  26.5 8.5 %collective-permute-start.8 = (bf16[8,3584]{1,0:T(8,128)(2,1)S(1)}, bf16[8,3584]{1,0:T(8,128)(2,1)S(1)}, u32[]{:S(2)}, u32[]{:S(2)}) collective-permute-start(bf16[8,3584]{1,0:T(8,128)(2,1)S(1)} %get-tuple-element.42), channel_id=1, source_target_pairs={{0,10},{2,8},{4,14},{6,12},{8,2},{10,0},{12,6},{14,4},{1,11},{3,9}... | collective-permute-start | bytes 172040 | tf_op jit(solution)/shard_map/ppermute | solution.py:162
  28.2 6.8 %collective-permute-start.9 = (bf16[8,3584]{1,0:T(8,128)(2,1)S(1)}, bf16[8,3584]{1,0:T(8,128)(2,1)S(1)}, u32[]{:S(2)}, u32[]{:S(2)}) collective-permute-start(bf16[8,3584]{1,0:T(8,128)(2,1)S(1)} %get-tuple-element.43), channel_id=1, source_target_pairs={{0,12},{2,14},{4,8},{6,10},{8,4},{10,6},{12,0},{14,2},{1,13},{3,15... | collective-permute-start | bytes 172040 | tf_op jit(solution)/shard_map/ppermute | solution.py:162
  29.7 7.3 %collective-permute-start.10 = (bf16[8,3584]{1,0:T(8,128)(2,1)S(1)}, bf16[8,3584]{1,0:T(8,128)(2,1)S(1)}, u32[]{:S(2)}, u32[]{:S(2)}) collective-permute-start(bf16[8,3584]{1,0:T(8,128)(2,1)S(1)} %get-tuple-element.44), channel_id=1, source_target_pairs={{0,14},{2,12},{4,10},{6,8},{8,6},{10,4},{12,2},{14,0},{1,15},{3,13... | collective-permute-start | bytes 172040 | tf_op jit(solution)/shard_map/ppermute | solution.py:162
  32.9 5.4 %collective-permute-start.11 = (bf16[8,3584]{1,0:T(8,128)(2,1)S(1)}, bf16[8,3584]{1,0:T(8,128)(2,1)S(1)}, u32[]{:S(2)}, u32[]{:S(2)}) collective-permute-start(bf16[8,3584]{1,0:T(8,128)(2,1)S(1)} %get-tuple-element.45), channel_id=1, source_target_pairs={{0,6},{2,4},{4,2},{6,0},{8,14},{10,12},{12,10},{14,8},{1,7},{3,5},... | collective-permute-start | bytes 172040 | tf_op jit(solution)/shard_map/ppermute | solution.py:162
  33.1 6.6 %collective-permute-start.12 = (bf16[8,3584]{1,0:T(8,128)(2,1)S(1)}, bf16[8,3584]{1,0:T(8,128)(2,1)S(1)}, u32[]{:S(2)}, u32[]{:S(2)}) collective-permute-start(bf16[8,3584]{1,0:T(8,128)(2,1)S(1)} %get-tuple-element.46), channel_id=1, source_target_pairs={{0,8},{2,10},{4,12},{6,14},{8,0},{10,2},{12,4},{14,6},{1,9},{3,11}... | collective-permute-start | bytes 172040 | tf_op jit(solution)/shard_map/ppermute | solution.py:162
  35.0 4.9 %collective-permute-start.13 = (bf16[8,3584]{1,0:T(8,128)(2,1)S(1)}, bf16[8,3584]{1,0:T(8,128)(2,1)S(1)}, u32[]{:S(2)}, u32[]{:S(2)}) collective-permute-start(bf16[8,3584]{1,0:T(8,128)(2,1)S(1)} %get-tuple-element.47), channel_id=1, source_target_pairs={{0,4},{2,6},{4,0},{6,2},{8,12},{10,14},{12,8},{14,10},{1,5},{3,7},... | collective-permute-start | bytes 172040 | tf_op jit(solution)/shard_map/ppermute | solution.py:162
  35.0 4.9 %collective-permute-start.14 = (bf16[8,3584]{1,0:T(8,128)(2,1)S(1)}, bf16[8,3584]{1,0:T(8,128)(2,1)S(1)}, u32[]{:S(2)}, u32[]{:S(2)}) collective-permute-start(bf16[8,3584]{1,0:T(8,128)(2,1)S(1)} %get-tuple-element.48), channel_id=1, source_target_pairs={{0,2},{2,0},{4,6},{6,4},{8,10},{10,8},{12,14},{14,12},{1,3},{3,1},... | collective-permute-start | bytes 172040 | tf_op jit(solution)/shard_map/ppermute | solution.py:162

commit v8 on v6

--- a/solution.py
+++ b/solution.py
@@ -9,7 +9,7 @@
 
 HIDDEN_SIZE = 2048
 ROUTED = 256
-ORDER = (0, 7, 6, 5, 3, 4, 2, 1)
+ORDER = (0, 7, 6, 3, 5, 4, 2, 1)
 RETURN = (0, 5, 6, 3, 7, 2, 4, 1)
 BF16 = jnp.bfloat16
 F32 = jnp.float32

time: 41 us -> 41 us (level)
  no operation moved by 1% of the time
where the time goes in v8:
time: 41 us; the launch traced here: 40.8 us
  starting transfers between devices  22.8 us (56%)
  waiting for transfers between devices  9.18 us (22%)
  Pallas kernels  8.76 us (21%)
    ppermute x14, starting transfers between devices, swap(): lax.ppermute(block, 'expert', [(i, i ^ j) for i in range(len(order))])  22.7 us
    ppermute x14, waiting for transfers between devices, swap(): lax.ppermute(block, 'expert', [(i, i ^ j) for i in range(len(order))])  7.28 us
    pallas_call x1, Pallas kernels, local(): pl.pallas_call(functools.partial(up_kernel, parts), in_specs=[VMEM] * (pa...  4 us
    pallas_call x1, Pallas kernels, local(): pl.pallas_call(down_kernel, in_specs=[VMEM] * 3, out_specs=[VMEM] * parts...  2.09 us
    ppermute x1, waiting for transfers between devices, local(): lax.ppermute(give, 'tensor', [(i, (i + 1) % cores) for i in range(cores)])  1.9 us
    pallas_call x1, Pallas kernels, local(): pl.pallas_call(functools.partial(route_kernel, slots, split, direct), in_...  1.24 us
    pallas_call x1, Pallas kernels, local(): pl.pallas_call(functools.partial(mix_kernel, parts), in_specs=[VMEM] * (1...  1.17 us
  transfers between devices with their start and end apart: 15, of which 11 were waited for; matrix products, arithmetic and copies ran while one was open for 0% of the time, Pallas kernels for 0%

profile of v8, /device:TPU:0, one launch (start us, length us, event | category | flops | bytes accessed | tf_op | source)
XLA Modules:
  0.0 40.8 jit_solution(17299991453343480789)
XLA Ops:
  0.0 1.2 %route.1 = (bf16[64,128]{1,0:T(8,128)(2,1)S(1)}, f32[64,128]{1,0:T(8,128)S(1)}, bf16[128,3584]{1,0:T(8,128)(2,1)S(1)}) custom-call(s32[8,128]{1,0:T(8,128)} %bitcast.8, f32[8,128]{1,0:T(8,128)} %bitcast.9, bf16[128,3584]{1,0:T(8,128)(2,1)} %tokens_hbm.1), custom_call_target="tpu_custom_call" | custom-call | flops 1000000 | tf_op jit(solution)/shard_map/route/pallas_call | solution.py:186
  1.3 0.3 send.1
  1.5 6.0 %collective-permute-start = (bf16[8,3584]{1,0:T(8,128)(2,1)S(1)}, bf16[8,3584]{1,0:T(8,128)(2,1)S(1)}, u32[]{:S(2)}, u32[]{:S(2)}) collective-permute-start(bf16[8,3584]{1,0:T(8,128)(2,1)S(1)} %get-tuple-element.30), channel_id=1, source_target_pairs={{0,14},{2,12},{4,10},{6,8},{8,6},{10,4},{12,2},{14,0},{1,15},{3,13... | collective-permute-start | bytes 172040 | tf_op jit(solution)/shard_map/ppermute | solution.py:162
  7.6 0.2 collective-permute-start.1
  7.8 5.1 %collective-permute-start.3 = (bf16[8,3584]{1,0:T(8,128)(2,1)S(1)}, bf16[8,3584]{1,0:T(8,128)(2,1)S(1)}, u32[]{:S(2)}, u32[]{:S(2)}) collective-permute-start(bf16[8,3584]{1,0:T(8,128)(2,1)S(1)} %get-tuple-element.33), channel_id=1, source_target_pairs={{0,10},{2,8},{4,14},{6,12},{8,2},{10,0},{12,6},{14,4},{1,11},{3,9}... | collective-permute-start | bytes 172040 | tf_op jit(solution)/shard_map/ppermute | solution.py:162
  12.9 0.8 %collective-permute-start.5 = (bf16[8,3584]{1,0:T(8,128)(2,1)S(1)}, bf16[8,3584]{1,0:T(8,128)(2,1)S(1)}, u32[]{:S(2)}, u32[]{:S(2)}) collective-permute-start(bf16[8,3584]{1,0:T(8,128)(2,1)S(1)} %get-tuple-element.35), channel_id=1, source_target_pairs={{0,4},{2,6},{4,0},{6,2},{8,12},{10,14},{12,8},{14,10},{1,5},{3,7},... | collective-permute-start | bytes 172040 | tf_op jit(solution)/shard_map/ppermute | solution.py:162
  13.7 0.5 %collective-permute-done.1.refs_2_ = bf16[8,3584]{1,0:T(8,128)(2,1)S(1)} collective-permute-done((bf16[8,3584]{1,0:T(8,128)(2,1)S(1)}, bf16[8,3584]{1,0:T(8,128)(2,1)S(1)}, u32[]{:S(2)}, u32[]{:S(2)}) %collective-permute-start.1) | collective-permute-done | bytes 57376 | tf_op jit(solution)/shard_map/ppermute | solution.py:162
  14.2 0.5 %collective-permute-start.6 = (bf16[8,3584]{1,0:T(8,128)(2,1)S(1)}, bf16[8,3584]{1,0:T(8,128)(2,1)S(1)}, u32[]{:S(2)}, u32[]{:S(2)}) collective-permute-start(bf16[8,3584]{1,0:T(8,128)(2,1)S(1)} %get-tuple-element.36), channel_id=1, source_target_pairs={{0,2},{2,0},{4,6},{6,4},{8,10},{10,8},{12,14},{14,12},{1,3},{3,1},... | collective-permute-start | bytes 172040 | tf_op jit(solution)/shard_map/ppermute | solution.py:162
  14.7 2.1 %collective-permute-done.3.refs_4_ = bf16[8,3584]{1,0:T(8,128)(2,1)S(1)} collective-permute-done((bf16[8,3584]{1,0:T(8,128)(2,1)S(1)}, bf16[8,3584]{1,0:T(8,128)(2,1)S(1)}, u32[]{:S(2)}, u32[]{:S(2)}) %collective-permute-start.3) | collective-permute-done | bytes 57376 | tf_op jit(solution)/shard_map/ppermute | solution.py:162
  16.8 1.2 %collective-permute-done.4.refs_5_ = bf16[8,3584]{1,0:T(8,128)(2,1)S(1)} collective-permute-done((bf16[8,3584]{1,0:T(8,128)(2,1)S(1)}, bf16[8,3584]{1,0:T(8,128)(2,1)S(1)}, u32[]{:S(2)}, u32[]{:S(2)}) %collective-permute-start.4) | collective-permute-done | bytes 57376 | tf_op jit(solution)/shard_map/ppermute | solution.py:162
  18.4 4.0 %up.1 = (f32[64,4096]{1,0:T(8,128)S(1)}, bf16[64,4096]{1,0:T(8,128)(2,1)S(1)}, bf16[128,192]{1,0:T(8,128)(2,1)S(1)}) custom-call(bf16[8,3584]{1,0:T(8,128)(2,1)S(1)} %get-tuple-element.29.refs_0_, bf16[8,3584]{1,0:T(8,128)(2,1)S(1)} %collective-permute-done.refs_1_, bf16[8,3584]{1,0:T(8,128)(2,1)S(1)} %collective-permute-done.1.refs_2_, ...), custom_call_target="tpu_custom_call" | custom-call | tf_op jit(solution)/shard_map/up/pallas_call | solution.py:221
  22.5 1.9 %collective-permute-done.7.other_ref = bf16[64,4096]{1,0:T(8,128)(2,1)S(1)} collective-permute-done((bf16[64,4096]{1,0:T(8,128)(2,1)S(1)}, bf16[64,4096]{1,0:T(8,128)(2,1)S(1)}, u32[]{:S(2)}, u32[]{:S(2)}) %collective-permute-start.7) | collective-permute-done | bytes 524320 | tf_op jit(solution)/shard_map/ppermute | solution.py:234
  24.4 2.1 %down.1 = (bf16[8,3584]{1,0:T(8,128)(2,1)S(1)}, bf16[8,3584]{1,0:T(8,128)(2,1)S(1)}, bf16[8,3584]{1,0:T(8,128)(2,1)S(1)}, bf16[8,3584]{1,0:T(8,128)(2,1)S(1)}, b...) custom-call(f32[64,4096]{1,0:T(8,128)S(1)} %get-tuple-element.39.own, ...), custom_call_target="tpu_custom_call" | custom-call | tf_op jit(solution)/shard_map/down/pallas_call | solution.py:235
  26.5 1.7 %collective-permute-start.8 = (bf16[8,3584]{1,0:T(8,128)(2,1)S(1)}, bf16[8,3584]{1,0:T(8,128)(2,1)S(1)}, u32[]{:S(2)}, u32[]{:S(2)}) collective-permute-start(bf16[8,3584]{1,0:T(8,128)(2,1)S(1)} %get-tuple-element.42), channel_id=1, source_target_pairs={{0,10},{2,8},{4,14},{6,12},{8,2},{10,0},{12,6},{14,4},{1,11},{3,9}... | collective-permute-start | bytes 172040 | tf_op jit(solution)/shard_map/ppermute | solution.py:162
  28.2 1.5 %collective-permute-start.9 = (bf16[8,3584]{1,0:T(8,128)(2,1)S(1)}, bf16[8,3584]{1,0:T(8,128)(2,1)S(1)}, u32[]{:S(2)}, u32[]{:S(2)}) collective-permute-start(bf16[8,3584]{1,0:T(8,128)(2,1)S(1)} %get-tuple-element.43), channel_id=1, source_target_pairs={{0,12},{2,14},{4,8},{6,10},{8,4},{10,6},{12,0},{14,2},{1,13},{3,15... | collective-permute-start | bytes 172040 | tf_op jit(solution)/shard_map/ppermute | solution.py:162
  29.7 1.4 %collective-permute-start.10 = (bf16[8,3584]{1,0:T(8,128)(2,1)S(1)}, bf16[8,3584]{1,0:T(8,128)(2,1)S(1)}, u32[]{:S(2)}, u32[]{:S(2)}) collective-permute-start(bf16[8,3584]{1,0:T(8,128)(2,1)S(1)} %get-tuple-element.44), channel_id=1, source_target_pairs={{0,6},{2,4},{4,2},{6,0},{8,14},{10,12},{12,10},{14,8},{1,7},{3,5},... | collective-permute-start | bytes 172040 | tf_op jit(solution)/shard_map/ppermute | solution.py:162
  31.1 2.9 %collective-permute-start.11 = (bf16[8,3584]{1,0:T(8,128)(2,1)S(1)}, bf16[8,3584]{1,0:T(8,128)(2,1)S(1)}, u32[]{:S(2)}, u32[]{:S(2)}) collective-permute-start(bf16[8,3584]{1,0:T(8,128)(2,1)S(1)} %get-tuple-element.45), channel_id=1, source_target_pairs={{0,14},{2,12},{4,10},{6,8},{8,6},{10,4},{12,2},{14,0},{1,15},{3,13... | collective-permute-start | bytes 172040 | tf_op jit(solution)/shard_map/ppermute | solution.py:162
  34.0 0.3 collective-permute-done.8.refs_1_
  34.4 1.1 %collective-permute-start.13 = (bf16[8,3584]{1,0:T(8,128)(2,1)S(1)}, bf16[8,3584]{1,0:T(8,128)(2,1)S(1)}, u32[]{:S(2)}, u32[]{:S(2)}) collective-permute-start(bf16[8,3584]{1,0:T(8,128)(2,1)S(1)} %get-tuple-element.47), channel_id=1, source_target_pairs={{0,8},{2,10},{4,12},{6,14},{8,0},{10,2},{12,4},{14,6},{1,9},{3,11}... | collective-permute-start | bytes 172040 | tf_op jit(solution)/shard_map/ppermute | solution.py:162
  35.4 1.5 %collective-permute-start.14 = (bf16[8,3584]{1,0:T(8,128)(2,1)S(1)}, bf16[8,3584]{1,0:T(8,128)(2,1)S(1)}, u32[]{:S(2)}, u32[]{:S(2)}) collective-permute-start(bf16[8,3584]{1,0:T(8,128)(2,1)S(1)} %get-tuple-element.48), channel_id=1, source_target_pairs={{0,2},{2,0},{4,6},{6,4},{8,10},{10,8},{12,14},{14,12},{1,3},{3,1},... | collective-permute-start | bytes 172040 | tf_op jit(solution)/shard_map/ppermute | solution.py:162
  36.9 1.1 %collective-permute-done.11.refs_4_ = bf16[8,3584]{1,0:T(8,128)(2,1)S(1)} collective-permute-done((bf16[8,3584]{1,0:T(8,128)(2,1)S(1)}, bf16[8,3584]{1,0:T(8,128)(2,1)S(1)}, u32[]{:S(2)}, u32[]{:S(2)}) %collective-permute-start.11) | collective-permute-done | bytes 57376 | tf_op jit(solution)/shard_map/ppermute | solution.py:162
  38.1 0.6 %collective-permute-done.12.refs_5_ = bf16[8,3584]{1,0:T(8,128)(2,1)S(1)} collective-permute-done((bf16[8,3584]{1,0:T(8,128)(2,1)S(1)}, bf16[8,3584]{1,0:T(8,128)(2,1)S(1)}, u32[]{:S(2)}, u32[]{:S(2)}) %collective-permute-start.12) | collective-permute-done | bytes 57376 | tf_op jit(solution)/shard_map/ppermute | solution.py:162
  38.7 0.8 %collective-permute-done.13.refs_6_ = bf16[8,3584]{1,0:T(8,128)(2,1)S(1)} collective-permute-done((bf16[8,3584]{1,0:T(8,128)(2,1)S(1)}, bf16[8,3584]{1,0:T(8,128)(2,1)S(1)}, u32[]{:S(2)}, u32[]{:S(2)}) %collective-permute-start.13) | collective-permute-done | bytes 57376 | tf_op jit(solution)/shard_map/ppermute | solution.py:162
  39.6 1.2 %mix.1 = bf16[128,3584]{1,0:T(8,128)(2,1)} custom-call(bf16[128,192]{1,0:T(8,128)(2,1)S(1)} %get-tuple-element.38.mix_ref, bf16[8,3584]{1,0:T(8,128)(2,1)S(1)} %get-tuple-element.41.refs_0_, bf16[8,3584]{1,0:T(8,128)(2,1)S(1)} %collective-permute-done.8.refs_1_, bf16[8,3584]{1,0:T(8,128)(2,1)S(1)} %collective-permute-done.9.refs_2_, ...), custom_call_target="tpu_custom_call" | custom-call | tf_op jit(solution)/shard_map/mix/pallas_call | solution.py:251
  (17 shorter events, 0.7 us)
Async XLA Ops:
  1.2 17.2 %copy-start = (bf16[1,3584,2048]{2,1,0:T(8,128)(2,1)S(1)}, bf16[1,3584,2048]{2,1,0:T(8,128)(2,1)}, u32[]{:S(2)}) copy-start(bf16[1,3584,2048]{2,1,0:T(8,128)(2,1)} %param.9) | copy-start | bytes 44040196
  1.3 17.1 %copy-start.1 = (bf16[1,3584,2048]{2,1,0:T(8,128)(2,1)S(1)}, bf16[1,3584,2048]{2,1,0:T(8,128)(2,1)}, u32[]{:S(2)}) copy-start(bf16[1,3584,2048]{2,1,0:T(8,128)(2,1)} %param.10) | copy-start | bytes 44040196
  1.5 11.3 %collective-permute-start = (bf16[8,3584]{1,0:T(8,128)(2,1)S(1)}, bf16[8,3584]{1,0:T(8,128)(2,1)S(1)}, u32[]{:S(2)}, u32[]{:S(2)}) collective-permute-start(bf16[8,3584]{1,0:T(8,128)(2,1)S(1)} %get-tuple-element.30), channel_id=1, source_target_pairs={{0,14},{2,12},{4,10},{6,8},{8,6},{10,4},{12,2},{14,0},{1,15},{3,13... | collective-permute-start | bytes 172040 | tf_op jit(solution)/shard_map/ppermute | solution.py:162
  7.6 6.6 %collective-permute-start.1 = (bf16[8,3584]{1,0:T(8,128)(2,1)S(1)}, bf16[8,3584]{1,0:T(8,128)(2,1)S(1)}, u32[]{:S(2)}, u32[]{:S(2)}) collective-permute-start(bf16[8,3584]{1,0:T(8,128)(2,1)S(1)} %get-tuple-element.31), channel_id=1, source_target_pairs={{0,12},{2,14},{4,8},{6,10},{8,4},{10,6},{12,0},{14,2},{1,13},{3,15... | collective-permute-start | bytes 172040 | tf_op jit(solution)/shard_map/ppermute | solution.py:162
  7.8 6.9 %collective-permute-start.2 = (bf16[8,3584]{1,0:T(8,128)(2,1)S(1)}, bf16[8,3584]{1,0:T(8,128)(2,1)S(1)}, u32[]{:S(2)}, u32[]{:S(2)}) collective-permute-start(bf16[8,3584]{1,0:T(8,128)(2,1)S(1)} %get-tuple-element.32), channel_id=1, source_target_pairs={{0,6},{2,4},{4,2},{6,0},{8,14},{10,12},{12,10},{14,8},{1,7},{3,5},... | collective-permute-start | bytes 172040 | tf_op jit(solution)/shard_map/ppermute | solution.py:162
  7.8 9.0 %collective-permute-start.3 = (bf16[8,3584]{1,0:T(8,128)(2,1)S(1)}, bf16[8,3584]{1,0:T(8,128)(2,1)S(1)}, u32[]{:S(2)}, u32[]{:S(2)}) collective-permute-start(bf16[8,3584]{1,0:T(8,128)(2,1)S(1)} %get-tuple-element.33), channel_id=1, source_target_pairs={{0,10},{2,8},{4,14},{6,12},{8,2},{10,0},{12,6},{14,4},{1,11},{3,9}... | collective-permute-start | bytes 172040 | tf_op jit(solution)/shard_map/ppermute | solution.py:162
  12.9 5.1 %collective-permute-start.4 = (bf16[8,3584]{1,0:T(8,128)(2,1)S(1)}, bf16[8,3584]{1,0:T(8,128)(2,1)S(1)}, u32[]{:S(2)}, u32[]{:S(2)}) collective-permute-start(bf16[8,3584]{1,0:T(8,128)(2,1)S(1)} %get-tuple-element.34), channel_id=1, source_target_pairs={{0,8},{2,10},{4,12},{6,14},{8,0},{10,2},{12,4},{14,6},{1,9},{3,11}... | collective-permute-start | bytes 172040 | tf_op jit(solution)/shard_map/ppermute | solution.py:162
  12.9 5.3 %collective-permute-start.5 = (bf16[8,3584]{1,0:T(8,128)(2,1)S(1)}, bf16[8,3584]{1,0:T(8,128)(2,1)S(1)}, u32[]{:S(2)}, u32[]{:S(2)}) collective-permute-start(bf16[8,3584]{1,0:T(8,128)(2,1)S(1)} %get-tuple-element.35), channel_id=1, source_target_pairs={{0,4},{2,6},{4,0},{6,2},{8,12},{10,14},{12,8},{14,10},{1,5},{3,7},... | collective-permute-start | bytes 172040 | tf_op jit(solution)/shard_map/ppermute | solution.py:162
  14.2 4.2 %collective-permute-start.6 = (bf16[8,3584]{1,0:T(8,128)(2,1)S(1)}, bf16[8,3584]{1,0:T(8,128)(2,1)S(1)}, u32[]{:S(2)}, u32[]{:S(2)}) collective-permute-start(bf16[8,3584]{1,0:T(8,128)(2,1)S(1)} %get-tuple-element.36), channel_id=1, source_target_pairs={{0,2},{2,0},{4,6},{6,4},{8,10},{10,8},{12,14},{14,12},{1,3},{3,1},... | collective-permute-start | bytes 172040 | tf_op jit(solution)/shard_map/ppermute | solution.py:162
  18.4 6.0 %copy-start.2 = (bf16[1,2048,3584]{2,1,0:T(8,128)(2,1)S(1)}, bf16[1,2048,3584]{2,1,0:T(8,128)(2,1)}, u32[]{:S(2)}) copy-start(bf16[1,2048,3584]{2,1,0:T(8,128)(2,1)} %param.11) | copy-start | bytes 44040196
  22.4 2.0 %collective-permute-start.7 = (bf16[64,4096]{1,0:T(8,128)(2,1)S(1)}, bf16[64,4096]{1,0:T(8,128)(2,1)S(1)}, u32[]{:S(2)}, u32[]{:S(2)}) collective-permute-start(bf16[64,4096]{1,0:T(8,128)(2,1)S(1)} %get-tuple-element.40), channel_id=1, source_target_pairs={{0,1},{1,0},{2,3},{3,2},{4,5},{5,4},{6,7},{7,6},{8,9},{9,8},{10,11... | collective-permute-start | bytes 1572872 | tf_op jit(solution)/shard_map/ppermute | solution.py:234
  26.5 7.9 %collective-permute-start.8 = (bf16[8,3584]{1,0:T(8,128)(2,1)S(1)}, bf16[8,3584]{1,0:T(8,128)(2,1)S(1)}, u32[]{:S(2)}, u32[]{:S(2)}) collective-permute-start(bf16[8,3584]{1,0:T(8,128)(2,1)S(1)} %get-tuple-element.42), channel_id=1, source_target_pairs={{0,10},{2,8},{4,14},{6,12},{8,2},{10,0},{12,6},{14,4},{1,11},{3,9}... | collective-permute-start | bytes 172040 | tf_op jit(solution)/shard_map/ppermute | solution.py:162
  28.2 7.3 %collective-permute-start.9 = (bf16[8,3584]{1,0:T(8,128)(2,1)S(1)}, bf16[8,3584]{1,0:T(8,128)(2,1)S(1)}, u32[]{:S(2)}, u32[]{:S(2)}) collective-permute-start(bf16[8,3584]{1,0:T(8,128)(2,1)S(1)} %get-tuple-element.43), channel_id=1, source_target_pairs={{0,12},{2,14},{4,8},{6,10},{8,4},{10,6},{12,0},{14,2},{1,13},{3,15... | collective-permute-start | bytes 172040 | tf_op jit(solution)/shard_map/ppermute | solution.py:162
  29.7 7.2 %collective-permute-start.10 = (bf16[8,3584]{1,0:T(8,128)(2,1)S(1)}, bf16[8,3584]{1,0:T(8,128)(2,1)S(1)}, u32[]{:S(2)}, u32[]{:S(2)}) collective-permute-start(bf16[8,3584]{1,0:T(8,128)(2,1)S(1)} %get-tuple-element.44), channel_id=1, source_target_pairs={{0,6},{2,4},{4,2},{6,0},{8,14},{10,12},{12,10},{14,8},{1,7},{3,5},... | collective-permute-start | bytes 172040 | tf_op jit(solution)/shard_map/ppermute | solution.py:162
  31.1 7.0 %collective-permute-start.11 = (bf16[8,3584]{1,0:T(8,128)(2,1)S(1)}, bf16[8,3584]{1,0:T(8,128)(2,1)S(1)}, u32[]{:S(2)}, u32[]{:S(2)}) collective-permute-start(bf16[8,3584]{1,0:T(8,128)(2,1)S(1)} %get-tuple-element.45), channel_id=1, source_target_pairs={{0,14},{2,12},{4,10},{6,8},{8,6},{10,4},{12,2},{14,0},{1,15},{3,13... | collective-permute-start | bytes 172040 | tf_op jit(solution)/shard_map/ppermute | solution.py:162
  34.0 4.7 %collective-permute-start.12 = (bf16[8,3584]{1,0:T(8,128)(2,1)S(1)}, bf16[8,3584]{1,0:T(8,128)(2,1)S(1)}, u32[]{:S(2)}, u32[]{:S(2)}) collective-permute-start(bf16[8,3584]{1,0:T(8,128)(2,1)S(1)} %get-tuple-element.46), channel_id=1, source_target_pairs={{0,4},{2,6},{4,0},{6,2},{8,12},{10,14},{12,8},{14,10},{1,5},{3,7},... | collective-permute-start | bytes 172040 | tf_op jit(solution)/shard_map/ppermute | solution.py:162
  34.4 5.1 %collective-permute-start.13 = (bf16[8,3584]{1,0:T(8,128)(2,1)S(1)}, bf16[8,3584]{1,0:T(8,128)(2,1)S(1)}, u32[]{:S(2)}, u32[]{:S(2)}) collective-permute-start(bf16[8,3584]{1,0:T(8,128)(2,1)S(1)} %get-tuple-element.47), channel_id=1, source_target_pairs={{0,8},{2,10},{4,12},{6,14},{8,0},{10,2},{12,4},{14,6},{1,9},{3,11}... | collective-permute-start | bytes 172040 | tf_op jit(solution)/shard_map/ppermute | solution.py:162
  35.4 4.2 %collective-permute-start.14 = (bf16[8,3584]{1,0:T(8,128)(2,1)S(1)}, bf16[8,3584]{1,0:T(8,128)(2,1)S(1)}, u32[]{:S(2)}, u32[]{:S(2)}) collective-permute-start(bf16[8,3584]{1,0:T(8,128)(2,1)S(1)} %get-tuple-element.48), channel_id=1, source_target_pairs={{0,2},{2,0},{4,6},{6,4},{8,10},{10,8},{12,14},{14,12},{1,3},{3,1},... | collective-permute-start | bytes 172040 | tf_op jit(solution)/shard_map/ppermute | solution.py:162
